TPU v7x, 256 devices: a whole 4x4x8 slice. The times are simulated.
256 devices in a mesh: ctx: 8 (over z_lo, y), dp: 32 (over x, z_hi, core).
Axes of the slice: x: 4, y: 4, z: 8 (z_hi: 4, z_lo: 2; z = z_hi * 2 + z_lo), core: 2. Of those that a mesh axis runs over, the one named last changes fastest.
Arguments:
- queries: bfloat16 [32, 1024, 2048], P('dp', 'ctx'), may hold values from -54 to 54
- key_states: bfloat16 [32, 1024, 1024], P('dp', 'ctx'), may hold values from -33 to 33
- value_states: bfloat16 [32, 1024, 1024], P('dp', 'ctx'), may hold values from -6 to 6
- saved_output: bfloat16 [32, 1024, 2048], P('dp', 'ctx'), may hold values from -6 to 6
- output_grad: bfloat16 [32, 1024, 2048], P('dp', 'ctx'), may hold values from -2.5 to 2.5
- layer_input: bfloat16 [32, 1024, 4608], P('dp', 'ctx'), may hold values from -6 to 6
- document_lengths: int32 [32, 8], P('dp'), may hold values from 1 to 512, 1024 in all within a row
Outputs:
- query_grad: bfloat16 [32, 1024, 2048], P('dp', 'ctx')
- key_grad: bfloat16 [32, 1024, 1024], P('dp', 'ctx')
- value_grad: bfloat16 [32, 1024, 1024], P('dp', 'ctx')
- weight_grad: float32 [4608, 1024], P('dp', 'ctx')
Inputs may be any that keep to these rules, and one draw needn't show every extreme that they name: `document_lengths`: in every pack the 8 lengths sum to 1024 and the longest is exactly 512.
All inputs are finite; a program needn't handle non-finite values.
Results may differ from a plain program's by a relative error of at most 0.018.
Values may be sent and summed in bfloat16 or wider, within the bound.
No kernel may reach another device: no remote copies, remote signals or barrier semaphores. Data moves between devices by JAX's collectives and lax.ppermute only.
A program may use at most 128 MiB of HBM per device.

v0:
```python
import math

import jax
import jax.numpy as jnp
from jax import lax
from jax.sharding import PartitionSpec as P

HQ = 16
KEY_VALUE_HEADS = 8
HEAD_SIZE = 128
QUERY_PER_KEY = 2
KVW = 1024


CAP = 50.0
SCALE = 144.0 ** (-0.5)


def from_behind(block, axis, distance):
    devices = range(lax.axis_size(axis))
    route = [((i - distance) % len(devices), i) for i in devices]
    return lax.ppermute(block, axis, route)


def doc_ids(ends, positions):
    return jnp.sum((positions[:, None] >= ends[None, :]).astype(jnp.int32), axis=1)


def softcap_scores(heads_of_query, heads_of_key):
    raw = (
        jnp.einsum(
            "qgrd,kgd->grqk", heads_of_query, heads_of_key, preferred_element_type=jnp.float32
        )
        * SCALE
    )
    return CAP * jnp.tanh(raw / CAP)


def tile_grads(
    rows_of_query,
    gradient_rows,
    lse_rows,
    delta_rows,
    query_pos,
    query_ids,
    rows_of_key,
    rows_of_value,
    key_pos,
    key_ids,
):
    query_count = rows_of_query.shape[0]
    key_count = rows_of_key.shape[0]
    live = (query_ids[:, None] == key_ids[None, :]) & (key_pos[None, :] <= query_pos[:, None])
    heads_of_query = rows_of_query.reshape(query_count, KEY_VALUE_HEADS, QUERY_PER_KEY, HEAD_SIZE)
    gradient_heads = gradient_rows.reshape(query_count, KEY_VALUE_HEADS, QUERY_PER_KEY, HEAD_SIZE)
    heads_of_key = rows_of_key.reshape(key_count, KEY_VALUE_HEADS, HEAD_SIZE)
    heads_of_value = rows_of_value.reshape(key_count, KEY_VALUE_HEADS, HEAD_SIZE)
    capped_logits = softcap_scores(heads_of_query, heads_of_key)
    prob = jnp.where(live[None, None], jnp.exp(capped_logits - lse_rows[..., None]), 0.0)
    dprob = jnp.einsum(
        "qgrd,kgd->grqk", gradient_heads, heads_of_value, preferred_element_type=jnp.float32
    )
    dscore = (
        prob * (dprob - delta_rows[..., None]) * (1.0 - (capped_logits / CAP) ** 2) * SCALE
    ).astype(jnp.bfloat16)
    prob_low = prob.astype(jnp.bfloat16)
    query_part = jnp.einsum(
        "grqk,kgd->qgrd", dscore, heads_of_key, preferred_element_type=jnp.float32
    )
    key_part = jnp.einsum(
        "grqk,qgrd->kgd", dscore, heads_of_query, preferred_element_type=jnp.float32
    )
    value_part = jnp.einsum(
        "grqk,qgrd->kgd", prob_low, gradient_heads, preferred_element_type=jnp.float32
    )
    return (
        query_part.reshape(query_count, HQ * HEAD_SIZE),
        key_part.reshape(key_count, KVW),
        value_part.reshape(key_count, KVW),
    )


def body(
    queries, key_states, value_states, saved_output, output_grad, layer_input, document_lengths
):
    row_matrix = queries.shape[1]
    parts = lax.axis_size("ctx")
    mine = lax.axis_index("ctx")
    rows_of_query = queries[0]
    rows_of_key = key_states[0]
    rows_of_value = value_states[0]
    gradient_rows = output_grad[0]
    ends = jnp.cumsum(document_lengths[0])
    offsets = jnp.arange(row_matrix, dtype=jnp.int32)
    own_pos = mine * row_matrix + offsets
    own_ids = doc_ids(ends, own_pos)
    heads_of_query = rows_of_query.reshape(row_matrix, KEY_VALUE_HEADS, QUERY_PER_KEY, HEAD_SIZE)
    slice_part = lax.all_gather(rows_of_key, "ctx", axis=0, tiled=True)
    row_count = slice_part.shape[0]
    key_pos = jnp.arange(row_count, dtype=jnp.int32)
    key_ids = doc_ids(ends, key_pos)
    live = (own_ids[:, None] == key_ids[None, :]) & (key_pos[None, :] <= own_pos[:, None])
    capped_logits = softcap_scores(
        heads_of_query, slice_part.reshape(row_count, KEY_VALUE_HEADS, HEAD_SIZE)
    )
    total = jnp.sum(jnp.where(live[None, None], jnp.exp(capped_logits), 0.0), axis=-1)
    lse = jnp.log(total)
    delta = jnp.einsum(
        "qgrd,qgrd->grq",
        gradient_rows.reshape(row_matrix, KEY_VALUE_HEADS, QUERY_PER_KEY, HEAD_SIZE),
        saved_output[0].reshape(row_matrix, KEY_VALUE_HEADS, QUERY_PER_KEY, HEAD_SIZE),
        preferred_element_type=jnp.float32,
    )
    width_q = rows_of_query.shape[1]
    width_k = rows_of_key.shape[1]

    def query_step(step, carry):
        visit, moved, key_sum, value_sum = carry
        source = (mine - step) % parts
        query_pos = source * row_matrix + offsets
        query_ids = doc_ids(ends, query_pos)
        query_part, key_part, value_part = tile_grads(
            visit[0],
            visit[1],
            moved[1],
            moved[2],
            query_pos,
            query_ids,
            rows_of_key,
            rows_of_value,
            own_pos,
            own_ids,
        )
        moved = from_behind((moved[0] + query_part, moved[1], moved[2]), "ctx", 1)
        visit = from_behind((visit[0], visit[1]), "ctx", 1)
        return (visit, moved, key_sum + key_part, value_sum + value_part)

    start = (
        (rows_of_query, gradient_rows),
        (jnp.zeros((row_matrix, width_q), jnp.float32), lse, delta),
        jnp.zeros((row_matrix, width_k), jnp.float32),
        jnp.zeros((row_matrix, width_k), jnp.float32),
    )
    unused, moved, key_sum, value_sum = lax.fori_loop(0, parts, query_step, start)
    query_sum = moved[0]
    value_low = value_sum.astype(jnp.bfloat16)
    groups = lax.axis_size("dp")
    factor = 1.0 / math.sqrt(float(groups * row_matrix * parts))
    term = (
        lax.dot_general(
            layer_input[0], value_low, (((0,), (0,)), ((), ())), preferred_element_type=jnp.float32
        )
        * factor
    )
    partial_sum = lax.psum_scatter(
        term.astype(jnp.bfloat16), "dp", scatter_dimension=0, tiled=True
    ).astype(jnp.float32)
    weight_grad = lax.psum_scatter(partial_sum, "ctx", scatter_dimension=1, tiled=True)
    return (
        query_sum.astype(jnp.bfloat16)[None],
        key_sum.astype(jnp.bfloat16)[None],
        value_low[None],
        weight_grad,
    )


def solution(mesh):
    return jax.shard_map(
        body,
        mesh=mesh,
        in_specs=(
            P("dp", "ctx", None),
            P("dp", "ctx", None),
            P("dp", "ctx", None),
            P("dp", "ctx", None),
            P("dp", "ctx", None),
            P("dp", "ctx", None),
            P("dp", None),
        ),
        out_specs=(
            P("dp", "ctx", None),
            P("dp", "ctx", None),
            P("dp", "ctx", None),
            P("dp", "ctx"),
        ),
        check_vma=False,
    )
```

profile of v0, /device:TPU:32, one launch (start us, length us, event | category | flops | bytes accessed | tf_op | source)
XLA Modules:
  0.0 707.9 jit_solution(17229702504439187502)
XLA Ops:
  23.8 36.5 %all-gather.3.cloned.1.call-done = bf16[1,1024,1024]{1,2,0:T(8,128)(2,1)} async-done(((bf16[1,128,1024]{1,2,0:T(8,128)(2,1)}), bf16[1,1024,1024]{1,2,0:T(8,128)(2,1)}) %all-gather.3.cloned.1.call-update) | async-done | bytes 2097168 | tf_op jit(solution)/shard_map/all_gather | solution.py:98
  60.3 4.9 fusion.22
  66.9 441.0 %while.28 = (s32[]{:T(128)}, bf16[128,2048]{0,1:T(8,128)(2,1)}, bf16[128,2048]{0,1:T(8,128)(2,1)}, f32[128,2048]{0,1:T(8,128)}, f32[8,2,128]{2,1,0:T(2,128)}, /*...) while((s32[]{:T(128)}, bf16[128,2048]{0,1:T(8,128)(2,1)}, ...), condition=%wide.region_6.7_spmd.clone, body=%wide.region_4.6_spmd.clone.sunk | while | flops 340315264 | bytes 27177512 | solution.py:144
  88.8 19.3 %collective-permute-done.4 = f32[8,2,128]{2,1,0:T(2,128)} collective-permute-done((f32[8,2,128]{2,1,0:T(2,128)}, f32[8,2,128]{2,1,0:T(2,128)}, u32[]{:S(2)}, u32[]{:S(2)}) %collective-permute-start.4) | collective-permute-done | bytes 8224 | tf_op jit(solution)/shard_map/while/body/eval_jaxpr/ppermute | solution.py:22
  108.3 11.2 %collective-permute-done = bf16[128,2048]{0,1:T(8,128)(2,1)} collective-permute-done((bf16[128,2048]{0,1:T(8,128)(2,1)S(1)}, bf16[128,2048]{0,1:T(8,128)(2,1)}, u32[]{:S(2)}, u32[]{:S(2)}) %collective-permute-start) | collective-permute-done | bytes 524320 | tf_op jit(solution)/shard_map/while/body/eval_jaxpr/ppermute | solution.py:22
  119.5 5.7 collective-permute-done.1
  139.4 3.9 collective-permute-start
  145.0 2.3 bitcast_add_fusion.6
  147.3 19.1 %collective-permute-done.4 = f32[8,2,128]{2,1,0:T(2,128)} collective-permute-done((f32[8,2,128]{2,1,0:T(2,128)}, f32[8,2,128]{2,1,0:T(2,128)}, u32[]{:S(2)}, u32[]{:S(2)}) %collective-permute-start.4) | collective-permute-done | bytes 8224 | tf_op jit(solution)/shard_map/while/body/eval_jaxpr/ppermute | solution.py:22
  166.6 10.4 %collective-permute-done = bf16[128,2048]{0,1:T(8,128)(2,1)} collective-permute-done((bf16[128,2048]{0,1:T(8,128)(2,1)S(1)}, bf16[128,2048]{0,1:T(8,128)(2,1)}, u32[]{:S(2)}, u32[]{:S(2)}) %collective-permute-start) | collective-permute-done | bytes 524320 | tf_op jit(solution)/shard_map/while/body/eval_jaxpr/ppermute | solution.py:22
  177.0 5.6 collective-permute-done.1
  196.8 4.6 collective-permute-start
  203.2 2.3 bitcast_add_fusion.6
  205.5 18.4 %collective-permute-done.4 = f32[8,2,128]{2,1,0:T(2,128)} collective-permute-done((f32[8,2,128]{2,1,0:T(2,128)}, f32[8,2,128]{2,1,0:T(2,128)}, u32[]{:S(2)}, u32[]{:S(2)}) %collective-permute-start.4) | collective-permute-done | bytes 8224 | tf_op jit(solution)/shard_map/while/body/eval_jaxpr/ppermute | solution.py:22
  224.1 9.5 %collective-permute-done = bf16[128,2048]{0,1:T(8,128)(2,1)} collective-permute-done((bf16[128,2048]{0,1:T(8,128)(2,1)S(1)}, bf16[128,2048]{0,1:T(8,128)(2,1)}, u32[]{:S(2)}, u32[]{:S(2)}) %collective-permute-start) | collective-permute-done | bytes 524320 | tf_op jit(solution)/shard_map/while/body/eval_jaxpr/ppermute | solution.py:22
  233.5 5.6 collective-permute-done.1
  251.7 2.4 collective-permute-start.3
  254.0 4.6 collective-permute-start
  260.4 2.3 bitcast_add_fusion.6
  262.7 17.7 %collective-permute-done.4 = f32[8,2,128]{2,1,0:T(2,128)} collective-permute-done((f32[8,2,128]{2,1,0:T(2,128)}, f32[8,2,128]{2,1,0:T(2,128)}, u32[]{:S(2)}, u32[]{:S(2)}) %collective-permute-start.4) | collective-permute-done | bytes 8224 | tf_op jit(solution)/shard_map/while/body/eval_jaxpr/ppermute | solution.py:22
  280.6 8.5 %collective-permute-done = bf16[128,2048]{0,1:T(8,128)(2,1)} collective-permute-done((bf16[128,2048]{0,1:T(8,128)(2,1)S(1)}, bf16[128,2048]{0,1:T(8,128)(2,1)}, u32[]{:S(2)}, u32[]{:S(2)}) %collective-permute-start) | collective-permute-done | bytes 524320 | tf_op jit(solution)/shard_map/while/body/eval_jaxpr/ppermute | solution.py:22
  289.1 5.6 collective-permute-done.1
  307.3 3.1 collective-permute-start.3
  310.3 4.6 collective-permute-start
  316.7 2.3 bitcast_add_fusion.6
  319.0 16.9 %collective-permute-done.4 = f32[8,2,128]{2,1,0:T(2,128)} collective-permute-done((f32[8,2,128]{2,1,0:T(2,128)}, f32[8,2,128]{2,1,0:T(2,128)}, u32[]{:S(2)}, u32[]{:S(2)}) %collective-permute-start.4) | collective-permute-done | bytes 8224 | tf_op jit(solution)/shard_map/while/body/eval_jaxpr/ppermute | solution.py:22
  336.1 7.6 %collective-permute-done = bf16[128,2048]{0,1:T(8,128)(2,1)} collective-permute-done((bf16[128,2048]{0,1:T(8,128)(2,1)S(1)}, bf16[128,2048]{0,1:T(8,128)(2,1)}, u32[]{:S(2)}, u32[]{:S(2)}) %collective-permute-start) | collective-permute-done | bytes 524320 | tf_op jit(solution)/shard_map/while/body/eval_jaxpr/ppermute | solution.py:22
  343.8 5.6 collective-permute-done.1
  361.9 3.8 collective-permute-start.3
  365.7 4.6 collective-permute-start
  372.1 2.3 bitcast_add_fusion.6
  374.4 16.2 %collective-permute-done.4 = f32[8,2,128]{2,1,0:T(2,128)} collective-permute-done((f32[8,2,128]{2,1,0:T(2,128)}, f32[8,2,128]{2,1,0:T(2,128)}, u32[]{:S(2)}, u32[]{:S(2)}) %collective-permute-start.4) | collective-permute-done | bytes 8224 | tf_op jit(solution)/shard_map/while/body/eval_jaxpr/ppermute | solution.py:22
  390.8 6.7 collective-permute-done
  397.5 5.6 collective-permute-done.1
  415.7 4.5 collective-permute-start.3
  420.2 4.6 collective-permute-start
  428.9 15.5 %collective-permute-done.4 = f32[8,2,128]{2,1,0:T(2,128)} collective-permute-done((f32[8,2,128]{2,1,0:T(2,128)}, f32[8,2,128]{2,1,0:T(2,128)}, u32[]{:S(2)}, u32[]{:S(2)}) %collective-permute-start.4) | collective-permute-done | bytes 8224 | tf_op jit(solution)/shard_map/while/body/eval_jaxpr/ppermute | solution.py:22
  444.5 5.8 collective-permute-done
  450.3 5.6 collective-permute-done.1
  469.1 4.6 collective-permute-start.3
  473.7 4.6 collective-permute-start
  482.4 14.1 %collective-permute-done.4 = f32[8,2,128]{2,1,0:T(2,128)} collective-permute-done((f32[8,2,128]{2,1,0:T(2,128)}, f32[8,2,128]{2,1,0:T(2,128)}, u32[]{:S(2)}, u32[]{:S(2)}) %collective-permute-start.4) | collective-permute-done | bytes 8224 | tf_op jit(solution)/shard_map/while/body/eval_jaxpr/ppermute | solution.py:22
  496.6 5.6 collective-permute-done
  502.2 5.6 collective-permute-done.1
  509.0 5.1 fusion.23
  514.2 12.7 %copy.102 = bf16[4608,1024]{1,0:T(8,128)(2,1)} copy(bf16[4608,1024]{0,1:T(8,128)(2,1)} %fusion.23) | data formatting | bytes 18874368
  526.9 130.1 %reduce-scatter.7.cloned.1.call-done = bf16[144,1024]{1,0:T(8,128)(2,1)} async-done(((bf16[4608,1024]{1,0:T(8,128)(2,1)}), bf16[144,1024]{1,0:T(8,128)(2,1)}) %reduce-scatter.7.cloned.1.call-update) | async-done | bytes 294928
  662.4 37.3 %reduce-scatter.5.cloned.1.call-done = f32[144,128]{0,1:T(8,128)} async-done(((f32[144,1024]{0,1:T(8,128)}), f32[144,128]{0,1:T(8,128)}) %reduce-scatter.5.cloned.1.call-update) | async-done | bytes 73744 | tf_op jit(solution)/shard_map/reduce_scatter | solution.py:158
  (204 shorter events, 158.0 us)
Async XLA Ops:
  7.2 501.9 %copy-start = (bf16[1,128,4608]{2,1,0:T(8,128)(2,1)S(1)}, bf16[1,128,4608]{2,1,0:T(8,128)(2,1)}, u32[]{:S(2)}) copy-start(bf16[1,128,4608]{2,1,0:T(8,128)(2,1)} %param.14) | copy-start | bytes 3538948
  7.2 53.1 %all-gather.3.cloned.1.call-start = ((), (), s32[]{:S(2)}) async-start(), calls=%async_computation.3 | async-start | bytes 2359296 | tf_op jit(solution)/shard_map/all_gather | solution.py:98
  9.1 648.0 %reduce-scatter.7.cloned.1.call-start = ((), (), s32[]{:S(2)}) async-start(), calls=%async_computation.4 | async-start | bytes 9732096
  60.3 6.5 copy-start.1
  79.4 45.8 %collective-permute-start.2 = (f32[128,2048]{0,1:T(8,128)}, f32[128,2048]{0,1:T(8,128)}, u32[]{:S(2)}, u32[]{:S(2)}) collective-permute-start(f32[128,2048]{0,1:T(8,128)} %bitcast_add_fusion.5), channel_id=1, source_target_pairs={{224,0},{0,32},{32,64},{64,96},{96,128},{128,160},{160,192},{192,2... | collective-permute-start | bytes 3145736 | tf_op jit(solution)/shard_map/while/body/eval_jaxpr/ppermute | solution.py:22
  80.4 27.7 %collective-permute-start.4 = (f32[8,2,128]{2,1,0:T(2,128)}, f32[8,2,128]{2,1,0:T(2,128)}, u32[]{:S(2)}, u32[]{:S(2)}) collective-permute-start(f32[8,2,128]{2,1,0:T(2,128)} %copy.126), channel_id=1, source_target_pairs={{224,0},{0,32},{32,64},{64,96},{96,128},{128,160},{160,192},{192,2... | collective-permute-start | bytes 24584 | tf_op jit(solution)/shard_map/while/body/eval_jaxpr/ppermute | solution.py:22
  81.8 26.5 %collective-permute-start.3 = (f32[8,2,128]{2,1,0:T(2,128)}, f32[8,2,128]{2,1,0:T(2,128)}, u32[]{:S(2)}, u32[]{:S(2)}) collective-permute-start(f32[8,2,128]{2,1,0:T(2,128)} %copy.125), channel_id=1, source_target_pairs={{224,0},{0,32},{32,64},{64,96},{96,128},{128,160},{160,192},{192,2... | collective-permute-start | bytes 24584 | tf_op jit(solution)/shard_map/while/body/eval_jaxpr/ppermute | solution.py:22
  83.9 35.6 %collective-permute-start = (bf16[128,2048]{0,1:T(8,128)(2,1)S(1)}, bf16[128,2048]{0,1:T(8,128)(2,1)}, u32[]{:S(2)}, u32[]{:S(2)}) collective-permute-start(bf16[128,2048]{0,1:T(8,128)(2,1)S(1)} %copy.122), channel_id=1, source_target_pairs={{224,0},{0,32},{32,64},{64,96},{96,128},{128,160},{160,192},{192,2... | collective-permute-start | bytes 1572872 | tf_op jit(solution)/shard_map/while/body/eval_jaxpr/ppermute | solution.py:22
  84.2 41.0 %collective-permute-start.1 = (bf16[128,2048]{0,1:T(8,128)(2,1)}, bf16[128,2048]{0,1:T(8,128)(2,1)}, u32[]{:S(2)}, u32[]{:S(2)}) collective-permute-start(bf16[128,2048]{0,1:T(8,128)(2,1)} %copy.123), channel_id=1, source_target_pairs={{224,0},{0,32},{32,64},{64,96},{96,128},{128,160},{160,192},{192,2... | collective-permute-start | bytes 1572872 | tf_op jit(solution)/shard_map/while/body/eval_jaxpr/ppermute | solution.py:22
  137.8 44.9 %collective-permute-start.2 = (f32[128,2048]{0,1:T(8,128)}, f32[128,2048]{0,1:T(8,128)}, u32[]{:S(2)}, u32[]{:S(2)}) collective-permute-start(f32[128,2048]{0,1:T(8,128)} %bitcast_add_fusion.5), channel_id=1, source_target_pairs={{224,0},{0,32},{32,64},{64,96},{96,128},{128,160},{160,192},{192,2... | collective-permute-start | bytes 3145736 | tf_op jit(solution)/shard_map/while/body/eval_jaxpr/ppermute | solution.py:22
  137.8 28.7 %collective-permute-start.4 = (f32[8,2,128]{2,1,0:T(2,128)}, f32[8,2,128]{2,1,0:T(2,128)}, u32[]{:S(2)}, u32[]{:S(2)}) collective-permute-start(f32[8,2,128]{2,1,0:T(2,128)} %copy.126), channel_id=1, source_target_pairs={{224,0},{0,32},{32,64},{64,96},{96,128},{128,160},{160,192},{192,2... | collective-permute-start | bytes 24584 | tf_op jit(solution)/shard_map/while/body/eval_jaxpr/ppermute | solution.py:22
  137.8 28.9 %collective-permute-start.3 = (f32[8,2,128]{2,1,0:T(2,128)}, f32[8,2,128]{2,1,0:T(2,128)}, u32[]{:S(2)}, u32[]{:S(2)}) collective-permute-start(f32[8,2,128]{2,1,0:T(2,128)} %copy.125), channel_id=1, source_target_pairs={{224,0},{0,32},{32,64},{64,96},{96,128},{128,160},{160,192},{192,2... | collective-permute-start | bytes 24584 | tf_op jit(solution)/shard_map/while/body/eval_jaxpr/ppermute | solution.py:22
  139.4 37.6 %collective-permute-start = (bf16[128,2048]{0,1:T(8,128)(2,1)S(1)}, bf16[128,2048]{0,1:T(8,128)(2,1)}, u32[]{:S(2)}, u32[]{:S(2)}) collective-permute-start(bf16[128,2048]{0,1:T(8,128)(2,1)S(1)} %copy.122), channel_id=1, source_target_pairs={{224,0},{0,32},{32,64},{64,96},{96,128},{128,160},{160,192},{192,2... | collective-permute-start | bytes 1572872 | tf_op jit(solution)/shard_map/while/body/eval_jaxpr/ppermute | solution.py:22
  143.3 39.4 %collective-permute-start.1 = (bf16[128,2048]{0,1:T(8,128)(2,1)}, bf16[128,2048]{0,1:T(8,128)(2,1)}, u32[]{:S(2)}, u32[]{:S(2)}) collective-permute-start(bf16[128,2048]{0,1:T(8,128)(2,1)} %copy.123), channel_id=1, source_target_pairs={{224,0},{0,32},{32,64},{64,96},{96,128},{128,160},{160,192},{192,2... | collective-permute-start | bytes 1572872 | tf_op jit(solution)/shard_map/while/body/eval_jaxpr/ppermute | solution.py:22
  195.2 44.0 %collective-permute-start.2 = (f32[128,2048]{0,1:T(8,128)}, f32[128,2048]{0,1:T(8,128)}, u32[]{:S(2)}, u32[]{:S(2)}) collective-permute-start(f32[128,2048]{0,1:T(8,128)} %bitcast_add_fusion.5), channel_id=1, source_target_pairs={{224,0},{0,32},{32,64},{64,96},{96,128},{128,160},{160,192},{192,2... | collective-permute-start | bytes 3145736 | tf_op jit(solution)/shard_map/while/body/eval_jaxpr/ppermute | solution.py:22
  195.2 28.7 %collective-permute-start.4 = (f32[8,2,128]{2,1,0:T(2,128)}, f32[8,2,128]{2,1,0:T(2,128)}, u32[]{:S(2)}, u32[]{:S(2)}) collective-permute-start(f32[8,2,128]{2,1,0:T(2,128)} %copy.126), channel_id=1, source_target_pairs={{224,0},{0,32},{32,64},{64,96},{96,128},{128,160},{160,192},{192,2... | collective-permute-start | bytes 24584 | tf_op jit(solution)/shard_map/while/body/eval_jaxpr/ppermute | solution.py:22
  195.2 28.9 %collective-permute-start.3 = (f32[8,2,128]{2,1,0:T(2,128)}, f32[8,2,128]{2,1,0:T(2,128)}, u32[]{:S(2)}, u32[]{:S(2)}) collective-permute-start(f32[8,2,128]{2,1,0:T(2,128)} %copy.125), channel_id=1, source_target_pairs={{224,0},{0,32},{32,64},{64,96},{96,128},{128,160},{160,192},{192,2... | collective-permute-start | bytes 24584 | tf_op jit(solution)/shard_map/while/body/eval_jaxpr/ppermute | solution.py:22
  196.8 36.7 %collective-permute-start = (bf16[128,2048]{0,1:T(8,128)(2,1)S(1)}, bf16[128,2048]{0,1:T(8,128)(2,1)}, u32[]{:S(2)}, u32[]{:S(2)}) collective-permute-start(bf16[128,2048]{0,1:T(8,128)(2,1)S(1)} %copy.122), channel_id=1, source_target_pairs={{224,0},{0,32},{32,64},{64,96},{96,128},{128,160},{160,192},{192,2... | collective-permute-start | bytes 1572872 | tf_op jit(solution)/shard_map/while/body/eval_jaxpr/ppermute | solution.py:22
  201.4 37.7 %collective-permute-start.1 = (bf16[128,2048]{0,1:T(8,128)(2,1)}, bf16[128,2048]{0,1:T(8,128)(2,1)}, u32[]{:S(2)}, u32[]{:S(2)}) collective-permute-start(bf16[128,2048]{0,1:T(8,128)(2,1)} %copy.123), channel_id=1, source_target_pairs={{224,0},{0,32},{32,64},{64,96},{96,128},{128,160},{160,192},{192,2... | collective-permute-start | bytes 1572872 | tf_op jit(solution)/shard_map/while/body/eval_jaxpr/ppermute | solution.py:22
  251.7 43.0 %collective-permute-start.2 = (f32[128,2048]{0,1:T(8,128)}, f32[128,2048]{0,1:T(8,128)}, u32[]{:S(2)}, u32[]{:S(2)}) collective-permute-start(f32[128,2048]{0,1:T(8,128)} %bitcast_add_fusion.5), channel_id=1, source_target_pairs={{224,0},{0,32},{32,64},{64,96},{96,128},{128,160},{160,192},{192,2... | collective-permute-start | bytes 3145736 | tf_op jit(solution)/shard_map/while/body/eval_jaxpr/ppermute | solution.py:22
  251.7 28.7 %collective-permute-start.4 = (f32[8,2,128]{2,1,0:T(2,128)}, f32[8,2,128]{2,1,0:T(2,128)}, u32[]{:S(2)}, u32[]{:S(2)}) collective-permute-start(f32[8,2,128]{2,1,0:T(2,128)} %copy.126), channel_id=1, source_target_pairs={{224,0},{0,32},{32,64},{64,96},{96,128},{128,160},{160,192},{192,2... | collective-permute-start | bytes 24584 | tf_op jit(solution)/shard_map/while/body/eval_jaxpr/ppermute | solution.py:22
  251.7 28.9 %collective-permute-start.3 = (f32[8,2,128]{2,1,0:T(2,128)}, f32[8,2,128]{2,1,0:T(2,128)}, u32[]{:S(2)}, u32[]{:S(2)}) collective-permute-start(f32[8,2,128]{2,1,0:T(2,128)} %copy.125), channel_id=1, source_target_pairs={{224,0},{0,32},{32,64},{64,96},{96,128},{128,160},{160,192},{192,2... | collective-permute-start | bytes 24584 | tf_op jit(solution)/shard_map/while/body/eval_jaxpr/ppermute | solution.py:22
  254.0 35.1 %collective-permute-start = (bf16[128,2048]{0,1:T(8,128)(2,1)S(1)}, bf16[128,2048]{0,1:T(8,128)(2,1)}, u32[]{:S(2)}, u32[]{:S(2)}) collective-permute-start(bf16[128,2048]{0,1:T(8,128)(2,1)S(1)} %copy.122), channel_id=1, source_target_pairs={{224,0},{0,32},{32,64},{64,96},{96,128},{128,160},{160,192},{192,2... | collective-permute-start | bytes 1572872 | tf_op jit(solution)/shard_map/while/body/eval_jaxpr/ppermute | solution.py:22
  258.6 36.1 %collective-permute-start.1 = (bf16[128,2048]{0,1:T(8,128)(2,1)}, bf16[128,2048]{0,1:T(8,128)(2,1)}, u32[]{:S(2)}, u32[]{:S(2)}) collective-permute-start(bf16[128,2048]{0,1:T(8,128)(2,1)} %copy.123), channel_id=1, source_target_pairs={{224,0},{0,32},{32,64},{64,96},{96,128},{128,160},{160,192},{192,2... | collective-permute-start | bytes 1572872 | tf_op jit(solution)/shard_map/while/body/eval_jaxpr/ppermute | solution.py:22
  307.3 42.1 %collective-permute-start.2 = (f32[128,2048]{0,1:T(8,128)}, f32[128,2048]{0,1:T(8,128)}, u32[]{:S(2)}, u32[]{:S(2)}) collective-permute-start(f32[128,2048]{0,1:T(8,128)} %bitcast_add_fusion.5), channel_id=1, source_target_pairs={{224,0},{0,32},{32,64},{64,96},{96,128},{128,160},{160,192},{192,2... | collective-permute-start | bytes 3145736 | tf_op jit(solution)/shard_map/while/body/eval_jaxpr/ppermute | solution.py:22
  307.3 28.7 %collective-permute-start.4 = (f32[8,2,128]{2,1,0:T(2,128)}, f32[8,2,128]{2,1,0:T(2,128)}, u32[]{:S(2)}, u32[]{:S(2)}) collective-permute-start(f32[8,2,128]{2,1,0:T(2,128)} %copy.126), channel_id=1, source_target_pairs={{224,0},{0,32},{32,64},{64,96},{96,128},{128,160},{160,192},{192,2... | collective-permute-start | bytes 24584 | tf_op jit(solution)/shard_map/while/body/eval_jaxpr/ppermute | solution.py:22
  307.3 28.9 %collective-permute-start.3 = (f32[8,2,128]{2,1,0:T(2,128)}, f32[8,2,128]{2,1,0:T(2,128)}, u32[]{:S(2)}, u32[]{:S(2)}) collective-permute-start(f32[8,2,128]{2,1,0:T(2,128)} %copy.125), channel_id=1, source_target_pairs={{224,0},{0,32},{32,64},{64,96},{96,128},{128,160},{160,192},{192,2... | collective-permute-start | bytes 24584 | tf_op jit(solution)/shard_map/while/body/eval_jaxpr/ppermute | solution.py:22
  310.3 33.4 %collective-permute-start = (bf16[128,2048]{0,1:T(8,128)(2,1)S(1)}, bf16[128,2048]{0,1:T(8,128)(2,1)}, u32[]{:S(2)}, u32[]{:S(2)}) collective-permute-start(bf16[128,2048]{0,1:T(8,128)(2,1)S(1)} %copy.122), channel_id=1, source_target_pairs={{224,0},{0,32},{32,64},{64,96},{96,128},{128,160},{160,192},{192,2... | collective-permute-start | bytes 1572872 | tf_op jit(solution)/shard_map/while/body/eval_jaxpr/ppermute | solution.py:22
  314.9 34.4 %collective-permute-start.1 = (bf16[128,2048]{0,1:T(8,128)(2,1)}, bf16[128,2048]{0,1:T(8,128)(2,1)}, u32[]{:S(2)}, u32[]{:S(2)}) collective-permute-start(bf16[128,2048]{0,1:T(8,128)(2,1)} %copy.123), channel_id=1, source_target_pairs={{224,0},{0,32},{32,64},{64,96},{96,128},{128,160},{160,192},{192,2... | collective-permute-start | bytes 1572872 | tf_op jit(solution)/shard_map/while/body/eval_jaxpr/ppermute | solution.py:22
  361.9 41.2 %collective-permute-start.2 = (f32[128,2048]{0,1:T(8,128)}, f32[128,2048]{0,1:T(8,128)}, u32[]{:S(2)}, u32[]{:S(2)}) collective-permute-start(f32[128,2048]{0,1:T(8,128)} %bitcast_add_fusion.5), channel_id=1, source_target_pairs={{224,0},{0,32},{32,64},{64,96},{96,128},{128,160},{160,192},{192,2... | collective-permute-start | bytes 3145736 | tf_op jit(solution)/shard_map/while/body/eval_jaxpr/ppermute | solution.py:22
  361.9 28.7 %collective-permute-start.4 = (f32[8,2,128]{2,1,0:T(2,128)}, f32[8,2,128]{2,1,0:T(2,128)}, u32[]{:S(2)}, u32[]{:S(2)}) collective-permute-start(f32[8,2,128]{2,1,0:T(2,128)} %copy.126), channel_id=1, source_target_pairs={{224,0},{0,32},{32,64},{64,96},{96,128},{128,160},{160,192},{192,2... | collective-permute-start | bytes 24584 | tf_op jit(solution)/shard_map/while/body/eval_jaxpr/ppermute | solution.py:22
  361.9 28.9 %collective-permute-start.3 = (f32[8,2,128]{2,1,0:T(2,128)}, f32[8,2,128]{2,1,0:T(2,128)}, u32[]{:S(2)}, u32[]{:S(2)}) collective-permute-start(f32[8,2,128]{2,1,0:T(2,128)} %copy.125), channel_id=1, source_target_pairs={{224,0},{0,32},{32,64},{64,96},{96,128},{128,160},{160,192},{192,2... | collective-permute-start | bytes 24584 | tf_op jit(solution)/shard_map/while/body/eval_jaxpr/ppermute | solution.py:22
  365.7 31.8 %collective-permute-start = (bf16[128,2048]{0,1:T(8,128)(2,1)S(1)}, bf16[128,2048]{0,1:T(8,128)(2,1)}, u32[]{:S(2)}, u32[]{:S(2)}) collective-permute-start(bf16[128,2048]{0,1:T(8,128)(2,1)S(1)} %copy.122), channel_id=1, source_target_pairs={{224,0},{0,32},{32,64},{64,96},{96,128},{128,160},{160,192},{192,2... | collective-permute-start | bytes 1572872 | tf_op jit(solution)/shard_map/while/body/eval_jaxpr/ppermute | solution.py:22
  370.3 32.8 %collective-permute-start.1 = (bf16[128,2048]{0,1:T(8,128)(2,1)}, bf16[128,2048]{0,1:T(8,128)(2,1)}, u32[]{:S(2)}, u32[]{:S(2)}) collective-permute-start(bf16[128,2048]{0,1:T(8,128)(2,1)} %copy.123), channel_id=1, source_target_pairs={{224,0},{0,32},{32,64},{64,96},{96,128},{128,160},{160,192},{192,2... | collective-permute-start | bytes 1572872 | tf_op jit(solution)/shard_map/while/body/eval_jaxpr/ppermute | solution.py:22
  415.7 40.3 %collective-permute-start.2 = (f32[128,2048]{0,1:T(8,128)}, f32[128,2048]{0,1:T(8,128)}, u32[]{:S(2)}, u32[]{:S(2)}) collective-permute-start(f32[128,2048]{0,1:T(8,128)} %bitcast_add_fusion.5), channel_id=1, source_target_pairs={{224,0},{0,32},{32,64},{64,96},{96,128},{128,160},{160,192},{192,2... | collective-permute-start | bytes 3145736 | tf_op jit(solution)/shard_map/while/body/eval_jaxpr/ppermute | solution.py:22
  415.7 28.7 %collective-permute-start.4 = (f32[8,2,128]{2,1,0:T(2,128)}, f32[8,2,128]{2,1,0:T(2,128)}, u32[]{:S(2)}, u32[]{:S(2)}) collective-permute-start(f32[8,2,128]{2,1,0:T(2,128)} %copy.126), channel_id=1, source_target_pairs={{224,0},{0,32},{32,64},{64,96},{96,128},{128,160},{160,192},{192,2... | collective-permute-start | bytes 24584 | tf_op jit(solution)/shard_map/while/body/eval_jaxpr/ppermute | solution.py:22
  415.7 28.9 %collective-permute-start.3 = (f32[8,2,128]{2,1,0:T(2,128)}, f32[8,2,128]{2,1,0:T(2,128)}, u32[]{:S(2)}, u32[]{:S(2)}) collective-permute-start(f32[8,2,128]{2,1,0:T(2,128)} %copy.125), channel_id=1, source_target_pairs={{224,0},{0,32},{32,64},{64,96},{96,128},{128,160},{160,192},{192,2... | collective-permute-start | bytes 24584 | tf_op jit(solution)/shard_map/while/body/eval_jaxpr/ppermute | solution.py:22
  420.2 30.1 %collective-permute-start = (bf16[128,2048]{0,1:T(8,128)(2,1)S(1)}, bf16[128,2048]{0,1:T(8,128)(2,1)}, u32[]{:S(2)}, u32[]{:S(2)}) collective-permute-start(bf16[128,2048]{0,1:T(8,128)(2,1)S(1)} %copy.122), channel_id=1, source_target_pairs={{224,0},{0,32},{32,64},{64,96},{96,128},{128,160},{160,192},{192,2... | collective-permute-start | bytes 1572872 | tf_op jit(solution)/shard_map/while/body/eval_jaxpr/ppermute | solution.py:22
  424.8 31.2 %collective-permute-start.1 = (bf16[128,2048]{0,1:T(8,128)(2,1)}, bf16[128,2048]{0,1:T(8,128)(2,1)}, u32[]{:S(2)}, u32[]{:S(2)}) collective-permute-start(bf16[128,2048]{0,1:T(8,128)(2,1)} %copy.123), channel_id=1, source_target_pairs={{224,0},{0,32},{32,64},{64,96},{96,128},{128,160},{160,192},{192,2... | collective-permute-start | bytes 1572872 | tf_op jit(solution)/shard_map/while/body/eval_jaxpr/ppermute | solution.py:22
  468.5 39.3 %collective-permute-start.2 = (f32[128,2048]{0,1:T(8,128)}, f32[128,2048]{0,1:T(8,128)}, u32[]{:S(2)}, u32[]{:S(2)}) collective-permute-start(f32[128,2048]{0,1:T(8,128)} %bitcast_add_fusion.5), channel_id=1, source_target_pairs={{224,0},{0,32},{32,64},{64,96},{96,128},{128,160},{160,192},{192,2... | collective-permute-start | bytes 3145736 | tf_op jit(solution)/shard_map/while/body/eval_jaxpr/ppermute | solution.py:22
  468.5 28.0 %collective-permute-start.4 = (f32[8,2,128]{2,1,0:T(2,128)}, f32[8,2,128]{2,1,0:T(2,128)}, u32[]{:S(2)}, u32[]{:S(2)}) collective-permute-start(f32[8,2,128]{2,1,0:T(2,128)} %copy.126), channel_id=1, source_target_pairs={{224,0},{0,32},{32,64},{64,96},{96,128},{128,160},{160,192},{192,2... | collective-permute-start | bytes 24584 | tf_op jit(solution)/shard_map/while/body/eval_jaxpr/ppermute | solution.py:22
  469.1 27.5 %collective-permute-start.3 = (f32[8,2,128]{2,1,0:T(2,128)}, f32[8,2,128]{2,1,0:T(2,128)}, u32[]{:S(2)}, u32[]{:S(2)}) collective-permute-start(f32[8,2,128]{2,1,0:T(2,128)} %copy.125), channel_id=1, source_target_pairs={{224,0},{0,32},{32,64},{64,96},{96,128},{128,160},{160,192},{192,2... | collective-permute-start | bytes 24584 | tf_op jit(solution)/shard_map/while/body/eval_jaxpr/ppermute | solution.py:22
  473.7 28.5 %collective-permute-start = (bf16[128,2048]{0,1:T(8,128)(2,1)S(1)}, bf16[128,2048]{0,1:T(8,128)(2,1)}, u32[]{:S(2)}, u32[]{:S(2)}) collective-permute-start(bf16[128,2048]{0,1:T(8,128)(2,1)S(1)} %copy.122), channel_id=1, source_target_pairs={{224,0},{0,32},{32,64},{64,96},{96,128},{128,160},{160,192},{192,2... | collective-permute-start | bytes 1572872 | tf_op jit(solution)/shard_map/while/body/eval_jaxpr/ppermute | solution.py:22
  478.3 29.5 %collective-permute-start.1 = (bf16[128,2048]{0,1:T(8,128)(2,1)}, bf16[128,2048]{0,1:T(8,128)(2,1)}, u32[]{:S(2)}, u32[]{:S(2)}) collective-permute-start(bf16[128,2048]{0,1:T(8,128)(2,1)} %copy.123), channel_id=1, source_target_pairs={{224,0},{0,32},{32,64},{64,96},{96,128},{128,160},{160,192},{192,2... | collective-permute-start | bytes 1572872 | tf_op jit(solution)/shard_map/while/body/eval_jaxpr/ppermute | solution.py:22
  509.0 17.8 %copy-start.3 = (bf16[128,1024]{1,0:T(8,128)(2,1)}, bf16[128,1024]{1,0:T(8,128)(2,1)S(1)}, u32[]{:S(2)}) copy-start(bf16[128,1024]{1,0:T(8,128)(2,1)S(1)} %copy.75) | copy-start | bytes 786436
  526.9 134.7 %copy-start.2 = (f32[128,1024]{0,1:T(8,128)S(1)}, f32[128,1024]{0,1:T(8,128)}, u32[]{:S(2)}) copy-start(f32[128,1024]{0,1:T(8,128)} %get-tuple-element.362) | copy-start | bytes 1572868
  526.9 172.8 %reduce-scatter.5.cloned.1.call-start = ((), (), s32[]{:S(2)}) async-start(), calls=%async_computation.2 | async-start | bytes 1179648 | tf_op jit(solution)/shard_map/reduce_scatter | solution.py:158
Sparse Core Ops, SparseCore 0:
  10.3 49.9 all-gather.2
  527.0 130.0 reduce-scatter.6
  659.8 39.8 reduce-scatter.4
where the time goes:
time: 713 us; the launch traced here: 708 us
  waiting for transfers between devices  453 us (64%)
  local copies, waits for them, and re-layouts  84.6 us (12%)
  starting transfers between devices  60.7 us (9%)
  other arithmetic  54 us (8%)
  matrix products  41.4 us (6%)
  between operations  13.8 us (2%)
    ppermute x40, waiting for transfers between devices, from_behind(): return lax.ppermute(block, axis, route)  249 us
    unnamed x4, waiting for transfers between devices  130 us
    ppermute x40, starting transfers between devices, from_behind(): return lax.ppermute(block, axis, route)  60.5 us
    while x40, local copies, waits for them, and re-layouts  52.1 us
    reduce_scatter x1, waiting for transfers between devices, body(): lax.psum_scatter(partial_sum, 'ctx', scatter_dimension=1, tiled=True)  37.3 us
    all_gather x1, waiting for transfers between devices, body(): slice_part = lax.all_gather(rows_of_key, 'ctx', axis=0, tiled=True)  36.5 us
    unnamed x14, local copies, waits for them, and re-layouts  21.5 us
    add x8, other arithmetic, query_step(): moved = from_behind((moved[0] + query_part, moved[1], moved[2]), 'ctx', 1)  18.5 us
  transfers between devices with their start and end apart: 43, of which 35 were waited for; matrix products, arithmetic and copies ran while one was open for 7% of the time, Pallas kernels for 0%

commit v1 on v0

v1 whole, which is shorter than its diff:
```python
import math

import jax
import jax.numpy as jnp
from jax import lax
from jax.experimental import pallas as pl
from jax.experimental.pallas import tpu as pltpu
from jax.sharding import PartitionSpec as P

ROWS = 128
HEAD = 128
BLOCKS = 8
TAIL = 16
PACKED = 768
BACK = 512
CAP = 50.0
SCALE = 144.0 ** (-0.5)
BF = jnp.bfloat16
F32 = jnp.float32
OFFSETS = [(a, b) for a in range(2) for b in range(4)]
VMEM_LIMIT = 48 * 1024 * 1024


def spread(block, place):
    route = []
    for ctx in range(8):
        for dp in range(32):
            here = (dp // 8, ctx % 4, (dp // 2) % 4 * 2 + ctx // 4, dp % 2)
            x, y, z, core = place(*here)
            x, y, z = x % 4, y % 4, z % 8
            route.append((ctx * 32 + dp, ((z % 2) * 4 + y) * 32 + x * 8 + z // 2 * 2 + core))
    return lax.ppermute(block, ("ctx", "dp"), route)


def nt(left, right):
    return lax.dot_general(left, right, (((1,), (1,)), ((), ())), preferred_element_type=F32)


def nn(left, right):
    return lax.dot_general(left, right, (((1,), (0,)), ((), ())), preferred_element_type=F32)


def partner(mine, a, b, sign):
    return ((mine // 4) ^ a) * 4 + (mine + sign * b) % 4


def split_three(value):
    first = value.astype(BF)
    rest = value - first.astype(F32)
    second = rest.astype(BF)
    third = (rest - second.astype(F32)).astype(BF)
    return first, second, third


def pack_kernel(where, q, k, v, do, o, *outs):
    mine = where[0]
    product = do[...].astype(F32) * o[...].astype(F32)
    high = product.astype(BF)
    low = (product - high.astype(F32)).astype(BF)
    row = lax.broadcasted_iota(jnp.int32, (TAIL, 2048), 0)
    col = lax.broadcasted_iota(jnp.int32, (TAIL, 2048), 1)
    pick = (row == col // HEAD).astype(BF)
    delta = nt(pick, high) + nt(pick, low)
    first, second, third = split_three(delta)
    for (a, b), out in zip(OFFSETS, outs):
        target = partner(mine, a, b, 1)
        wide = pl.ds(pl.multiple_of(target * 256, 256), 256)
        thin = pl.ds(pl.multiple_of(target * 128, 128), 128)
        out[0:ROWS, 0:256] = q[:, wide]
        out[0:ROWS, 256:512] = do[:, wide]
        out[0:ROWS, 512:640] = k[:, thin]
        out[0:ROWS, 640:768] = v[:, thin]
        out[ROWS:, 0:128] = first
        out[ROWS:, 128:256] = second
        out[ROWS:, 256:384] = third
        out[ROWS:, 384:768] = jnp.zeros((TAIL, 384), BF)


def attention_kernel(where, lengths, *refs):
    pieces = refs[:8]
    backs = refs[8:16]
    values_a, values_b = refs[16:18]
    held, key_turned, dq, dk, dv, sems = refs[18:]
    mine = where[0]
    core = where[1]
    copies = []
    for n, ((a, b), piece) in enumerate(zip(OFFSETS, pieces)):
        copy = pltpu.make_async_copy(piece, held.at[partner(mine, a, b, -1)], sems.at[n])
        copy.start()
        copies.append(copy)
    dk[...] = jnp.zeros_like(dk)
    dv[...] = jnp.zeros_like(dv)
    ends = []
    total = 0
    for d in range(8):
        total = total + lengths[0, d]
        ends.append(total)
    for copy in copies:
        copy.wait()
    for n in range(BLOCKS):
        key_turned[n] = held[n, 0:ROWS, 512:640].T

    def block(b, carry):
        base = b * ROWS
        first = 0
        for end in ends:
            first = jnp.where(base >= end, end, first)
        kb0 = first // ROWS
        count = b - kb0 + 1
        lane = lax.broadcasted_iota(jnp.int32, (1, 256), 1)
        query = base + lane % ROWS
        begin = jnp.zeros((1, 256), jnp.int32)
        for end in ends:
            begin = jnp.where(query >= end, end, begin)
        tail = held[b, ROWS:, 0:384].astype(F32)
        tail = tail[:, 0:128] + tail[:, 128:256] + tail[:, 256:384]
        head = lax.broadcasted_iota(jnp.int32, (TAIL, 128), 0)
        delta = jnp.concatenate(
            [
                jnp.sum(jnp.where(head == 2 * mine + s, tail, 0.0), axis=0, keepdims=True)
                for s in range(2)
            ],
            axis=1,
        )
        queries = jnp.concatenate([held[b, 0:ROWS, 0:128], held[b, 0:ROWS, 128:256]], axis=0)
        grads = jnp.concatenate([held[b, 0:ROWS, 256:384], held[b, 0:ROWS, 384:512]], axis=0)
        sub = lax.broadcasted_iota(jnp.int32, (ROWS, 256), 0)

        def window(number):
            powers, tanhs = [], []
            sums = jnp.zeros((1, 256), F32)
            for n in range(number):
                kb = kb0 + n
                raw = nt(held[kb, 0:ROWS, 512:640], queries)
                tanh = jnp.tanh(raw * (SCALE / CAP))
                key = sub + kb * ROWS
                live = key >= begin
                if n == number - 1:
                    live = live & (key <= query)
                power = jnp.where(live, jnp.exp(CAP * tanh), 0.0)
                sums = sums + jnp.sum(power, axis=0, keepdims=True)
                powers.append(power)
                tanhs.append(tanh)
            inverse = 1.0 / sums
            turned = jnp.zeros((HEAD, 256), F32)
            for n in range(number):
                kb = kb0 + n
                prob = powers[n] * inverse
                dprob = nt(held[kb, 0:ROWS, 640:768], grads)
                slope = SCALE - (SCALE * tanhs[n]) * tanhs[n]
                dscore = (prob * (dprob - delta) * slope).astype(BF)
                dv[kb] += nn(prob.astype(BF), grads)
                dk[kb] += nn(dscore, queries)
                turned = turned + nn(key_turned[kb], dscore)
            straight = turned.T
            dq[b, :, 0:128] = straight[0:ROWS].astype(BF)
            dq[b, :, 128:256] = straight[ROWS:].astype(BF)

        for number in range(1, 6):

            @pl.when(count == number)
            def _():
                window(number)

        return carry

    lax.fori_loop(0, BLOCKS, block, 0)
    for (a, b), back in zip(OFFSETS, backs):
        target = partner(mine, a, b, 1)
        back[:, 0:256] = dq[target]
        back[:, 256:384] = dk[target].astype(BF)
        back[:, 384:512] = dv[target].astype(BF)
    for n in range(4):
        values_a[n * ROWS : (n + 1) * ROWS, :] = dv[core * 4 + n].astype(BF)
        values_b[n * ROWS : (n + 1) * ROWS, :] = dv[(1 - core) * 4 + n].astype(BF)


def turn_kernel(where, *refs):
    pieces, out = refs[:8], refs[8]
    held, sems = refs[9:]
    mine, core = where[0], where[1]
    copies = []
    for n in range(8):
        pack = core if n < 4 else 1 - core
        slot = pack * 4 + (mine - n % 4) % 4
        copy = pltpu.make_async_copy(pieces[n], held.at[slot], sems.at[n])
        copy.start()
        copies.append(copy)
    for copy in copies:
        copy.wait()

    @pl.loop(0, 8)
    def _(n):
        out[n] = held[n].T


def weight_kernel(where, turned, *refs):
    pieces = refs[:8]
    outs = refs[8:12]
    left, right, sems = refs[12:]
    mine, core, x = where[0], where[1], where[2]
    half = mine // 4
    copies = []
    for n in range(8):
        copy = pltpu.make_async_copy(
            turned.at[n], left.at[:, pl.ds(n * ROWS, ROWS)], sems.at[8 + n]
        )
        copy.start()
        copies.append(copy)
    for n in range(8):
        pack = half if n < 4 else 1 - half
        source = (mine - n % 4) % 4
        copy = pltpu.make_async_copy(
            pieces[n],
            right.at[
                pl.ds(pl.multiple_of(pack * 512, 512), 512),
                pl.ds(pl.multiple_of(source * 128, 128), 128),
            ],
            sems.at[n],
        )
        copy.start()
        copies.append(copy)
    for copy in copies:
        copy.wait()
    factor = 1.0 / math.sqrt(32768.0)
    for step, out in enumerate(outs):
        target = (x + step) % 4
        rows = left[pl.ds(pl.multiple_of(target * 288, 32), 288), :]
        out[...] = (nn(rows, right[...]) * factor).astype(BF)


def sum_kernel(where, first, second, third, fourth, *outs):
    z = where[3]
    total = first[...].astype(F32) + second[...].astype(F32)
    total = total + third[...].astype(F32) + fourth[...].astype(F32)
    total = total.astype(BF)
    blocks = [
        total[u * 144 : (u + 1) * 144, w * 128 : (w + 1) * 128] for w in range(4) for u in range(2)
    ]
    for m, value in enumerate(blocks):
        for step, out in enumerate(outs):

            @pl.when((z ^ step) == m)
            def _():
                out[...] = value


def last_kernel(*refs):
    total = refs[0][...].astype(F32)
    for ref in refs[1:8]:
        total = total + ref[...].astype(F32)
    refs[8][...] = total


def unpack_kernel(where, *refs):
    pieces = refs[:8]
    query_grad, key_grad, value_grad = refs[8:]
    mine = where[0]
    for (a, b), piece in zip(OFFSETS, pieces):
        source = partner(mine, a, b, -1)
        wide = pl.ds(pl.multiple_of(source * 256, 256), 256)
        thin = pl.ds(pl.multiple_of(source * 128, 128), 128)
        query_grad[:, wide] = piece[:, 0:256]
        key_grad[:, thin] = piece[:, 256:384]
        value_grad[:, thin] = piece[:, 384:512]


SMEM = pl.BlockSpec(memory_space=pltpu.SMEM)
VMEM = pl.BlockSpec(memory_space=pltpu.VMEM)
ANY = pl.BlockSpec(memory_space=pl.ANY)


def shape(*dims, dtype=BF):
    return jax.ShapeDtypeStruct(dims, dtype)


def call(kernel, outs, ins, scratch=(), flops=0, moved=0):
    return pl.pallas_call(
        kernel,
        out_shape=outs,
        in_specs=ins,
        out_specs=jax.tree.map(lambda _: VMEM, outs),
        scratch_shapes=list(scratch),
        compiler_params=pltpu.CompilerParams(vmem_limit_bytes=VMEM_LIMIT),
        cost_estimate=pl.CostEstimate(flops=flops, bytes_accessed=moved, transcendentals=0),
    )


def body(
    queries, key_states, value_states, saved_output, output_grad, layer_input, document_lengths
):
    mine = lax.axis_index("ctx")
    dp = lax.axis_index("dp")
    core = dp % 2
    where = jnp.stack([mine, core, dp // 8, dp // 2 % 4 * 2 + mine // 4]).astype(jnp.int32)

    packed = call(pack_kernel, [shape(ROWS + TAIL, PACKED)] * 8, [SMEM] + [VMEM] * 5)(
        where, queries[0], key_states[0], value_states[0], output_grad[0], saved_output[0]
    )
    arrived = [packed[0]]
    for (a, b), block in list(zip(OFFSETS, packed))[1:]:
        arrived.append(spread(block, lambda x, y, z, c: (x, y + b, z ^ a, c)))

    inputs = layer_input[0]
    y = mine % 4
    own = []
    for b in range(4):
        piece = lax.dynamic_slice(inputs, (0, (y + b) % 4 * 1152), (ROWS, 1152))
        own.append(spread(piece, lambda x, y, z, c: (x, y + b, z, c)) if b else piece)
    other = [spread(piece, lambda x, y, z, c: (x, y, z, 1 - c)) for piece in own]
    turned = call(
        turn_kernel,
        shape(8, 1152, ROWS),
        [SMEM] + [ANY] * 8,
        [pltpu.VMEM((8, ROWS, 1152), BF), pltpu.SemaphoreType.DMA((8,))],
    )(where, *own, *other)

    results = call(
        attention_kernel,
        [shape(ROWS, BACK)] * 8 + [shape(512, HEAD)] * 2,
        [SMEM, SMEM] + [ANY] * 8,
        [
            pltpu.VMEM((BLOCKS, ROWS + TAIL, PACKED), BF),
            pltpu.VMEM((BLOCKS, HEAD, ROWS), BF),
            pltpu.VMEM((BLOCKS, ROWS, 256), BF),
            pltpu.VMEM((BLOCKS, ROWS, HEAD), F32),
            pltpu.VMEM((BLOCKS, ROWS, HEAD), F32),
            pltpu.SemaphoreType.DMA((8,)),
        ],
        flops=4_000_000_000,
        moved=4_000_000,
    )(where, document_lengths, *arrived)
    backs, values_a, values_b = results[:8], results[8], results[9]

    gathered = []
    for b in range(4):
        gathered.append(
            spread(values_a, lambda x, y, z, c: (x, y + b, z // 2 * 2 + c, z % 2))
        )
    for b in range(4):
        gathered.append(
            spread(values_b, lambda x, y, z, c: (x, y + b, z // 2 * 2 + 1 - c, z % 2))
        )

    parts = call(
        weight_kernel,
        [shape(288, 512)] * 4,
        [SMEM, ANY] + [ANY] * 8,
        [
            pltpu.VMEM((1152, 1024), BF),
            pltpu.VMEM((1024, 512), BF),
            pltpu.SemaphoreType.DMA((16,)),
        ],
        flops=1_300_000_000,
        moved=4_000_000,
    )(where, turned, *gathered)
    reduced = [parts[0]]
    for step in range(1, 4):
        reduced.append(spread(parts[step], lambda x, y, z, c: (x + step, y, z, c)))
    blocks = call(sum_kernel, [shape(144, 128)] * 8, [SMEM] + [VMEM] * 4)(where, *reduced)
    landed = []
    for step in range(8):
        landed.append(
            spread(
                blocks[step],
                lambda x, y, z, c: (y, (z ^ step) // 2, 2 * x + c, (z ^ step) % 2),
            )
        )
    weight_grad = call(last_kernel, shape(144, 128, dtype=F32), [VMEM] * 8)(*landed)

    returned = [backs[0]]
    for (a, b), block in list(zip(OFFSETS, backs))[1:]:
        returned.append(spread(block, lambda x, y, z, c: (x, y + b, z ^ a, c)))
    query_grad, key_grad, value_grad = call(
        unpack_kernel,
        [shape(ROWS, 2048), shape(ROWS, 1024), shape(ROWS, 1024)],
        [SMEM] + [VMEM] * 8,
    )(where, *returned)
    return query_grad[None], key_grad[None], value_grad[None], weight_grad


def solution(mesh):
    return jax.shard_map(
        body,
        mesh=mesh,
        in_specs=(P("dp", "ctx", None),) * 6 + (P("dp", None),),
        out_specs=(P("dp", "ctx", None),) * 3 + (P("dp", "ctx"),),
        check_vma=False,
    )
```

time: 713 us -> 153 us (0.21)
  the two profiles are of different devices: /device:TPU:32 before, /device:TPU:15 now
where the time goes in v1:
time: 153 us; the launch traced here: 152 us
  starting transfers between devices  91.8 us (60%)
  waiting for transfers between devices  33.1 us (22%)
  Pallas kernels  20.1 us (13%)
  local copies, waits for them, and re-layouts  6.36 us (4%)
    ppermute x40, starting transfers between devices, spread(): return lax.ppermute(block, ('ctx', 'dp'), route)  91.8 us
    ppermute x40, waiting for transfers between devices, spread(): return lax.ppermute(block, ('ctx', 'dp'), route)  33.1 us
    pallas_call x1, Pallas kernels, body(): call(attention_kernel, [shape(ROWS, BACK)] * 8 + [shape(512, HEAD)] * 2,...  10.3 us
    unnamed x12, local copies, waits for them, and re-layouts  5.03 us
  transfers between devices with their start and end apart: 40, of which 12 were waited for; matrix products, arithmetic and copies ran while one was open for 1% of the time, Pallas kernels for 10%

profile of v1, /device:TPU:15, one launch (start us, length us, event | category | flops | bytes accessed | tf_op | source)
XLA Modules:
  0.0 152.3 jit_solution(14074353400437374109)
XLA Ops:
  0.8 1.0 copy-done
  1.8 1.0 copy-done.1
  2.9 1.0 copy-done.2
  3.9 0.9 copy-done.3
  4.8 0.9 copy-done.4
  5.8 1.1 shard_map.102
  6.9 1.4 collective-permute-start
  8.2 0.8 collective-permute-start.1
  9.1 2.0 %collective-permute-start.2 = (bf16[144,768]{1,0:T(8,128)(2,1)S(1)}, bf16[144,768]{1,0:T(8,128)(2,1)S(1)}, u32[]{:S(2)}, u32[]{:S(2)}) collective-permute-start(bf16[144,768]{1,0:T(8,128)(2,1)S(1)} %get-tuple-element.40), channel_id=1, source_target_pairs={{0,96},{1,97},{2,98},{3,99},{4,100},{5,101},{6,102},{7,103},{8,104... | collective-permute-start | bytes 663560 | tf_op jit(solution)/shard_map/ppermute | solution.py:32
  11.0 1.6 %collective-permute-start.3 = (bf16[144,768]{1,0:T(8,128)(2,1)S(1)}, bf16[144,768]{1,0:T(8,128)(2,1)S(1)}, u32[]{:S(2)}, u32[]{:S(2)}) collective-permute-start(bf16[144,768]{1,0:T(8,128)(2,1)S(1)} %get-tuple-element.41), channel_id=1, source_target_pairs={{0,128},{1,129},{2,130},{3,131},{4,132},{5,133},{6,134},{7,135},{8... | collective-permute-start | bytes 663560 | tf_op jit(solution)/shard_map/ppermute | solution.py:32
  12.7 1.3 dynamic-slice_bitcast_fusion
  14.0 1.3 collective-permute-start.16
  15.8 7.0 %collective-permute-start.14 = (bf16[128,1152]{1,0:T(8,128)(2,1)S(1)}, bf16[128,1152]{1,0:T(8,128)(2,1)S(1)}, u32[]{:S(2)}, u32[]{:S(2)}) collective-permute-start(bf16[128,1152]{1,0:T(8,128)(2,1)S(1)} %get-tuple-element.71), channel_id=1, source_target_pairs={{0,32},{1,33},{2,34},{3,35},{4,36},{5,37},{6,38},{7,39},{8,40},{9,... | collective-permute-start | bytes 884744 | tf_op jit(solution)/shard_map/ppermute | solution.py:32
  22.8 4.4 %collective-permute-start.15 = (bf16[128,1152]{1,0:T(8,128)(2,1)S(1)}, bf16[128,1152]{1,0:T(8,128)(2,1)S(1)}, u32[]{:S(2)}, u32[]{:S(2)}) collective-permute-start(bf16[128,1152]{1,0:T(8,128)(2,1)S(1)} %get-tuple-element.73), channel_id=1, source_target_pairs={{0,64},{1,65},{2,66},{3,67},{4,68},{5,69},{6,70},{7,71},{8,72},{9,... | collective-permute-start | bytes 884744 | tf_op jit(solution)/shard_map/ppermute | solution.py:32
  27.2 1.4 collective-permute-start.5
  29.3 7.3 %collective-permute-done.5.refs_6_ = bf16[144,768]{1,0:T(8,128)(2,1)S(1)} collective-permute-done((bf16[144,768]{1,0:T(8,128)(2,1)S(1)}, bf16[144,768]{1,0:T(8,128)(2,1)S(1)}, u32[]{:S(2)}, u32[]{:S(2)}) %collective-permute-start.5) | collective-permute-done | bytes 221216 | tf_op jit(solution)/shard_map/ppermute | solution.py:32
  36.6 5.6 %collective-permute-start.17 = (bf16[128,1152]{1,0:T(8,128)(2,1)S(1)}, bf16[128,1152]{1,0:T(8,128)(2,1)S(1)}, u32[]{:S(2)}, u32[]{:S(2)}) collective-permute-start(bf16[128,1152]{1,0:T(8,128)(2,1)S(1)} %get-tuple-element.72.refs_0_), channel_id=1, source_target_pairs={{0,1},{1,0},{2,3},{3,2},{4,5},{5,4},{6,7},{7,6},{8,9},{9,8},{10,11... | collective-permute-start | bytes 884744 | tf_op jit(solution)/shard_map/ppermute | solution.py:32
  42.7 2.6 %collective-permute-done.15.refs_2_ = bf16[128,1152]{1,0:T(8,128)(2,1)S(1)} collective-permute-done((bf16[128,1152]{1,0:T(8,128)(2,1)S(1)}, bf16[128,1152]{1,0:T(8,128)(2,1)S(1)}, u32[]{:S(2)}, u32[]{:S(2)}) %collective-permute-start.15) | collective-permute-done | bytes 294944 | tf_op jit(solution)/shard_map/ppermute | solution.py:32
  45.3 3.9 %collective-permute-start.19 = (bf16[128,1152]{1,0:T(8,128)(2,1)S(1)}, bf16[128,1152]{1,0:T(8,128)(2,1)S(1)}, u32[]{:S(2)}, u32[]{:S(2)}) collective-permute-start(bf16[128,1152]{1,0:T(8,128)(2,1)S(1)} %collective-permute-done.15.refs_2_), channel_id=1, source_target_pairs={{0,1},{1,0},{2,3},{3,2},{4,5},{5,4},{6,7},{7,6},{8,9},{9,8},{10,11... | collective-permute-start | bytes 884744 | tf_op jit(solution)/shard_map/ppermute | solution.py:32
  49.2 10.3 %shard_map.103 = (bf16[128,512]{1,0:T(8,128)(2,1)S(1)}, bf16[128,512]{1,0:T(8,128)(2,1)S(1)}, bf16[128,512]{1,0:T(8,128)(2,1)S(1)}, bf16[128,512]{1,0:T(8,128)(2...) custom-call(s32[4]{0:T(128)S(1)} %pad_add_fusion.where, ...), custom_call_target="tpu_custom_call" | custom-call | flops 4000000000 | bytes 4000000 | tf_op jit(solution)/shard_map/pallas_call | solution.py:318
  59.6 0.7 collective-permute-start.23
  60.3 5.4 %collective-permute-done.24.refs_3_ = bf16[512,128]{1,0:T(8,128)(2,1)S(1)} collective-permute-done((bf16[512,128]{1,0:T(8,128)(2,1)S(1)}, bf16[512,128]{1,0:T(8,128)(2,1)S(1)}, u32[]{:S(2)}, u32[]{:S(2)}) %collective-permute-start.24) | collective-permute-done | bytes 131104 | tf_op jit(solution)/shard_map/ppermute | solution.py:32
  65.8 1.6 %collective-permute-done.23.refs_2_ = bf16[512,128]{1,0:T(8,128)(2,1)S(1)} collective-permute-done((bf16[512,128]{1,0:T(8,128)(2,1)S(1)}, bf16[512,128]{1,0:T(8,128)(2,1)S(1)}, u32[]{:S(2)}, u32[]{:S(2)}) %collective-permute-start.23) | collective-permute-done | bytes 131104 | tf_op jit(solution)/shard_map/ppermute | solution.py:32
  67.4 3.5 %collective-permute-start.21 = (bf16[512,128]{1,0:T(8,128)(2,1)S(1)}, bf16[512,128]{1,0:T(8,128)(2,1)S(1)}, u32[]{:S(2)}, u32[]{:S(2)}) collective-permute-start(bf16[512,128]{1,0:T(8,128)(2,1)S(1)} %get-tuple-element.56), channel_id=1, source_target_pairs={{0,0},{1,128},{2,2},{3,130},{4,4},{5,132},{6,6},{7,134},{8,8},{9,1... | collective-permute-start | bytes 393224 | tf_op jit(solution)/shard_map/ppermute | solution.py:32
  71.1 1.9 %collective-permute-start.28 = (bf16[512,128]{1,0:T(8,128)(2,1)S(1)}, bf16[512,128]{1,0:T(8,128)(2,1)S(1)}, u32[]{:S(2)}, u32[]{:S(2)}) collective-permute-start(bf16[512,128]{1,0:T(8,128)(2,1)S(1)} %get-tuple-element.57), channel_id=1, source_target_pairs={{0,224},{1,96},{2,226},{3,98},{4,228},{5,100},{6,230},{7,102},{8,2... | collective-permute-start | bytes 393224 | tf_op jit(solution)/shard_map/ppermute | solution.py:32
  73.0 1.2 collective-permute-start.27
  74.2 2.1 %collective-permute-start.26 = (bf16[512,128]{1,0:T(8,128)(2,1)S(1)}, bf16[512,128]{1,0:T(8,128)(2,1)S(1)}, u32[]{:S(2)}, u32[]{:S(2)}) collective-permute-start(bf16[512,128]{1,0:T(8,128)(2,1)S(1)} %get-tuple-element.57), channel_id=1, source_target_pairs={{0,160},{1,32},{2,162},{3,34},{4,164},{5,36},{6,166},{7,38},{8,168... | collective-permute-start | bytes 393224 | tf_op jit(solution)/shard_map/ppermute | solution.py:32
  76.2 2.2 %shard_map.105.turned = bf16[8,1152,128]{2,1,0:T(8,128)(2,1)S(1)} custom-call(s32[4]{0:T(128)S(1)} %pad_add_fusion.where, bf16[128,1152]{1,0:T(8,128)(2,1)S(1)} %get-tuple-element.72.refs_0_, bf16[128,1152]{1,0:T(8,128)(2,1)S(1)} %collective-permute-done.14.refs_1_, bf16[128,1152]{1,0:T(8,128)(2,1)S(1)} %collective-permute-done.15.refs_2_, ...), custom_call_target="tpu_custom_call" | custom-call | tf_op jit(solution)/shard_map/pallas_call | solution.py:311
  78.5 0.9 collective-permute-done.27.refs_6_
  79.4 2.7 %collective-permute-done.26.refs_5_ = bf16[512,128]{1,0:T(8,128)(2,1)S(1)} collective-permute-done((bf16[512,128]{1,0:T(8,128)(2,1)S(1)}, bf16[512,128]{1,0:T(8,128)(2,1)S(1)}, u32[]{:S(2)}, u32[]{:S(2)}) %collective-permute-start.26) | collective-permute-done | bytes 131104 | tf_op jit(solution)/shard_map/ppermute | solution.py:32
  82.1 3.0 %shard_map.106 = (bf16[288,512]{1,0:T(8,128)(2,1)S(1)}, bf16[288,512]{1,0:T(8,128)(2,1)S(1)}, bf16[288,512]{1,0:T(8,128)(2,1)S(1)}, bf16[288,512]{1,0:T(8,128)(2,1)S(1)}) custom-call(s32[4]{0:T(128)S(1)} %pad_add_fusion.where, bf16[8,1152,128]{2,1,0:T(8,128)(2,1)S(1)} %shard_map.105.turned, bf16[512,128]{1,0:T(8,128)(2,1)S(1)} %collective-permute-done.21.refs_0_, ...), custom_call_target="tpu_custom_call" | custom-call | flops 1300000000 | bytes 4000000 | tf_op jit(solution)/shard_map/pallas_call | solution.py:345
  85.2 2.3 %collective-permute-start.30 = (bf16[288,512]{1,0:T(8,128)(2,1)S(1)}, bf16[288,512]{1,0:T(8,128)(2,1)S(1)}, u32[]{:S(2)}, u32[]{:S(2)}) collective-permute-start(bf16[288,512]{1,0:T(8,128)(2,1)S(1)} %get-tuple-element.60), channel_id=1, source_target_pairs={{0,16},{1,17},{2,18},{3,19},{4,20},{5,21},{6,22},{7,23},{8,24},{9,... | collective-permute-start | bytes 884744 | tf_op jit(solution)/shard_map/ppermute | solution.py:32
  87.8 3.2 %collective-permute-start.8 = (bf16[128,512]{1,0:T(8,128)(2,1)S(1)}, bf16[128,512]{1,0:T(8,128)(2,1)S(1)}, u32[]{:S(2)}, u32[]{:S(2)}) collective-permute-start(bf16[128,512]{1,0:T(8,128)(2,1)S(1)} %get-tuple-element.47), channel_id=1, source_target_pairs={{0,64},{1,65},{2,66},{3,67},{4,68},{5,69},{6,70},{7,71},{8,72},{9,... | collective-permute-start | bytes 393224 | tf_op jit(solution)/shard_map/ppermute | solution.py:32
  91.0 0.9 collective-permute-done.7.refs_1_
  91.9 6.0 %collective-permute-start.9 = (bf16[128,512]{1,0:T(8,128)(2,1)S(1)}, bf16[128,512]{1,0:T(8,128)(2,1)S(1)}, u32[]{:S(2)}, u32[]{:S(2)}) collective-permute-start(bf16[128,512]{1,0:T(8,128)(2,1)S(1)} %get-tuple-element.48), channel_id=1, source_target_pairs={{0,96},{1,97},{2,98},{3,99},{4,100},{5,101},{6,102},{7,103},{8,104... | collective-permute-start | bytes 393224 | tf_op jit(solution)/shard_map/ppermute | solution.py:32
  97.9 0.9 collective-permute-start.10
  98.9 2.7 %collective-permute-start.12 = (bf16[128,512]{1,0:T(8,128)(2,1)S(1)}, bf16[128,512]{1,0:T(8,128)(2,1)S(1)}, u32[]{:S(2)}, u32[]{:S(2)}) collective-permute-start(bf16[128,512]{1,0:T(8,128)(2,1)S(1)} %get-tuple-element.51), channel_id=1, source_target_pairs={{0,192},{1,193},{2,194},{3,195},{4,196},{5,197},{6,198},{7,199},{8... | collective-permute-start | bytes 393224 | tf_op jit(solution)/shard_map/ppermute | solution.py:32
  101.5 0.8 collective-permute-done.31.fourth
  102.3 2.3 %collective-permute-start.13 = (bf16[128,512]{1,0:T(8,128)(2,1)S(1)}, bf16[128,512]{1,0:T(8,128)(2,1)S(1)}, u32[]{:S(2)}, u32[]{:S(2)}) collective-permute-start(bf16[128,512]{1,0:T(8,128)(2,1)S(1)} %get-tuple-element.52), channel_id=1, source_target_pairs={{0,224},{1,225},{2,226},{3,227},{4,228},{5,229},{6,230},{7,231},{8... | collective-permute-start | bytes 393224 | tf_op jit(solution)/shard_map/ppermute | solution.py:32
  104.6 1.1 shard_map.107
  105.7 11.0 %collective-permute-start.32 = (bf16[144,128]{1,0:T(8,128)(2,1)S(1)}, bf16[144,128]{1,0:T(8,128)(2,1)S(1)}, u32[]{:S(2)}, u32[]{:S(2)}) collective-permute-start(bf16[144,128]{1,0:T(8,128)(2,1)S(1)} %get-tuple-element.62), channel_id=1, source_target_pairs={{0,0},{1,128},{2,32},{3,160},{4,64},{5,192},{6,96},{7,224},{8,2},{... | collective-permute-start | bytes 110600 | tf_op jit(solution)/shard_map/ppermute | solution.py:32
  116.9 2.4 %collective-permute-start.34 = (bf16[144,128]{1,0:T(8,128)(2,1)S(1)}, bf16[144,128]{1,0:T(8,128)(2,1)S(1)}, u32[]{:S(2)}, u32[]{:S(2)}) collective-permute-start(bf16[144,128]{1,0:T(8,128)(2,1)S(1)} %get-tuple-element.64), channel_id=1, source_target_pairs={{0,32},{1,160},{2,0},{3,128},{4,96},{5,224},{6,64},{7,192},{8,34},... | collective-permute-start | bytes 110600 | tf_op jit(solution)/shard_map/ppermute | solution.py:32
  119.3 6.6 %collective-permute-start.36 = (bf16[144,128]{1,0:T(8,128)(2,1)S(1)}, bf16[144,128]{1,0:T(8,128)(2,1)S(1)}, u32[]{:S(2)}, u32[]{:S(2)}) collective-permute-start(bf16[144,128]{1,0:T(8,128)(2,1)S(1)} %get-tuple-element.66), channel_id=1, source_target_pairs={{0,64},{1,192},{2,96},{3,224},{4,0},{5,128},{6,32},{7,160},{8,66},... | collective-permute-start | bytes 110600 | tf_op jit(solution)/shard_map/ppermute | solution.py:32
  125.9 5.9 %collective-permute-start.37 = (bf16[144,128]{1,0:T(8,128)(2,1)S(1)}, bf16[144,128]{1,0:T(8,128)(2,1)S(1)}, u32[]{:S(2)}, u32[]{:S(2)}) collective-permute-start(bf16[144,128]{1,0:T(8,128)(2,1)S(1)} %get-tuple-element.67), channel_id=1, source_target_pairs={{0,65},{1,193},{2,97},{3,225},{4,1},{5,129},{6,33},{7,161},{8,67},... | collective-permute-start | bytes 110600 | tf_op jit(solution)/shard_map/ppermute | solution.py:32
  131.8 8.0 %collective-permute-start.38 = (bf16[144,128]{1,0:T(8,128)(2,1)S(1)}, bf16[144,128]{1,0:T(8,128)(2,1)S(1)}, u32[]{:S(2)}, u32[]{:S(2)}) collective-permute-start(bf16[144,128]{1,0:T(8,128)(2,1)S(1)} %get-tuple-element.68), channel_id=1, source_target_pairs={{0,96},{1,224},{2,64},{3,192},{4,32},{5,160},{6,0},{7,128},{8,98},... | collective-permute-start | bytes 110600 | tf_op jit(solution)/shard_map/ppermute | solution.py:32
  139.8 1.7 %shard_map.104 = (bf16[128,2048]{1,0:T(8,128)(2,1)}, bf16[128,1024]{1,0:T(8,128)(2,1)}, bf16[128,1024]{1,0:T(8,128)(2,1)}) custom-call(s32[4]{0:T(128)S(1)} %pad_add_fusion.where, bf16[128,512]{1,0:T(8,128)(2,1)S(1)} %get-tuple-element.45.refs_0_, bf16[128,512]{1,0:T(8,128)(2,1)S(1)} %collective-permute-done.7.refs_1_, ...), custom_call_target="tpu_custom_call" | custom-call | tf_op jit(solution)/shard_map/pallas_call | solution.py:374
  141.5 1.4 collective-permute-done.38.refs_6_
  142.9 8.7 %collective-permute-done.39.refs_7_ = bf16[144,128]{1,0:T(8,128)(2,1)S(1)} collective-permute-done((bf16[144,128]{1,0:T(8,128)(2,1)S(1)}, bf16[144,128]{1,0:T(8,128)(2,1)S(1)}, u32[]{:S(2)}, u32[]{:S(2)}) %collective-permute-start.39) | collective-permute-done | bytes 36896 | tf_op jit(solution)/shard_map/ppermute | solution.py:32
  (53 shorter events, 3.3 us)
Async XLA Ops:
  0.8 1.0 copy-start
  1.8 1.0 copy-start.1
  2.8 1.0 copy-start.2
  3.9 0.9 copy-start.3
  4.8 0.9 copy-start.4
  6.9 7.1 %collective-permute-start = (bf16[144,768]{1,0:T(8,128)(2,1)S(1)}, bf16[144,768]{1,0:T(8,128)(2,1)S(1)}, u32[]{:S(2)}, u32[]{:S(2)}) collective-permute-start(bf16[144,768]{1,0:T(8,128)(2,1)S(1)} %get-tuple-element.38), channel_id=1, source_target_pairs={{0,32},{1,33},{2,34},{3,35},{4,36},{5,37},{6,38},{7,39},{8,40},{9,... | collective-permute-start | bytes 663560 | tf_op jit(solution)/shard_map/ppermute | solution.py:32
  8.2 7.6 %collective-permute-start.1 = (bf16[144,768]{1,0:T(8,128)(2,1)S(1)}, bf16[144,768]{1,0:T(8,128)(2,1)S(1)}, u32[]{:S(2)}, u32[]{:S(2)}) collective-permute-start(bf16[144,768]{1,0:T(8,128)(2,1)S(1)} %get-tuple-element.39), channel_id=1, source_target_pairs={{0,64},{1,65},{2,66},{3,67},{4,68},{5,69},{6,70},{7,71},{8,72},{9,... | collective-permute-start | bytes 663560 | tf_op jit(solution)/shard_map/ppermute | solution.py:32
  9.1 13.8 %collective-permute-start.2 = (bf16[144,768]{1,0:T(8,128)(2,1)S(1)}, bf16[144,768]{1,0:T(8,128)(2,1)S(1)}, u32[]{:S(2)}, u32[]{:S(2)}) collective-permute-start(bf16[144,768]{1,0:T(8,128)(2,1)S(1)} %get-tuple-element.40), channel_id=1, source_target_pairs={{0,96},{1,97},{2,98},{3,99},{4,100},{5,101},{6,102},{7,103},{8,104... | collective-permute-start | bytes 663560 | tf_op jit(solution)/shard_map/ppermute | solution.py:32
  11.0 16.1 %collective-permute-start.3 = (bf16[144,768]{1,0:T(8,128)(2,1)S(1)}, bf16[144,768]{1,0:T(8,128)(2,1)S(1)}, u32[]{:S(2)}, u32[]{:S(2)}) collective-permute-start(bf16[144,768]{1,0:T(8,128)(2,1)S(1)} %get-tuple-element.41), channel_id=1, source_target_pairs={{0,128},{1,129},{2,130},{3,131},{4,132},{5,133},{6,134},{7,135},{8... | collective-permute-start | bytes 663560 | tf_op jit(solution)/shard_map/ppermute | solution.py:32
  12.7 15.9 %collective-permute-start.4 = (bf16[144,768]{1,0:T(8,128)(2,1)S(1)}, bf16[144,768]{1,0:T(8,128)(2,1)S(1)}, u32[]{:S(2)}, u32[]{:S(2)}) collective-permute-start(bf16[144,768]{1,0:T(8,128)(2,1)S(1)} %get-tuple-element.42), channel_id=1, source_target_pairs={{0,160},{1,161},{2,162},{3,163},{4,164},{5,165},{6,166},{7,167},{8... | collective-permute-start | bytes 663560 | tf_op jit(solution)/shard_map/ppermute | solution.py:32
  12.7 36.5 %copy-start.5 = (s32[1,8]{1,0:T(1,128)S(1)}, s32[1,8]{1,0:T(1,128)}, u32[]{:S(2)}) copy-start(s32[1,8]{1,0:T(1,128)} %lengths.1) | copy-start | bytes 100
  14.0 28.1 %collective-permute-start.16 = (bf16[128,1152]{1,0:T(8,128)(2,1)S(1)}, bf16[128,1152]{1,0:T(8,128)(2,1)S(1)}, u32[]{:S(2)}, u32[]{:S(2)}) collective-permute-start(bf16[128,1152]{1,0:T(8,128)(2,1)S(1)} %get-tuple-element.70), channel_id=1, source_target_pairs={{0,96},{1,97},{2,98},{3,99},{4,100},{5,101},{6,102},{7,103},{8,104... | collective-permute-start | bytes 884744 | tf_op jit(solution)/shard_map/ppermute | solution.py:32
  15.8 26.4 %collective-permute-start.14 = (bf16[128,1152]{1,0:T(8,128)(2,1)S(1)}, bf16[128,1152]{1,0:T(8,128)(2,1)S(1)}, u32[]{:S(2)}, u32[]{:S(2)}) collective-permute-start(bf16[128,1152]{1,0:T(8,128)(2,1)S(1)} %get-tuple-element.71), channel_id=1, source_target_pairs={{0,32},{1,33},{2,34},{3,35},{4,36},{5,37},{6,38},{7,39},{8,40},{9,... | collective-permute-start | bytes 884744 | tf_op jit(solution)/shard_map/ppermute | solution.py:32
  22.8 22.5 %collective-permute-start.15 = (bf16[128,1152]{1,0:T(8,128)(2,1)S(1)}, bf16[128,1152]{1,0:T(8,128)(2,1)S(1)}, u32[]{:S(2)}, u32[]{:S(2)}) collective-permute-start(bf16[128,1152]{1,0:T(8,128)(2,1)S(1)} %get-tuple-element.73), channel_id=1, source_target_pairs={{0,64},{1,65},{2,66},{3,67},{4,68},{5,69},{6,70},{7,71},{8,72},{9,... | collective-permute-start | bytes 884744 | tf_op jit(solution)/shard_map/ppermute | solution.py:32
  27.2 9.4 %collective-permute-start.5 = (bf16[144,768]{1,0:T(8,128)(2,1)S(1)}, bf16[144,768]{1,0:T(8,128)(2,1)S(1)}, u32[]{:S(2)}, u32[]{:S(2)}) collective-permute-start(bf16[144,768]{1,0:T(8,128)(2,1)S(1)} %get-tuple-element.43), channel_id=1, source_target_pairs={{0,192},{1,193},{2,194},{3,195},{4,196},{5,197},{6,198},{7,199},{8... | collective-permute-start | bytes 663560 | tf_op jit(solution)/shard_map/ppermute | solution.py:32
  28.6 20.6 %collective-permute-start.6 = (bf16[144,768]{1,0:T(8,128)(2,1)S(1)}, bf16[144,768]{1,0:T(8,128)(2,1)S(1)}, u32[]{:S(2)}, u32[]{:S(2)}) collective-permute-start(bf16[144,768]{1,0:T(8,128)(2,1)S(1)} %get-tuple-element.44), channel_id=1, source_target_pairs={{0,224},{1,225},{2,226},{3,227},{4,228},{5,229},{6,230},{7,231},{8... | collective-permute-start | bytes 663560 | tf_op jit(solution)/shard_map/ppermute | solution.py:32
  36.6 23.0 %collective-permute-start.17 = (bf16[128,1152]{1,0:T(8,128)(2,1)S(1)}, bf16[128,1152]{1,0:T(8,128)(2,1)S(1)}, u32[]{:S(2)}, u32[]{:S(2)}) collective-permute-start(bf16[128,1152]{1,0:T(8,128)(2,1)S(1)} %get-tuple-element.72.refs_0_), channel_id=1, source_target_pairs={{0,1},{1,0},{2,3},{3,2},{4,5},{5,4},{6,7},{7,6},{8,9},{9,8},{10,11... | collective-permute-start | bytes 884744 | tf_op jit(solution)/shard_map/ppermute | solution.py:32
  42.2 30.8 %collective-permute-start.20 = (bf16[128,1152]{1,0:T(8,128)(2,1)S(1)}, bf16[128,1152]{1,0:T(8,128)(2,1)S(1)}, u32[]{:S(2)}, u32[]{:S(2)}) collective-permute-start(bf16[128,1152]{1,0:T(8,128)(2,1)S(1)} %collective-permute-done.16.refs_3_), channel_id=1, source_target_pairs={{0,1},{1,0},{2,3},{3,2},{4,5},{5,4},{6,7},{7,6},{8,9},{9,8},{10,11... | collective-permute-start | bytes 884744 | tf_op jit(solution)/shard_map/ppermute | solution.py:32
  42.2 32.0 %collective-permute-start.18 = (bf16[128,1152]{1,0:T(8,128)(2,1)S(1)}, bf16[128,1152]{1,0:T(8,128)(2,1)S(1)}, u32[]{:S(2)}, u32[]{:S(2)}) collective-permute-start(bf16[128,1152]{1,0:T(8,128)(2,1)S(1)} %collective-permute-done.14.refs_1_), channel_id=1, source_target_pairs={{0,1},{1,0},{2,3},{3,2},{4,5},{5,4},{6,7},{7,6},{8,9},{9,8},{10,11... | collective-permute-start | bytes 884744 | tf_op jit(solution)/shard_map/ppermute | solution.py:32
  45.3 30.9 %collective-permute-start.19 = (bf16[128,1152]{1,0:T(8,128)(2,1)S(1)}, bf16[128,1152]{1,0:T(8,128)(2,1)S(1)}, u32[]{:S(2)}, u32[]{:S(2)}) collective-permute-start(bf16[128,1152]{1,0:T(8,128)(2,1)S(1)} %collective-permute-done.15.refs_2_), channel_id=1, source_target_pairs={{0,1},{1,0},{2,3},{3,2},{4,5},{5,4},{6,7},{7,6},{8,9},{9,8},{10,11... | collective-permute-start | bytes 884744 | tf_op jit(solution)/shard_map/ppermute | solution.py:32
  59.5 6.3 %collective-permute-start.24 = (bf16[512,128]{1,0:T(8,128)(2,1)S(1)}, bf16[512,128]{1,0:T(8,128)(2,1)S(1)}, u32[]{:S(2)}, u32[]{:S(2)}) collective-permute-start(bf16[512,128]{1,0:T(8,128)(2,1)S(1)} %get-tuple-element.56), channel_id=1, source_target_pairs={{0,96},{1,224},{2,98},{3,226},{4,100},{5,228},{6,102},{7,230},{8,1... | collective-permute-start | bytes 393224 | tf_op jit(solution)/shard_map/ppermute | solution.py:32
  59.6 7.8 %collective-permute-start.23 = (bf16[512,128]{1,0:T(8,128)(2,1)S(1)}, bf16[512,128]{1,0:T(8,128)(2,1)S(1)}, u32[]{:S(2)}, u32[]{:S(2)}) collective-permute-start(bf16[512,128]{1,0:T(8,128)(2,1)S(1)} %get-tuple-element.56), channel_id=1, source_target_pairs={{0,64},{1,192},{2,66},{3,194},{4,68},{5,196},{6,70},{7,198},{8,72}... | collective-permute-start | bytes 393224 | tf_op jit(solution)/shard_map/ppermute | solution.py:32
  65.8 5.3 %collective-permute-start.22 = (bf16[512,128]{1,0:T(8,128)(2,1)S(1)}, bf16[512,128]{1,0:T(8,128)(2,1)S(1)}, u32[]{:S(2)}, u32[]{:S(2)}) collective-permute-start(bf16[512,128]{1,0:T(8,128)(2,1)S(1)} %get-tuple-element.56), channel_id=1, source_target_pairs={{0,32},{1,160},{2,34},{3,162},{4,36},{5,164},{6,38},{7,166},{8,40}... | collective-permute-start | bytes 393224 | tf_op jit(solution)/shard_map/ppermute | solution.py:32
  67.4 11.1 %collective-permute-start.21 = (bf16[512,128]{1,0:T(8,128)(2,1)S(1)}, bf16[512,128]{1,0:T(8,128)(2,1)S(1)}, u32[]{:S(2)}, u32[]{:S(2)}) collective-permute-start(bf16[512,128]{1,0:T(8,128)(2,1)S(1)} %get-tuple-element.56), channel_id=1, source_target_pairs={{0,0},{1,128},{2,2},{3,130},{4,4},{5,132},{6,6},{7,134},{8,8},{9,1... | collective-permute-start | bytes 393224 | tf_op jit(solution)/shard_map/ppermute | solution.py:32
  71.1 7.4 %collective-permute-start.28 = (bf16[512,128]{1,0:T(8,128)(2,1)S(1)}, bf16[512,128]{1,0:T(8,128)(2,1)S(1)}, u32[]{:S(2)}, u32[]{:S(2)}) collective-permute-start(bf16[512,128]{1,0:T(8,128)(2,1)S(1)} %get-tuple-element.57), channel_id=1, source_target_pairs={{0,224},{1,96},{2,226},{3,98},{4,228},{5,100},{6,230},{7,102},{8,2... | collective-permute-start | bytes 393224 | tf_op jit(solution)/shard_map/ppermute | solution.py:32
  73.0 6.4 %collective-permute-start.27 = (bf16[512,128]{1,0:T(8,128)(2,1)S(1)}, bf16[512,128]{1,0:T(8,128)(2,1)S(1)}, u32[]{:S(2)}, u32[]{:S(2)}) collective-permute-start(bf16[512,128]{1,0:T(8,128)(2,1)S(1)} %get-tuple-element.57), channel_id=1, source_target_pairs={{0,192},{1,64},{2,194},{3,66},{4,196},{5,68},{6,198},{7,70},{8,200... | collective-permute-start | bytes 393224 | tf_op jit(solution)/shard_map/ppermute | solution.py:32
  74.2 8.0 %collective-permute-start.26 = (bf16[512,128]{1,0:T(8,128)(2,1)S(1)}, bf16[512,128]{1,0:T(8,128)(2,1)S(1)}, u32[]{:S(2)}, u32[]{:S(2)}) collective-permute-start(bf16[512,128]{1,0:T(8,128)(2,1)S(1)} %get-tuple-element.57), channel_id=1, source_target_pairs={{0,160},{1,32},{2,162},{3,34},{4,164},{5,36},{6,166},{7,38},{8,168... | collective-permute-start | bytes 393224 | tf_op jit(solution)/shard_map/ppermute | solution.py:32
  76.2 5.9 %collective-permute-start.25 = (bf16[512,128]{1,0:T(8,128)(2,1)S(1)}, bf16[512,128]{1,0:T(8,128)(2,1)S(1)}, u32[]{:S(2)}, u32[]{:S(2)}) collective-permute-start(bf16[512,128]{1,0:T(8,128)(2,1)S(1)} %get-tuple-element.57), channel_id=1, source_target_pairs={{0,128},{1,0},{2,130},{3,2},{4,132},{5,4},{6,134},{7,6},{8,136},{9... | collective-permute-start | bytes 393224 | tf_op jit(solution)/shard_map/ppermute | solution.py:32
  85.2 13.7 %collective-permute-start.29 = (bf16[288,512]{1,0:T(8,128)(2,1)S(1)}, bf16[288,512]{1,0:T(8,128)(2,1)S(1)}, u32[]{:S(2)}, u32[]{:S(2)}) collective-permute-start(bf16[288,512]{1,0:T(8,128)(2,1)S(1)} %get-tuple-element.59), channel_id=1, source_target_pairs={{0,8},{1,9},{2,10},{3,11},{4,12},{5,13},{6,14},{7,15},{8,16},{9,17... | collective-permute-start | bytes 884744 | tf_op jit(solution)/shard_map/ppermute | solution.py:32
  85.2 13.6 %collective-permute-start.30 = (bf16[288,512]{1,0:T(8,128)(2,1)S(1)}, bf16[288,512]{1,0:T(8,128)(2,1)S(1)}, u32[]{:S(2)}, u32[]{:S(2)}) collective-permute-start(bf16[288,512]{1,0:T(8,128)(2,1)S(1)} %get-tuple-element.60), channel_id=1, source_target_pairs={{0,16},{1,17},{2,18},{3,19},{4,20},{5,21},{6,22},{7,23},{8,24},{9,... | collective-permute-start | bytes 884744 | tf_op jit(solution)/shard_map/ppermute | solution.py:32
  87.6 14.7 %collective-permute-start.31 = (bf16[288,512]{1,0:T(8,128)(2,1)S(1)}, bf16[288,512]{1,0:T(8,128)(2,1)S(1)}, u32[]{:S(2)}, u32[]{:S(2)}) collective-permute-start(bf16[288,512]{1,0:T(8,128)(2,1)S(1)} %get-tuple-element.61), channel_id=1, source_target_pairs={{0,24},{1,25},{2,26},{3,27},{4,28},{5,29},{6,30},{7,31},{8,0},{9,1... | collective-permute-start | bytes 884744 | tf_op jit(solution)/shard_map/ppermute | solution.py:32
  87.6 4.3 %collective-permute-start.7 = (bf16[128,512]{1,0:T(8,128)(2,1)S(1)}, bf16[128,512]{1,0:T(8,128)(2,1)S(1)}, u32[]{:S(2)}, u32[]{:S(2)}) collective-permute-start(bf16[128,512]{1,0:T(8,128)(2,1)S(1)} %get-tuple-element.46), channel_id=1, source_target_pairs={{0,32},{1,33},{2,34},{3,35},{4,36},{5,37},{6,38},{7,39},{8,40},{9,... | collective-permute-start | bytes 393224 | tf_op jit(solution)/shard_map/ppermute | solution.py:32
  87.8 10.1 %collective-permute-start.8 = (bf16[128,512]{1,0:T(8,128)(2,1)S(1)}, bf16[128,512]{1,0:T(8,128)(2,1)S(1)}, u32[]{:S(2)}, u32[]{:S(2)}) collective-permute-start(bf16[128,512]{1,0:T(8,128)(2,1)S(1)} %get-tuple-element.47), channel_id=1, source_target_pairs={{0,64},{1,65},{2,66},{3,67},{4,68},{5,69},{6,70},{7,71},{8,72},{9,... | collective-permute-start | bytes 393224 | tf_op jit(solution)/shard_map/ppermute | solution.py:32
  91.9 13.8 %collective-permute-start.9 = (bf16[128,512]{1,0:T(8,128)(2,1)S(1)}, bf16[128,512]{1,0:T(8,128)(2,1)S(1)}, u32[]{:S(2)}, u32[]{:S(2)}) collective-permute-start(bf16[128,512]{1,0:T(8,128)(2,1)S(1)} %get-tuple-element.48), channel_id=1, source_target_pairs={{0,96},{1,97},{2,98},{3,99},{4,100},{5,101},{6,102},{7,103},{8,104... | collective-permute-start | bytes 393224 | tf_op jit(solution)/shard_map/ppermute | solution.py:32
  97.9 18.8 %collective-permute-start.10 = (bf16[128,512]{1,0:T(8,128)(2,1)S(1)}, bf16[128,512]{1,0:T(8,128)(2,1)S(1)}, u32[]{:S(2)}, u32[]{:S(2)}) collective-permute-start(bf16[128,512]{1,0:T(8,128)(2,1)S(1)} %get-tuple-element.49), channel_id=1, source_target_pairs={{0,128},{1,129},{2,130},{3,131},{4,132},{5,133},{6,134},{7,135},{8... | collective-permute-start | bytes 393224 | tf_op jit(solution)/shard_map/ppermute | solution.py:32
  98.8 18.0 %collective-permute-start.11 = (bf16[128,512]{1,0:T(8,128)(2,1)S(1)}, bf16[128,512]{1,0:T(8,128)(2,1)S(1)}, u32[]{:S(2)}, u32[]{:S(2)}) collective-permute-start(bf16[128,512]{1,0:T(8,128)(2,1)S(1)} %get-tuple-element.50), channel_id=1, source_target_pairs={{0,160},{1,161},{2,162},{3,163},{4,164},{5,165},{6,166},{7,167},{8... | collective-permute-start | bytes 393224 | tf_op jit(solution)/shard_map/ppermute | solution.py:32
  98.9 20.4 %collective-permute-start.12 = (bf16[128,512]{1,0:T(8,128)(2,1)S(1)}, bf16[128,512]{1,0:T(8,128)(2,1)S(1)}, u32[]{:S(2)}, u32[]{:S(2)}) collective-permute-start(bf16[128,512]{1,0:T(8,128)(2,1)S(1)} %get-tuple-element.51), channel_id=1, source_target_pairs={{0,192},{1,193},{2,194},{3,195},{4,196},{5,197},{6,198},{7,199},{8... | collective-permute-start | bytes 393224 | tf_op jit(solution)/shard_map/ppermute | solution.py:32
  102.3 17.0 %collective-permute-start.13 = (bf16[128,512]{1,0:T(8,128)(2,1)S(1)}, bf16[128,512]{1,0:T(8,128)(2,1)S(1)}, u32[]{:S(2)}, u32[]{:S(2)}) collective-permute-start(bf16[128,512]{1,0:T(8,128)(2,1)S(1)} %get-tuple-element.52), channel_id=1, source_target_pairs={{0,224},{1,225},{2,226},{3,227},{4,228},{5,229},{6,230},{7,231},{8... | collective-permute-start | bytes 393224 | tf_op jit(solution)/shard_map/ppermute | solution.py:32
  105.7 20.2 %collective-permute-start.32 = (bf16[144,128]{1,0:T(8,128)(2,1)S(1)}, bf16[144,128]{1,0:T(8,128)(2,1)S(1)}, u32[]{:S(2)}, u32[]{:S(2)}) collective-permute-start(bf16[144,128]{1,0:T(8,128)(2,1)S(1)} %get-tuple-element.62), channel_id=1, source_target_pairs={{0,0},{1,128},{2,32},{3,160},{4,64},{5,192},{6,96},{7,224},{8,2},{... | collective-permute-start | bytes 110600 | tf_op jit(solution)/shard_map/ppermute | solution.py:32
  116.7 15.1 %collective-permute-start.33 = (bf16[144,128]{1,0:T(8,128)(2,1)S(1)}, bf16[144,128]{1,0:T(8,128)(2,1)S(1)}, u32[]{:S(2)}, u32[]{:S(2)}) collective-permute-start(bf16[144,128]{1,0:T(8,128)(2,1)S(1)} %get-tuple-element.63), channel_id=1, source_target_pairs={{0,1},{1,129},{2,33},{3,161},{4,65},{5,193},{6,97},{7,225},{8,3},{... | collective-permute-start | bytes 110600 | tf_op jit(solution)/shard_map/ppermute | solution.py:32
  116.9 23.0 %collective-permute-start.34 = (bf16[144,128]{1,0:T(8,128)(2,1)S(1)}, bf16[144,128]{1,0:T(8,128)(2,1)S(1)}, u32[]{:S(2)}, u32[]{:S(2)}) collective-permute-start(bf16[144,128]{1,0:T(8,128)(2,1)S(1)} %get-tuple-element.64), channel_id=1, source_target_pairs={{0,32},{1,160},{2,0},{3,128},{4,96},{5,224},{6,64},{7,192},{8,34},... | collective-permute-start | bytes 110600 | tf_op jit(solution)/shard_map/ppermute | solution.py:32
  119.2 22.3 %collective-permute-start.35 = (bf16[144,128]{1,0:T(8,128)(2,1)S(1)}, bf16[144,128]{1,0:T(8,128)(2,1)S(1)}, u32[]{:S(2)}, u32[]{:S(2)}) collective-permute-start(bf16[144,128]{1,0:T(8,128)(2,1)S(1)} %get-tuple-element.65), channel_id=1, source_target_pairs={{0,33},{1,161},{2,1},{3,129},{4,97},{5,225},{6,65},{7,193},{8,35},... | collective-permute-start | bytes 110600 | tf_op jit(solution)/shard_map/ppermute | solution.py:32
  119.3 22.2 %collective-permute-start.36 = (bf16[144,128]{1,0:T(8,128)(2,1)S(1)}, bf16[144,128]{1,0:T(8,128)(2,1)S(1)}, u32[]{:S(2)}, u32[]{:S(2)}) collective-permute-start(bf16[144,128]{1,0:T(8,128)(2,1)S(1)} %get-tuple-element.66), channel_id=1, source_target_pairs={{0,64},{1,192},{2,96},{3,224},{4,0},{5,128},{6,32},{7,160},{8,66},... | collective-permute-start | bytes 110600 | tf_op jit(solution)/shard_map/ppermute | solution.py:32
  125.9 15.7 %collective-permute-start.37 = (bf16[144,128]{1,0:T(8,128)(2,1)S(1)}, bf16[144,128]{1,0:T(8,128)(2,1)S(1)}, u32[]{:S(2)}, u32[]{:S(2)}) collective-permute-start(bf16[144,128]{1,0:T(8,128)(2,1)S(1)} %get-tuple-element.67), channel_id=1, source_target_pairs={{0,65},{1,193},{2,97},{3,225},{4,1},{5,129},{6,33},{7,161},{8,67},... | collective-permute-start | bytes 110600 | tf_op jit(solution)/shard_map/ppermute | solution.py:32
  131.8 11.1 %collective-permute-start.38 = (bf16[144,128]{1,0:T(8,128)(2,1)S(1)}, bf16[144,128]{1,0:T(8,128)(2,1)S(1)}, u32[]{:S(2)}, u32[]{:S(2)}) collective-permute-start(bf16[144,128]{1,0:T(8,128)(2,1)S(1)} %get-tuple-element.68), channel_id=1, source_target_pairs={{0,96},{1,224},{2,64},{3,192},{4,32},{5,160},{6,0},{7,128},{8,98},... | collective-permute-start | bytes 110600 | tf_op jit(solution)/shard_map/ppermute | solution.py:32
  139.8 11.8 %collective-permute-start.39 = (bf16[144,128]{1,0:T(8,128)(2,1)S(1)}, bf16[144,128]{1,0:T(8,128)(2,1)S(1)}, u32[]{:S(2)}, u32[]{:S(2)}) collective-permute-start(bf16[144,128]{1,0:T(8,128)(2,1)S(1)} %get-tuple-element.69), channel_id=1, source_target_pairs={{0,97},{1,225},{2,65},{3,193},{4,33},{5,161},{6,1},{7,129},{8,99},... | collective-permute-start | bytes 110600 | tf_op jit(solution)/shard_map/ppermute | solution.py:32

commit v2 on v1

v2 whole, which is shorter than its diff:
```python
import math

import jax
import jax.numpy as jnp
from jax import lax
from jax.experimental import pallas as pl
from jax.experimental.pallas import tpu as pltpu
from jax.sharding import PartitionSpec as P

ROWS = 128
HEAD = 128
BLOCKS = 8
TAIL = 16
PACKED = 768
BACK = 384
CAP = 50.0
SCALE = 144.0 ** (-0.5)
BF = jnp.bfloat16
F32 = jnp.float32
MIB = 1024 * 1024


def spread(block, place):
    route = []
    for ctx in range(8):
        for dp in range(32):
            here = (dp // 8, ctx % 4, (dp // 2) % 4 * 2 + ctx // 4, dp % 2)
            x, y, z, core = place(*here)
            x, y, z = x % 4, y % 4, z % 8
            route.append((ctx * 32 + dp, ((z % 2) * 4 + y) * 32 + x * 8 + z // 2 * 2 + core))
    return lax.ppermute(block, ("ctx", "dp"), route)


def over_ctx(block, k):
    return spread(block, lambda x, y, z, c: (x, y ^ k % 4, z ^ k // 4, c)) if k else block


def over_x(block, k):
    return spread(block, lambda x, y, z, c: (x ^ k, y, z, c)) if k else block


def over_y(block, k):
    return over_ctx(block, k)


def over_z(block, k):
    return spread(block, lambda x, y, z, c: (x, y, z ^ 2 * k, c)) if k else block


def over_core(block):
    return spread(block, lambda x, y, z, c: (x, y, z, 1 - c))


def after(value, *others):
    return lax.optimization_barrier((value, *others))[0]


def nt(left, right):
    return lax.dot_general(left, right, (((1,), (1,)), ((), ())), preferred_element_type=F32)


def nn(left, right):
    return lax.dot_general(left, right, (((1,), (0,)), ((), ())), preferred_element_type=F32)


def split_three(value):
    first = value.astype(BF)
    rest = value - first.astype(F32)
    second = rest.astype(BF)
    third = (rest - second.astype(F32)).astype(BF)
    return first, second, third


def pack_kernel(*refs):
    out = refs[5]
    q, k, v, do, o = refs[6:11]
    sems = refs[11]
    copies = []
    for n, (source, held) in enumerate(zip(refs[:5], refs[6:11])):
        copy = pltpu.make_async_copy(source, held, sems.at[n])
        copy.start()
        copies.append(copy)
    for copy in copies:
        copy.wait()
    product = do[...].astype(F32) * o[...].astype(F32)
    high = product.astype(BF)
    low = (product - high.astype(F32)).astype(BF)
    row = lax.broadcasted_iota(jnp.int32, (TAIL, 2048), 0)
    col = lax.broadcasted_iota(jnp.int32, (TAIL, 2048), 1)
    pick = (row == col // HEAD).astype(BF)
    delta = nt(pick, high) + nt(pick, low)
    first, second, third = split_three(delta)
    for n in range(BLOCKS):
        out[n, 0:ROWS, 0:256] = q[:, n * 256 : (n + 1) * 256]
        out[n, 0:ROWS, 256:512] = do[:, n * 256 : (n + 1) * 256]
        out[n, 0:ROWS, 512:640] = k[:, n * 128 : (n + 1) * 128]
        out[n, 0:ROWS, 640:768] = v[:, n * 128 : (n + 1) * 128]
        out[n, ROWS:, 0:128] = first
        out[n, ROWS:, 128:256] = second
        out[n, ROWS:, 256:384] = third
        out[n, ROWS:, 384:768] = jnp.zeros((TAIL, 384), BF)


def attention_kernel(where, lengths, *refs):
    packed, back = refs[:2]
    values = refs[2:6]
    held, key_turned, dk, dv, sem = refs[6:]
    mine = where[0]
    copy = pltpu.make_async_copy(packed, held, sem)
    copy.start()
    dk[...] = jnp.zeros_like(dk)
    dv[...] = jnp.zeros_like(dv)
    ends = []
    total = 0
    for d in range(8):
        total = total + lengths[0, d]
        ends.append(total)
    copy.wait()
    for n in range(BLOCKS):
        key_turned[n] = held[n, 0:ROWS, 512:640].T

    def block(b, carry):
        base = b * ROWS
        first = 0
        for end in ends:
            first = jnp.where(base >= end, end, first)
        kb0 = first // ROWS
        count = b - kb0 + 1
        lane = lax.broadcasted_iota(jnp.int32, (1, 256), 1)
        query = base + lane % ROWS
        begin = jnp.zeros((1, 256), jnp.int32)
        for end in ends:
            begin = jnp.where(query >= end, end, begin)
        tail = held[b, ROWS:, 0:384].astype(F32)
        tail = tail[:, 0:128] + tail[:, 128:256] + tail[:, 256:384]
        head = lax.broadcasted_iota(jnp.int32, (TAIL, 128), 0)
        delta = jnp.concatenate(
            [
                jnp.sum(jnp.where(head == 2 * mine + s, tail, 0.0), axis=0, keepdims=True)
                for s in range(2)
            ],
            axis=1,
        )
        queries = jnp.concatenate([held[b, 0:ROWS, 0:128], held[b, 0:ROWS, 128:256]], axis=0)
        grads = jnp.concatenate([held[b, 0:ROWS, 256:384], held[b, 0:ROWS, 384:512]], axis=0)
        sub = lax.broadcasted_iota(jnp.int32, (ROWS, 256), 0)

        def window(number):
            powers, tanhs = [], []
            sums = jnp.zeros((1, 256), F32)
            for n in range(number):
                kb = kb0 + n
                raw = nt(held[kb, 0:ROWS, 512:640], queries)
                tanh = jnp.tanh(raw * (SCALE / CAP))
                key = sub + kb * ROWS
                live = key >= begin
                if n == number - 1:
                    live = live & (key <= query)
                power = jnp.where(live, jnp.exp(CAP * tanh), 0.0)
                sums = sums + jnp.sum(power, axis=0, keepdims=True)
                powers.append(power)
                tanhs.append(tanh)
            inverse = 1.0 / sums
            turned = jnp.zeros((HEAD, 256), F32)
            for n in range(number):
                kb = kb0 + n
                prob = powers[n] * inverse
                dprob = nt(held[kb, 0:ROWS, 640:768], grads)
                slope = SCALE - (SCALE * tanhs[n]) * tanhs[n]
                dscore = (prob * (dprob - delta) * slope).astype(BF)
                dv[kb] += nn(prob.astype(BF), grads)
                dk[kb] += nn(dscore, queries)
                turned = turned + nn(key_turned[kb], dscore)
            straight = turned.T
            back[b, :, 0:128] = straight[0:ROWS].astype(BF)
            back[b, :, 128:256] = straight[ROWS:].astype(BF)

        for number in range(1, 6):

            @pl.when(count == number)
            def _():
                window(number)

        return carry

    lax.fori_loop(0, BLOCKS, block, 0)
    for n in range(BLOCKS):
        back[n, :, 256:384] = dk[n].astype(BF)
    for k in range(4):
        for half in range(2):
            values[k][half] = dv[half * 4 + (mine % 4 ^ k)].astype(BF)


def turn_kernel(where, *refs):
    pieces, low, high, far = refs[:4], refs[4], refs[5], refs[6]
    held, turned, sems = refs[7:]
    core = where[1]
    copies = []
    for n in range(4):
        copy = pltpu.make_async_copy(pieces[n], held.at[n], sems.at[n])
        copy.start()
        copies.append(copy)
    for copy in copies:
        copy.wait()

    for n in range(4):
        turned[...] = held[n].T
        lanes = slice(n * ROWS, (n + 1) * ROWS)
        for z in range(4):
            rows = pl.ds(z * 144, 144)
            near = (low, high)[z // 2]
            near[pl.ds(z % 2 * 144, 144), lanes] = turned[pl.ds(pl.multiple_of((z * 2 + core) * 144, 16), 144)]
            far[rows, lanes] = turned[pl.ds(pl.multiple_of((z * 2 + 1 - core) * 144, 16), 144)]


def join_kernel(where, *refs):
    pieces, joined, near, far = refs[:4], refs[4], refs[5], refs[6]
    mine = where[0]
    half = mine // 4
    for k, piece in enumerate(pieces):
        columns = pl.ds(pl.multiple_of((mine % 4 ^ k) * HEAD, HEAD), HEAD)
        joined[0, :, columns] = piece[0]
        joined[1, :, columns] = piece[1]
    near[...] = joined[half]
    far[...] = joined[1 - half]


def weight_kernel(where, *refs):
    lefts, rights, outs = refs[:6], refs[6:14], refs[14:18]
    left, right, total, sems = refs[18:]
    mine = where[0]
    half = mine // 4
    copies = [[], [], [], []]

    def fetch(n, source, target):
        copy = pltpu.make_async_copy(source, target, sems.at[n, len(copies[n])])
        copy.start()
        copies[n].append(copy)

    for n in range(4):
        if n % 2:
            fetch(n, lefts[2 + n // 2 * 3], left.at[n])
        else:
            fetch(n, lefts[n // 2 * 3], left.at[n, pl.ds(0, 288)])
            fetch(n, lefts[n // 2 * 3 + 1], left.at[n, pl.ds(288, 288)])
        for k in range(4):
            fetch(
                n,
                rights[n % 2 * 4 + k].at[half if n < 2 else 1 - half],
                right.at[n, pl.ds(k * ROWS, ROWS)],
            )
    value = jnp.zeros((576, 512), F32)
    for n in range(4):
        for copy in copies[n]:
            copy.wait()
        value = value + nn(left[n], right[n])
    total[...] = (value * (1.0 / math.sqrt(32768.0))).astype(BF)
    for k, out in enumerate(outs):
        out[...] = total[:, pl.ds(pl.multiple_of((mine % 4 ^ k) * HEAD, HEAD), HEAD)]


def sum_kernel(where, *refs):
    total = refs[8]
    z_hi = where[2]
    value = refs[0][...].astype(F32)
    for ref in refs[1:4]:
        value = value + ref[...].astype(F32)
    total[...] = value.astype(BF)
    for k, out in enumerate(refs[4:8]):
        out[...] = total[pl.ds(pl.multiple_of((z_hi ^ k) * 144, 16), 144)]


def last_kernel(*refs):
    total = refs[0][...].astype(F32)
    for ref in refs[1:4]:
        total = total + ref[...].astype(F32)
    refs[4][...] = total


def unpack_kernel(where, returned, near, far, query_grad, key_grad, value_grad):
    half = where[0] // 4
    for n in range(BLOCKS):
        query_grad[:, n * 256 : (n + 1) * 256] = returned[n, :, 0:256]
        key_grad[:, n * 128 : (n + 1) * 128] = returned[n, :, 256:384]
    value_grad[:, pl.ds(pl.multiple_of(half * 512, 512), 512)] = near[...]
    value_grad[:, pl.ds(pl.multiple_of((1 - half) * 512, 512), 512)] = far[...]


SMEM = pl.BlockSpec(memory_space=pltpu.SMEM)
VMEM = pl.BlockSpec(memory_space=pltpu.VMEM)
ANY = pl.BlockSpec(memory_space=pl.ANY)


def shape(*dims, dtype=BF):
    return jax.ShapeDtypeStruct(dims, dtype)


def call(kernel, outs, ins, scratch=(), flops=0, moved=0, limit=16):
    return pl.pallas_call(
        kernel,
        out_shape=outs,
        in_specs=ins,
        out_specs=jax.tree.map(lambda _: VMEM, outs),
        scratch_shapes=list(scratch),
        compiler_params=pltpu.CompilerParams(vmem_limit_bytes=limit * MIB),
        cost_estimate=pl.CostEstimate(flops=flops, bytes_accessed=moved, transcendentals=0),
    )


def body(
    queries, key_states, value_states, saved_output, output_grad, layer_input, document_lengths
):
    mine = lax.axis_index("ctx")
    dp = lax.axis_index("dp")
    x = dp // 8
    where = jnp.stack([mine, dp % 2, dp // 2 % 4]).astype(jnp.int32)

    packed = call(
        pack_kernel,
        shape(BLOCKS, ROWS + TAIL, PACKED),
        [ANY] * 5,
        [
            pltpu.VMEM((ROWS, 2048), BF),
            pltpu.VMEM((ROWS, 1024), BF),
            pltpu.VMEM((ROWS, 1024), BF),
            pltpu.VMEM((ROWS, 2048), BF),
            pltpu.VMEM((ROWS, 2048), BF),
            pltpu.SemaphoreType.DMA((5,)),
        ],
        limit=60,
    )(queries[0], key_states[0], value_states[0], output_grad[0], saved_output[0])
    arrived = lax.all_to_all(packed, "ctx", 0, 0, tiled=True)

    inputs = layer_input[0]
    own = []
    for k in range(4):
        piece = lax.dynamic_slice(inputs, (0, (x ^ k) * 1152), (ROWS, 1152))
        own.append(over_x(after(piece, packed), k))
    near_low, near_high, far_rows = call(
        turn_kernel,
        [shape(288, 512)] * 2 + [shape(576, 512)],
        [SMEM] + [ANY] * 4,
        [
            pltpu.VMEM((4, ROWS, 1152), BF),
            pltpu.VMEM((1152, ROWS), BF),
            pltpu.SemaphoreType.DMA((4,)),
        ],
    )(where, *own)
    far_rows = over_core(far_rows)
    across_low = over_ctx(near_low, 4)

    back, *values = call(
        attention_kernel,
        [shape(BLOCKS, ROWS, BACK)] + [shape(2, ROWS, HEAD)] * 4,
        [SMEM, SMEM, ANY],
        [
            pltpu.VMEM((BLOCKS, ROWS + TAIL, PACKED), BF),
            pltpu.VMEM((BLOCKS, HEAD, ROWS), BF),
            pltpu.VMEM((BLOCKS, ROWS, HEAD), F32),
            pltpu.VMEM((BLOCKS, ROWS, HEAD), F32),
            pltpu.SemaphoreType.DMA,
        ],
        flops=4_000_000_000,
        moved=4_000_000,
    )(where, document_lengths, arrived)

    values = [after(value, across_low) for value in values]
    across_high = over_ctx(near_high, 4)
    across_far = over_ctx(far_rows, 4)
    pieces = [after(over_y(values[k], k), across_high) for k in range(4)]
    joined, near, far = call(
        join_kernel,
        [shape(2, ROWS, 512), shape(ROWS, 512), shape(ROWS, 512)],
        [SMEM] + [VMEM] * 4,
    )(where, *pieces)
    rights = [over_x(joined, k) for k in range(4)]
    rights = rights + [over_core(right) for right in rights]
    returned = lax.all_to_all(after(back, joined), "ctx", 0, 0, tiled=True)

    parts = call(
        weight_kernel,
        [shape(576, HEAD)] * 4,
        [SMEM] + [ANY] * 14,
        [
            pltpu.VMEM((4, 576, 512), BF),
            pltpu.VMEM((4, 512, 512), BF),
            pltpu.VMEM((576, 512), BF),
            pltpu.SemaphoreType.DMA((4, 6)),
        ],
        flops=1_300_000_000,
        moved=4_000_000,
    )(where, near_low, near_high, far_rows, across_low, across_high, across_far, *rights)
    far = over_ctx(far, 4)
    reduced = [over_y(parts[k], k) for k in range(4)]
    blocks = call(
        sum_kernel, [shape(144, HEAD)] * 4, [SMEM] + [VMEM] * 4, [pltpu.VMEM((576, HEAD), BF)]
    )(where, *reduced)
    landed = [over_z(blocks[k], k) for k in range(4)]
    weight_grad = call(last_kernel, shape(144, HEAD, dtype=F32), [VMEM] * 4)(*landed)
    query_grad, key_grad, value_grad = call(
        unpack_kernel,
        [shape(ROWS, 2048), shape(ROWS, 1024), shape(ROWS, 1024)],
        [SMEM] + [VMEM] * 3,
    )(where, returned, near, far)
    return query_grad[None], key_grad[None], value_grad[None], weight_grad


def solution(mesh):
    return jax.shard_map(
        body,
        mesh=mesh,
        in_specs=(P("dp", "ctx", None),) * 6 + (P("dp", None),),
        out_specs=(P("dp", "ctx", None),) * 3 + (P("dp", "ctx"),),
        check_vma=False,
    )
```

time: 153 us -> 114 us (0.75)
  the two profiles are of different devices: /device:TPU:15 before, /device:TPU:32 now
where the time goes in v2:
time: 114 us
  waiting for transfers between devices  47.3 us (41%)
  starting transfers between devices  42.3 us (37%)
  Pallas kernels  22.8 us (20%)
    ppermute x24, waiting for transfers between devices, spread(): return lax.ppermute(block, ('ctx', 'dp'), route)  47.3 us
    ppermute x24, starting transfers between devices, spread(): return lax.ppermute(block, ('ctx', 'dp'), route)  31.9 us
    pallas_call x1, Pallas kernels, body(): call(attention_kernel, [shape(BLOCKS, ROWS, BACK)] + [shape(2, ROWS, HEAD...  8.33 us
    all_to_all x1, starting transfers between devices, body(): arrived = lax.all_to_all(packed, 'ctx', 0, 0, tiled=True)  6.07 us
    pallas_call x1, Pallas kernels, body(): call(weight_kernel, [shape(576, HEAD)] * 4, [SMEM] + [ANY] * 14, [pltpu.V...  5.53 us
    all_to_all x1, starting transfers between devices, body(): returned = lax.all_to_all(after(back, joined), 'ctx', 0, 0, tiled=True)  4.33 us
    pallas_call x1, Pallas kernels, body(): call(pack_kernel, shape(BLOCKS, ROWS + TAIL, PACKED), [ANY] * 5, [pltpu.V...  3.22 us
  transfers between devices with their start and end apart: 26, of which 12 were waited for; matrix products, arithmetic and copies ran while one was open for 1% of the time, Pallas kernels for 16%

profile of v2, /device:TPU:32, one launch (start us, length us, event | category | flops | bytes accessed | tf_op | source)
XLA Modules:
  0.0 114.1 jit_solution(9153204394162804211)
XLA Ops:
  0.6 3.2 %shard_map.102 = bf16[8,144,768]{2,1,0:T(8,128)(2,1)} custom-call(bf16[128,2048]{1,0:T(8,128)(2,1)} %bitcast.19, bf16[128,1024]{1,0:T(8,128)(2,1)} %bitcast.22, bf16[128,1024]{1,0:T(8,128)(2,1)} %bitcast.23, bf16[128,2048]{1,0:T(8,128)(2,1)} %bitcast.20, bf16[128,2048]{1,0:T(8,128)(2,1)} %bitcast.21), custom_call_target="tpu_custom_call" | custom-call | tf_op jit(solution)/shard_map/pallas_call | solution.py:318
  3.9 0.0 copy-start.3
  3.9 6.1 %all-to-all-start = ((bf16[8,144,768]{2,1,0:T(8,128)(2,1)}), bf16[8,144,768]{2,1,0:T(8,128)(2,1)S(1)}, u32[]{:S(2)}, u32[]{:S(2)}) async-start(bf16[8,144,768]{2,1,0:T(8,128)(2,1)} %shard_map.102), calls=%async_computation | async-start | bytes 3538944 | tf_op jit(solution)/shard_map/all_to_all | solution.py:332
  9.9 0.9 dynamic-slice_bitcast_fusion
  10.9 1.5 %collective-permute-start = (bf16[128,1152]{1,0:T(8,128)(2,1)}, bf16[128,1152]{1,0:T(8,128)(2,1)S(1)}, u32[]{:S(2)}, u32[]{:S(2)}) collective-permute-start(bf16[128,1152]{1,0:T(8,128)(2,1)} %get-tuple-element.42), channel_id=1, source_target_pairs={{0,8},{1,9},{2,10},{3,11},{4,12},{5,13},{6,14},{7,15},{8,0},{9,1},... | collective-permute-start | bytes 884744 | tf_op jit(solution)/shard_map/ppermute | solution.py:31
  12.3 2.7 %collective-permute-start.1 = (bf16[128,1152]{1,0:T(8,128)(2,1)}, bf16[128,1152]{1,0:T(8,128)(2,1)S(1)}, u32[]{:S(2)}, u32[]{:S(2)}) collective-permute-start(bf16[128,1152]{1,0:T(8,128)(2,1)} %get-tuple-element.43), channel_id=1, source_target_pairs={{0,16},{1,17},{2,18},{3,19},{4,20},{5,21},{6,22},{7,23},{8,24},{9,... | collective-permute-start | bytes 884744 | tf_op jit(solution)/shard_map/ppermute | solution.py:31
  15.1 0.5 collective-permute-start.2
  15.6 0.1 pad_add_fusion.where
  15.6 5.4 %collective-permute-done.refs_1_ = bf16[128,1152]{1,0:T(8,128)(2,1)S(1)} collective-permute-done((bf16[128,1152]{1,0:T(8,128)(2,1)}, bf16[128,1152]{1,0:T(8,128)(2,1)S(1)}, u32[]{:S(2)}, u32[]{:S(2)}) %collective-permute-start) | collective-permute-done | bytes 294944 | tf_op jit(solution)/shard_map/ppermute | solution.py:31
  21.0 6.9 %collective-permute-done.1.refs_2_ = bf16[128,1152]{1,0:T(8,128)(2,1)S(1)} collective-permute-done((bf16[128,1152]{1,0:T(8,128)(2,1)}, bf16[128,1152]{1,0:T(8,128)(2,1)S(1)}, u32[]{:S(2)}, u32[]{:S(2)}) %collective-permute-start.1) | collective-permute-done | bytes 294944 | tf_op jit(solution)/shard_map/ppermute | solution.py:31
  27.9 2.4 %collective-permute-done.2.refs_3_ = bf16[128,1152]{1,0:T(8,128)(2,1)S(1)} collective-permute-done((bf16[128,1152]{1,0:T(8,128)(2,1)S(1)}, bf16[128,1152]{1,0:T(8,128)(2,1)S(1)}, u32[]{:S(2)}, u32[]{:S(2)}) %collective-permute-start.2) | collective-permute-done | bytes 294944 | tf_op jit(solution)/shard_map/ppermute | solution.py:31
  30.2 2.1 %shard_map.104 = (bf16[288,512]{1,0:T(8,128)(2,1)}, bf16[288,512]{1,0:T(8,128)(2,1)}, bf16[576,512]{1,0:T(8,128)(2,1)S(1)}) custom-call(s32[3]{0:T(128)S(1)} %pad_add_fusion.where, bf16[128,1152]{1,0:T(8,128)(2,1)S(1)} %get-tuple-element.41.refs_0_, bf16[128,1152]{1,0:T(8,128)(2,1)S(1)} %collective-permute-done.refs_1_, ...), custom_call_target="tpu_custom_call" | custom-call | tf_op jit(solution)/shard_map/pallas_call | solution.py:339
  32.4 0.4 collective-permute-start.3
  32.8 1.7 %collective-permute-start.4 = (bf16[288,512]{1,0:T(8,128)(2,1)}, bf16[288,512]{1,0:T(8,128)(2,1)S(1)}, u32[]{:S(2)}, u32[]{:S(2)}) collective-permute-start(bf16[288,512]{1,0:T(8,128)(2,1)} %get-tuple-element.47.refs_1_), channel_id=1, source_target_pairs={{0,128},{1,129},{2,130},{3,131},{4,132},{5,133},{6,134},{7,135},{8... | collective-permute-start | bytes 884744 | tf_op jit(solution)/shard_map/ppermute | solution.py:31
  34.5 0.0 collective-permute-start.9
  34.5 0.0 all-to-all-done.refs_0_
  34.5 8.3 %shard_map.103 = (bf16[8,128,384]{2,1,0:T(8,128)(2,1)}, bf16[2,128,128]{2,1,0:T(8,128)(2,1)S(1)}, bf16[2,128,128]{2,1,0:T(8,128)(2,1)S(1)}, bf16[2,128,128]{2,1,0:T(8,128)(2,1)S(1)}, bf16[2,128,128]{2,1,0:T(8,128)(2,1)S(1)}) custom-call(s32[3]{0:T(128)S(1)} %pad_add_fusion.where, s32[1,8]{1,0:T(1,128)S(1)} %copy-done.2, ...), custom_call_target="tpu_custom_call" | custom-call | flops 4000000000 | bytes 4000000 | tf_op jit(solution)/shard_map/pallas_call | solution.py:352
  42.8 2.7 %collective-permute-start.7 = (bf16[2,128,128]{2,1,0:T(8,128)(2,1)S(1)}, bf16[2,128,128]{2,1,0:T(8,128)(2,1)S(1)}, u32[]{:S(2)}, u32[]{:S(2)}) collective-permute-start(bf16[2,128,128]{2,1,0:T(8,128)(2,1)S(1)} %get-tuple-element.56), channel_id=1, source_target_pairs={{0,96},{1,97},{2,98},{3,99},{4,100},{5,101},{6,102},{7,103},{8,104... | collective-permute-start | bytes 196616 | tf_op jit(solution)/shard_map/ppermute | solution.py:31
  45.6 0.9 collective-permute-start.6
  46.5 0.6 collective-permute-start.5
  47.0 2.0 %collective-permute-done.7.refs_3_ = bf16[2,128,128]{2,1,0:T(8,128)(2,1)S(1)} collective-permute-done((bf16[2,128,128]{2,1,0:T(8,128)(2,1)S(1)}, bf16[2,128,128]{2,1,0:T(8,128)(2,1)S(1)}, u32[]{:S(2)}, u32[]{:S(2)}) %collective-permute-start.7) | collective-permute-done | bytes 65568 | tf_op jit(solution)/shard_map/ppermute | solution.py:31
  49.1 3.0 %collective-permute-done.6.refs_2_ = bf16[2,128,128]{2,1,0:T(8,128)(2,1)S(1)} collective-permute-done((bf16[2,128,128]{2,1,0:T(8,128)(2,1)S(1)}, bf16[2,128,128]{2,1,0:T(8,128)(2,1)S(1)}, u32[]{:S(2)}, u32[]{:S(2)}) %collective-permute-start.6) | collective-permute-done | bytes 65568 | tf_op jit(solution)/shard_map/ppermute | solution.py:31
  52.0 0.6 shard_map.105
  52.6 0.0 copy-start
  52.7 4.3 %all-to-all-start.1 = ((bf16[8,128,384]{2,1,0:T(8,128)(2,1)}), bf16[8,128,384]{2,1,0:T(8,128)(2,1)S(1)}, u32[]{:S(2)}, u32[]{:S(2)}) async-start(bf16[8,128,384]{2,1,0:T(8,128)(2,1)} %get-tuple-element.59), calls=%async_computation.1 | async-start | bytes 1572864 | tf_op jit(solution)/shard_map/all_to_all | solution.py:378
  57.0 0.1 collective-permute-start.10
  57.1 1.1 collective-permute-start.13
  58.2 0.5 collective-permute-start.12
  58.7 2.4 %collective-permute-start.11 = (bf16[2,128,512]{2,1,0:T(8,128)(2,1)S(1)}, bf16[2,128,512]{2,1,0:T(8,128)(2,1)S(1)}, u32[]{:S(2)}, u32[]{:S(2)}) collective-permute-start(bf16[2,128,512]{2,1,0:T(8,128)(2,1)S(1)} %get-tuple-element.58.refs_6_), channel_id=1, source_target_pairs={{0,8},{1,9},{2,10},{3,11},{4,12},{5,13},{6,14},{7,15},{8,0},{9,1},... | collective-permute-start | bytes 786440 | tf_op jit(solution)/shard_map/ppermute | solution.py:31
  61.2 10.0 %collective-permute-done.13.refs_9_ = bf16[2,128,512]{2,1,0:T(8,128)(2,1)S(1)} collective-permute-done((bf16[2,128,512]{2,1,0:T(8,128)(2,1)S(1)}, bf16[2,128,512]{2,1,0:T(8,128)(2,1)S(1)}, u32[]{:S(2)}, u32[]{:S(2)}) %collective-permute-start.13) | collective-permute-done | bytes 262176 | tf_op jit(solution)/shard_map/ppermute | solution.py:31
  71.2 0.5 collective-permute-start.16
  71.7 0.1 collective-permute-done.11.refs_7_
  71.8 6.6 %collective-permute-done.10.refs_5_ = bf16[576,512]{1,0:T(8,128)(2,1)S(1)} collective-permute-done((bf16[576,512]{1,0:T(8,128)(2,1)S(1)}, bf16[576,512]{1,0:T(8,128)(2,1)S(1)}, u32[]{:S(2)}, u32[]{:S(2)}) %collective-permute-start.10) | collective-permute-done | bytes 589856 | tf_op jit(solution)/shard_map/ppermute | solution.py:31
  78.4 5.5 %shard_map.107 = (bf16[576,128]{1,0:T(8,128)(2,1)S(1)}, bf16[576,128]{1,0:T(8,128)(2,1)S(1)}, bf16[576,128]{1,0:T(8,128)(2,1)S(1)}, bf16[576,128]{1,0:T(8,128)(2,1)S(1)}) custom-call(s32[3]{0:T(128)S(1)} %pad_add_fusion.where, bf16[288,512]{1,0:T(8,128)(2,1)} %get-tuple-element.45.refs_0_, bf16[288,512]{1,0:T(8,128)(2,1)} %get-tuple-element.47.refs_1_, ...), custom_call_target="tpu_custom_call" | custom-call | flops 1300000000 | bytes 4000000 | tf_op jit(solution)/shard_map/pallas_call | solution.py:380
  84.0 1.9 %collective-permute-start.18 = (bf16[576,128]{1,0:T(8,128)(2,1)S(1)}, bf16[576,128]{1,0:T(8,128)(2,1)S(1)}, u32[]{:S(2)}, u32[]{:S(2)}) collective-permute-start(bf16[576,128]{1,0:T(8,128)(2,1)S(1)} %get-tuple-element.67), channel_id=1, source_target_pairs={{0,32},{1,33},{2,34},{3,35},{4,36},{5,37},{6,38},{7,39},{8,40},{9,... | collective-permute-start | bytes 442376 | tf_op jit(solution)/shard_map/ppermute | solution.py:31
  85.8 2.7 %collective-permute-start.19 = (bf16[576,128]{1,0:T(8,128)(2,1)S(1)}, bf16[576,128]{1,0:T(8,128)(2,1)S(1)}, u32[]{:S(2)}, u32[]{:S(2)}) collective-permute-start(bf16[576,128]{1,0:T(8,128)(2,1)S(1)} %get-tuple-element.68), channel_id=1, source_target_pairs={{0,64},{1,65},{2,66},{3,67},{4,68},{5,69},{6,70},{7,71},{8,72},{9,... | collective-permute-start | bytes 442376 | tf_op jit(solution)/shard_map/ppermute | solution.py:31
  88.5 0.2 collective-permute-start.20
  88.8 1.7 %collective-permute-start.8 = (bf16[128,512]{1,0:T(8,128)(2,1)S(1)}, bf16[128,512]{1,0:T(8,128)(2,1)S(1)}, u32[]{:S(2)}, u32[]{:S(2)}) collective-permute-start(bf16[128,512]{1,0:T(8,128)(2,1)S(1)} %copy-done.1), channel_id=1, source_target_pairs={{0,128},{1,129},{2,130},{3,131},{4,132},{5,133},{6,134},{7,135},{8... | collective-permute-start | bytes 393224 | tf_op jit(solution)/shard_map/ppermute | solution.py:31
  90.5 0.0 collective-permute-done.18.refs_1_
  90.6 3.3 %collective-permute-done.19.refs_2_ = bf16[576,128]{1,0:T(8,128)(2,1)S(1)} collective-permute-done((bf16[576,128]{1,0:T(8,128)(2,1)S(1)}, bf16[576,128]{1,0:T(8,128)(2,1)S(1)}, u32[]{:S(2)}, u32[]{:S(2)}) %collective-permute-start.19) | collective-permute-done | bytes 147488 | tf_op jit(solution)/shard_map/ppermute | solution.py:31
  93.9 1.5 %collective-permute-done.20.refs_3_ = bf16[576,128]{1,0:T(8,128)(2,1)S(1)} collective-permute-done((bf16[576,128]{1,0:T(8,128)(2,1)S(1)}, bf16[576,128]{1,0:T(8,128)(2,1)S(1)}, u32[]{:S(2)}, u32[]{:S(2)}) %collective-permute-start.20) | collective-permute-done | bytes 147488 | tf_op jit(solution)/shard_map/ppermute | solution.py:31
  95.4 0.7 shard_map.108
  96.1 3.5 %collective-permute-start.21 = (bf16[144,128]{1,0:T(8,128)(2,1)S(1)}, bf16[144,128]{1,0:T(8,128)(2,1)S(1)}, u32[]{:S(2)}, u32[]{:S(2)}) collective-permute-start(bf16[144,128]{1,0:T(8,128)(2,1)S(1)} %get-tuple-element.71), channel_id=1, source_target_pairs={{0,2},{1,3},{2,0},{3,1},{4,6},{5,7},{6,4},{7,5},{8,10},{9,11},{10,... | collective-permute-start | bytes 110600 | tf_op jit(solution)/shard_map/ppermute | solution.py:31
  99.5 6.2 %collective-permute-start.22 = (bf16[144,128]{1,0:T(8,128)(2,1)S(1)}, bf16[144,128]{1,0:T(8,128)(2,1)S(1)}, u32[]{:S(2)}, u32[]{:S(2)}) collective-permute-start(bf16[144,128]{1,0:T(8,128)(2,1)S(1)} %get-tuple-element.72), channel_id=1, source_target_pairs={{0,4},{1,5},{2,6},{3,7},{4,0},{5,1},{6,2},{7,3},{8,12},{9,13},{10,... | collective-permute-start | bytes 110600 | tf_op jit(solution)/shard_map/ppermute | solution.py:31
  105.8 2.0 %collective-permute-done.22.refs_2_ = bf16[144,128]{1,0:T(8,128)(2,1)S(1)} collective-permute-done((bf16[144,128]{1,0:T(8,128)(2,1)S(1)}, bf16[144,128]{1,0:T(8,128)(2,1)S(1)}, u32[]{:S(2)}, u32[]{:S(2)}) %collective-permute-start.22) | collective-permute-done | bytes 36896 | tf_op jit(solution)/shard_map/ppermute | solution.py:31
  107.8 4.1 %collective-permute-done.23.refs_3_ = bf16[144,128]{1,0:T(8,128)(2,1)S(1)} collective-permute-done((bf16[144,128]{1,0:T(8,128)(2,1)S(1)}, bf16[144,128]{1,0:T(8,128)(2,1)S(1)}, u32[]{:S(2)}, u32[]{:S(2)}) %collective-permute-start.23) | collective-permute-done | bytes 36896 | tf_op jit(solution)/shard_map/ppermute | solution.py:31
  111.8 0.7 shard_map.109
  112.5 1.6 %shard_map.106 = (bf16[128,2048]{1,0:T(8,128)(2,1)}, bf16[128,1024]{1,0:T(8,128)(2,1)}, bf16[128,1024]{1,0:T(8,128)(2,1)}) custom-call(s32[3]{0:T(128)S(1)} %pad_add_fusion.where, bf16[8,128,384]{2,1,0:T(8,128)(2,1)S(1)} %all-to-all-done.1.returned, bf16[128,512]{1,0:T(8,128)(2,1)S(1)} %get-tuple-element.60.near, bf16[128,512]{1,0:T(8,128)(2,1)S(1)} %collective-permute-done.8.far), custom_call_target="tpu_custom_call" | custom-call | tf_op jit(solution)/shard_map/pallas_call | solution.py:400
  (22 shorter events, 0.1 us)
Async XLA Ops:
  3.9 6.1 %copy-start.3 = (bf16[1,128,4608]{2,1,0:T(8,128)(2,1)S(1)}, bf16[1,128,4608]{2,1,0:T(8,128)(2,1)}, u32[]{:S(2)}) copy-start(bf16[1,128,4608]{2,1,0:T(8,128)(2,1)} %param.12) | copy-start | bytes 3538948
  3.9 30.6 %all-to-all-start = ((bf16[8,144,768]{2,1,0:T(8,128)(2,1)}), bf16[8,144,768]{2,1,0:T(8,128)(2,1)S(1)}, u32[]{:S(2)}, u32[]{:S(2)}) async-start(bf16[8,144,768]{2,1,0:T(8,128)(2,1)} %shard_map.102), calls=%async_computation | async-start | bytes 3538944 | tf_op jit(solution)/shard_map/all_to_all | solution.py:332
  9.9 24.6 %copy-start.2 = (s32[1,8]{1,0:T(1,128)S(1)}, s32[1,8]{1,0:T(1,128)}, u32[]{:S(2)}) copy-start(s32[1,8]{1,0:T(1,128)} %lengths.1) | copy-start | bytes 100
  10.9 10.2 %collective-permute-start = (bf16[128,1152]{1,0:T(8,128)(2,1)}, bf16[128,1152]{1,0:T(8,128)(2,1)S(1)}, u32[]{:S(2)}, u32[]{:S(2)}) collective-permute-start(bf16[128,1152]{1,0:T(8,128)(2,1)} %get-tuple-element.42), channel_id=1, source_target_pairs={{0,8},{1,9},{2,10},{3,11},{4,12},{5,13},{6,14},{7,15},{8,0},{9,1},... | collective-permute-start | bytes 884744 | tf_op jit(solution)/shard_map/ppermute | solution.py:31
  12.3 15.5 %collective-permute-start.1 = (bf16[128,1152]{1,0:T(8,128)(2,1)}, bf16[128,1152]{1,0:T(8,128)(2,1)S(1)}, u32[]{:S(2)}, u32[]{:S(2)}) collective-permute-start(bf16[128,1152]{1,0:T(8,128)(2,1)} %get-tuple-element.43), channel_id=1, source_target_pairs={{0,16},{1,17},{2,18},{3,19},{4,20},{5,21},{6,22},{7,23},{8,24},{9,... | collective-permute-start | bytes 884744 | tf_op jit(solution)/shard_map/ppermute | solution.py:31
  15.1 15.2 %collective-permute-start.2 = (bf16[128,1152]{1,0:T(8,128)(2,1)S(1)}, bf16[128,1152]{1,0:T(8,128)(2,1)S(1)}, u32[]{:S(2)}, u32[]{:S(2)}) collective-permute-start(bf16[128,1152]{1,0:T(8,128)(2,1)S(1)} %get-tuple-element.44), channel_id=1, source_target_pairs={{0,24},{1,25},{2,26},{3,27},{4,28},{5,29},{6,30},{7,31},{8,16},{9,... | collective-permute-start | bytes 884744 | tf_op jit(solution)/shard_map/ppermute | solution.py:31
  32.4 10.5 %collective-permute-start.3 = (bf16[288,512]{1,0:T(8,128)(2,1)}, bf16[288,512]{1,0:T(8,128)(2,1)S(1)}, u32[]{:S(2)}, u32[]{:S(2)}) collective-permute-start(bf16[288,512]{1,0:T(8,128)(2,1)} %get-tuple-element.45.refs_0_), channel_id=1, source_target_pairs={{0,128},{1,129},{2,130},{3,131},{4,132},{5,133},{6,134},{7,135},{8... | collective-permute-start | bytes 884744 | tf_op jit(solution)/shard_map/ppermute | solution.py:31
  32.8 14.3 %collective-permute-start.4 = (bf16[288,512]{1,0:T(8,128)(2,1)}, bf16[288,512]{1,0:T(8,128)(2,1)S(1)}, u32[]{:S(2)}, u32[]{:S(2)}) collective-permute-start(bf16[288,512]{1,0:T(8,128)(2,1)} %get-tuple-element.47.refs_1_), channel_id=1, source_target_pairs={{0,128},{1,129},{2,130},{3,131},{4,132},{5,133},{6,134},{7,135},{8... | collective-permute-start | bytes 884744 | tf_op jit(solution)/shard_map/ppermute | solution.py:31
  34.5 22.5 %collective-permute-start.9 = (bf16[576,512]{1,0:T(8,128)(2,1)S(1)}, bf16[576,512]{1,0:T(8,128)(2,1)S(1)}, u32[]{:S(2)}, u32[]{:S(2)}) collective-permute-start(bf16[576,512]{1,0:T(8,128)(2,1)S(1)} %get-tuple-element.65), channel_id=1, source_target_pairs={{0,1},{1,0},{2,3},{3,2},{4,5},{5,4},{6,7},{7,6},{8,9},{9,8},{10,11... | collective-permute-start | bytes 1769480 | tf_op jit(solution)/shard_map/ppermute | solution.py:31
  42.8 6.2 %collective-permute-start.7 = (bf16[2,128,128]{2,1,0:T(8,128)(2,1)S(1)}, bf16[2,128,128]{2,1,0:T(8,128)(2,1)S(1)}, u32[]{:S(2)}, u32[]{:S(2)}) collective-permute-start(bf16[2,128,128]{2,1,0:T(8,128)(2,1)S(1)} %get-tuple-element.56), channel_id=1, source_target_pairs={{0,96},{1,97},{2,98},{3,99},{4,100},{5,101},{6,102},{7,103},{8,104... | collective-permute-start | bytes 196616 | tf_op jit(solution)/shard_map/ppermute | solution.py:31
  45.6 6.4 %collective-permute-start.6 = (bf16[2,128,128]{2,1,0:T(8,128)(2,1)S(1)}, bf16[2,128,128]{2,1,0:T(8,128)(2,1)S(1)}, u32[]{:S(2)}, u32[]{:S(2)}) collective-permute-start(bf16[2,128,128]{2,1,0:T(8,128)(2,1)S(1)} %get-tuple-element.53), channel_id=1, source_target_pairs={{0,64},{1,65},{2,66},{3,67},{4,68},{5,69},{6,70},{7,71},{8,72},{9,... | collective-permute-start | bytes 196616 | tf_op jit(solution)/shard_map/ppermute | solution.py:31
  46.5 5.6 %collective-permute-start.5 = (bf16[2,128,128]{2,1,0:T(8,128)(2,1)S(1)}, bf16[2,128,128]{2,1,0:T(8,128)(2,1)S(1)}, u32[]{:S(2)}, u32[]{:S(2)}) collective-permute-start(bf16[2,128,128]{2,1,0:T(8,128)(2,1)S(1)} %get-tuple-element.50), channel_id=1, source_target_pairs={{0,32},{1,33},{2,34},{3,35},{4,36},{5,37},{6,38},{7,39},{8,40},{9,... | collective-permute-start | bytes 196616 | tf_op jit(solution)/shard_map/ppermute | solution.py:31
  52.6 6.1 %copy-start = (bf16[128,512]{1,0:T(8,128)(2,1)}, bf16[128,512]{1,0:T(8,128)(2,1)S(1)}, u32[]{:S(2)}) copy-start(bf16[128,512]{1,0:T(8,128)(2,1)S(1)} %get-tuple-element.61) | copy-start | bytes 393220
  52.7 59.8 %all-to-all-start.1 = ((bf16[8,128,384]{2,1,0:T(8,128)(2,1)}), bf16[8,128,384]{2,1,0:T(8,128)(2,1)S(1)}, u32[]{:S(2)}, u32[]{:S(2)}) async-start(bf16[8,128,384]{2,1,0:T(8,128)(2,1)} %get-tuple-element.59), calls=%async_computation.1 | async-start | bytes 1572864 | tf_op jit(solution)/shard_map/all_to_all | solution.py:378
  57.0 21.4 %collective-permute-start.10 = (bf16[576,512]{1,0:T(8,128)(2,1)S(1)}, bf16[576,512]{1,0:T(8,128)(2,1)S(1)}, u32[]{:S(2)}, u32[]{:S(2)}) collective-permute-start(bf16[576,512]{1,0:T(8,128)(2,1)S(1)} %collective-permute-done.9.refs_2_), channel_id=1, source_target_pairs={{0,128},{1,129},{2,130},{3,131},{4,132},{5,133},{6,134},{7,135},{8... | collective-permute-start | bytes 1769480 | tf_op jit(solution)/shard_map/ppermute | solution.py:31
  57.1 14.1 %collective-permute-start.13 = (bf16[2,128,512]{2,1,0:T(8,128)(2,1)S(1)}, bf16[2,128,512]{2,1,0:T(8,128)(2,1)S(1)}, u32[]{:S(2)}, u32[]{:S(2)}) collective-permute-start(bf16[2,128,512]{2,1,0:T(8,128)(2,1)S(1)} %get-tuple-element.58.refs_6_), channel_id=1, source_target_pairs={{0,24},{1,25},{2,26},{3,27},{4,28},{5,29},{6,30},{7,31},{8,16},{9,... | collective-permute-start | bytes 786440 | tf_op jit(solution)/shard_map/ppermute | solution.py:31
  58.2 12.9 %collective-permute-start.12 = (bf16[2,128,512]{2,1,0:T(8,128)(2,1)S(1)}, bf16[2,128,512]{2,1,0:T(8,128)(2,1)S(1)}, u32[]{:S(2)}, u32[]{:S(2)}) collective-permute-start(bf16[2,128,512]{2,1,0:T(8,128)(2,1)S(1)} %get-tuple-element.58.refs_6_), channel_id=1, source_target_pairs={{0,16},{1,17},{2,18},{3,19},{4,20},{5,21},{6,22},{7,23},{8,24},{9,... | collective-permute-start | bytes 786440 | tf_op jit(solution)/shard_map/ppermute | solution.py:31
  58.7 13.0 %collective-permute-start.11 = (bf16[2,128,512]{2,1,0:T(8,128)(2,1)S(1)}, bf16[2,128,512]{2,1,0:T(8,128)(2,1)S(1)}, u32[]{:S(2)}, u32[]{:S(2)}) collective-permute-start(bf16[2,128,512]{2,1,0:T(8,128)(2,1)S(1)} %get-tuple-element.58.refs_6_), channel_id=1, source_target_pairs={{0,8},{1,9},{2,10},{3,11},{4,12},{5,13},{6,14},{7,15},{8,0},{9,1},... | collective-permute-start | bytes 786440 | tf_op jit(solution)/shard_map/ppermute | solution.py:31
  61.2 27.6 %copy-start.1 = (bf16[128,512]{1,0:T(8,128)(2,1)S(1)}, bf16[128,512]{1,0:T(8,128)(2,1)}, u32[]{:S(2)}) copy-start(bf16[128,512]{1,0:T(8,128)(2,1)} %copy-done) | copy-start | bytes 393220
  61.2 17.2 %collective-permute-start.14 = (bf16[2,128,512]{2,1,0:T(8,128)(2,1)S(1)}, bf16[2,128,512]{2,1,0:T(8,128)(2,1)S(1)}, u32[]{:S(2)}, u32[]{:S(2)}) collective-permute-start(bf16[2,128,512]{2,1,0:T(8,128)(2,1)S(1)} %get-tuple-element.58.refs_6_), channel_id=1, source_target_pairs={{0,1},{1,0},{2,3},{3,2},{4,5},{5,4},{6,7},{7,6},{8,9},{9,8},{10,11... | collective-permute-start | bytes 786440 | tf_op jit(solution)/shard_map/ppermute | solution.py:31
  71.1 7.3 %collective-permute-start.17 = (bf16[2,128,512]{2,1,0:T(8,128)(2,1)S(1)}, bf16[2,128,512]{2,1,0:T(8,128)(2,1)S(1)}, u32[]{:S(2)}, u32[]{:S(2)}) collective-permute-start(bf16[2,128,512]{2,1,0:T(8,128)(2,1)S(1)} %collective-permute-done.13.refs_9_), channel_id=1, source_target_pairs={{0,1},{1,0},{2,3},{3,2},{4,5},{5,4},{6,7},{7,6},{8,9},{9,8},{10,11... | collective-permute-start | bytes 786440 | tf_op jit(solution)/shard_map/ppermute | solution.py:31
  71.2 7.3 %collective-permute-start.16 = (bf16[2,128,512]{2,1,0:T(8,128)(2,1)S(1)}, bf16[2,128,512]{2,1,0:T(8,128)(2,1)S(1)}, u32[]{:S(2)}, u32[]{:S(2)}) collective-permute-start(bf16[2,128,512]{2,1,0:T(8,128)(2,1)S(1)} %collective-permute-done.12.refs_8_), channel_id=1, source_target_pairs={{0,1},{1,0},{2,3},{3,2},{4,5},{5,4},{6,7},{7,6},{8,9},{9,8},{10,11... | collective-permute-start | bytes 786440 | tf_op jit(solution)/shard_map/ppermute | solution.py:31
  71.8 6.7 %collective-permute-start.15 = (bf16[2,128,512]{2,1,0:T(8,128)(2,1)S(1)}, bf16[2,128,512]{2,1,0:T(8,128)(2,1)S(1)}, u32[]{:S(2)}, u32[]{:S(2)}) collective-permute-start(bf16[2,128,512]{2,1,0:T(8,128)(2,1)S(1)} %collective-permute-done.11.refs_7_), channel_id=1, source_target_pairs={{0,1},{1,0},{2,3},{3,2},{4,5},{5,4},{6,7},{7,6},{8,9},{9,8},{10,11... | collective-permute-start | bytes 786440 | tf_op jit(solution)/shard_map/ppermute | solution.py:31
  84.0 6.6 %collective-permute-start.18 = (bf16[576,128]{1,0:T(8,128)(2,1)S(1)}, bf16[576,128]{1,0:T(8,128)(2,1)S(1)}, u32[]{:S(2)}, u32[]{:S(2)}) collective-permute-start(bf16[576,128]{1,0:T(8,128)(2,1)S(1)} %get-tuple-element.67), channel_id=1, source_target_pairs={{0,32},{1,33},{2,34},{3,35},{4,36},{5,37},{6,38},{7,39},{8,40},{9,... | collective-permute-start | bytes 442376 | tf_op jit(solution)/shard_map/ppermute | solution.py:31
  85.8 8.0 %collective-permute-start.19 = (bf16[576,128]{1,0:T(8,128)(2,1)S(1)}, bf16[576,128]{1,0:T(8,128)(2,1)S(1)}, u32[]{:S(2)}, u32[]{:S(2)}) collective-permute-start(bf16[576,128]{1,0:T(8,128)(2,1)S(1)} %get-tuple-element.68), channel_id=1, source_target_pairs={{0,64},{1,65},{2,66},{3,67},{4,68},{5,69},{6,70},{7,71},{8,72},{9,... | collective-permute-start | bytes 442376 | tf_op jit(solution)/shard_map/ppermute | solution.py:31
  88.5 6.9 %collective-permute-start.20 = (bf16[576,128]{1,0:T(8,128)(2,1)S(1)}, bf16[576,128]{1,0:T(8,128)(2,1)S(1)}, u32[]{:S(2)}, u32[]{:S(2)}) collective-permute-start(bf16[576,128]{1,0:T(8,128)(2,1)S(1)} %get-tuple-element.69), channel_id=1, source_target_pairs={{0,96},{1,97},{2,98},{3,99},{4,100},{5,101},{6,102},{7,103},{8,104... | collective-permute-start | bytes 442376 | tf_op jit(solution)/shard_map/ppermute | solution.py:31
  88.8 23.7 %collective-permute-start.8 = (bf16[128,512]{1,0:T(8,128)(2,1)S(1)}, bf16[128,512]{1,0:T(8,128)(2,1)S(1)}, u32[]{:S(2)}, u32[]{:S(2)}) collective-permute-start(bf16[128,512]{1,0:T(8,128)(2,1)S(1)} %copy-done.1), channel_id=1, source_target_pairs={{0,128},{1,129},{2,130},{3,131},{4,132},{5,133},{6,134},{7,135},{8... | collective-permute-start | bytes 393224 | tf_op jit(solution)/shard_map/ppermute | solution.py:31
  96.1 9.7 %collective-permute-start.21 = (bf16[144,128]{1,0:T(8,128)(2,1)S(1)}, bf16[144,128]{1,0:T(8,128)(2,1)S(1)}, u32[]{:S(2)}, u32[]{:S(2)}) collective-permute-start(bf16[144,128]{1,0:T(8,128)(2,1)S(1)} %get-tuple-element.71), channel_id=1, source_target_pairs={{0,2},{1,3},{2,0},{3,1},{4,6},{5,7},{6,4},{7,5},{8,10},{9,11},{10,... | collective-permute-start | bytes 110600 | tf_op jit(solution)/shard_map/ppermute | solution.py:31
  99.5 8.2 %collective-permute-start.22 = (bf16[144,128]{1,0:T(8,128)(2,1)S(1)}, bf16[144,128]{1,0:T(8,128)(2,1)S(1)}, u32[]{:S(2)}, u32[]{:S(2)}) collective-permute-start(bf16[144,128]{1,0:T(8,128)(2,1)S(1)} %get-tuple-element.72), channel_id=1, source_target_pairs={{0,4},{1,5},{2,6},{3,7},{4,0},{5,1},{6,2},{7,3},{8,12},{9,13},{10,... | collective-permute-start | bytes 110600 | tf_op jit(solution)/shard_map/ppermute | solution.py:31
  105.8 6.1 %collective-permute-start.23 = (bf16[144,128]{1,0:T(8,128)(2,1)S(1)}, bf16[144,128]{1,0:T(8,128)(2,1)S(1)}, u32[]{:S(2)}, u32[]{:S(2)}) collective-permute-start(bf16[144,128]{1,0:T(8,128)(2,1)S(1)} %get-tuple-element.73), channel_id=1, source_target_pairs={{0,6},{1,7},{2,4},{3,5},{4,2},{5,3},{6,0},{7,1},{8,14},{9,15},{10,... | collective-permute-start | bytes 110600 | tf_op jit(solution)/shard_map/ppermute | solution.py:31

commit v3 on v2

--- a/solution.py
+++ b/solution.py
@@ -102,12 +102,11 @@
 
 
 def attention_kernel(where, lengths, *refs):
-    packed, back = refs[:2]
-    values = refs[2:6]
-    held, key_turned, dk, dv, sem = refs[6:]
-    mine = where[0]
-    copy = pltpu.make_async_copy(packed, held, sem)
-    copy.start()
+    held = refs[0]
+    backs = refs[1:5]
+    values = refs[5:9]
+    key_turned, dq, dk, dv = refs[9:]
+    mine = where[0]
     dk[...] = jnp.zeros_like(dk)
     dv[...] = jnp.zeros_like(dv)
     ends = []
@@ -115,7 +114,6 @@
     for d in range(8):
         total = total + lengths[0, d]
         ends.append(total)
-    copy.wait()
     for n in range(BLOCKS):
         key_turned[n] = held[n, 0:ROWS, 512:640].T
 
@@ -172,8 +170,8 @@
                 dk[kb] += nn(dscore, queries)
                 turned = turned + nn(key_turned[kb], dscore)
             straight = turned.T
-            back[b, :, 0:128] = straight[0:ROWS].astype(BF)
-            back[b, :, 128:256] = straight[ROWS:].astype(BF)
+            dq[b, :, 0:128] = straight[0:ROWS].astype(BF)
+            dq[b, :, 128:256] = straight[ROWS:].astype(BF)
 
         for number in range(1, 6):
 
@@ -184,32 +182,23 @@
         return carry
 
     lax.fori_loop(0, BLOCKS, block, 0)
-    for n in range(BLOCKS):
-        back[n, :, 256:384] = dk[n].astype(BF)
     for k in range(4):
         for half in range(2):
-            values[k][half] = dv[half * 4 + (mine % 4 ^ k)].astype(BF)
+            block = half * 4 + (mine % 4 ^ k)
+            backs[k][half, :, 0:256] = dq[block]
+            backs[k][half, :, 256:384] = dk[block].astype(BF)
+            values[k][half] = dv[block].astype(BF)
 
 
 def turn_kernel(where, *refs):
-    pieces, low, high, far = refs[:4], refs[4], refs[5], refs[6]
-    held, turned, sems = refs[7:]
+    pieces, near, far, turned = refs[:4], refs[4], refs[5], refs[6]
     core = where[1]
-    copies = []
     for n in range(4):
-        copy = pltpu.make_async_copy(pieces[n], held.at[n], sems.at[n])
-        copy.start()
-        copies.append(copy)
-    for copy in copies:
-        copy.wait()
-
-    for n in range(4):
-        turned[...] = held[n].T
+        turned[...] = pieces[n][...].T
         lanes = slice(n * ROWS, (n + 1) * ROWS)
         for z in range(4):
             rows = pl.ds(z * 144, 144)
-            near = (low, high)[z // 2]
-            near[pl.ds(z % 2 * 144, 144), lanes] = turned[pl.ds(pl.multiple_of((z * 2 + core) * 144, 16), 144)]
+            near[rows, lanes] = turned[pl.ds(pl.multiple_of((z * 2 + core) * 144, 16), 144)]
             far[rows, lanes] = turned[pl.ds(pl.multiple_of((z * 2 + 1 - core) * 144, 16), 144)]
 
 
@@ -226,37 +215,23 @@
 
 
 def weight_kernel(where, *refs):
-    lefts, rights, outs = refs[:6], refs[6:14], refs[14:18]
-    left, right, total, sems = refs[18:]
+    lefts, rights, outs, total = refs[:4], refs[4:12], refs[12:16], refs[16]
     mine = where[0]
     half = mine // 4
-    copies = [[], [], [], []]
-
-    def fetch(n, source, target):
-        copy = pltpu.make_async_copy(source, target, sems.at[n, len(copies[n])])
-        copy.start()
-        copies[n].append(copy)
-
-    for n in range(4):
-        if n % 2:
-            fetch(n, lefts[2 + n // 2 * 3], left.at[n])
-        else:
-            fetch(n, lefts[n // 2 * 3], left.at[n, pl.ds(0, 288)])
-            fetch(n, lefts[n // 2 * 3 + 1], left.at[n, pl.ds(288, 288)])
-        for k in range(4):
-            fetch(
-                n,
-                rights[n % 2 * 4 + k].at[half if n < 2 else 1 - half],
-                right.at[n, pl.ds(k * ROWS, ROWS)],
-            )
     value = jnp.zeros((576, 512), F32)
-    for n in range(4):
-        for copy in copies[n]:
-            copy.wait()
-        value = value + nn(left[n], right[n])
+    for n, left in enumerate(lefts):
+        source = half if n < 2 else 1 - half
+        rows = [right[source] for right in rights[n % 2 * 4 : n % 2 * 4 + 4]]
+        value = value + nn(left[...], jnp.concatenate(rows, axis=0))
     total[...] = (value * (1.0 / math.sqrt(32768.0))).astype(BF)
     for k, out in enumerate(outs):
         out[...] = total[:, pl.ds(pl.multiple_of((mine % 4 ^ k) * HEAD, HEAD), HEAD)]
+
+
+def merge_kernel(where, *refs):
+    mine = where[0]
+    for k, piece in enumerate(refs[:4]):
+        refs[4][mine % 4 ^ k] = piece[1 - mine // 4]
 
 
 def sum_kernel(where, *refs):
@@ -277,11 +252,22 @@
     refs[4][...] = total
 
 
-def unpack_kernel(where, returned, near, far, query_grad, key_grad, value_grad):
-    half = where[0] // 4
-    for n in range(BLOCKS):
-        query_grad[:, n * 256 : (n + 1) * 256] = returned[n, :, 0:256]
-        key_grad[:, n * 128 : (n + 1) * 128] = returned[n, :, 256:384]
+def unpack_kernel(where, *refs):
+    pieces = refs[:4]
+    crossed, near, far, query_grad, key_grad, value_grad = refs[4:]
+    mine = where[0]
+    half = mine // 4
+    for k, piece in enumerate(pieces):
+        head = mine ^ k
+        wide = pl.ds(pl.multiple_of(head * 256, 256), 256)
+        thin = pl.ds(pl.multiple_of(head * 128, 128), 128)
+        query_grad[:, wide] = piece[half, :, 0:256]
+        key_grad[:, thin] = piece[half, :, 256:384]
+        head = (1 - half) * 4 + k
+        wide = pl.ds(pl.multiple_of(head * 256, 256), 256)
+        thin = pl.ds(pl.multiple_of(head * 128, 128), 128)
+        query_grad[:, wide] = crossed[k, :, 0:256]
+        key_grad[:, thin] = crossed[k, :, 256:384]
     value_grad[:, pl.ds(pl.multiple_of(half * 512, 512), 512)] = near[...]
     value_grad[:, pl.ds(pl.multiple_of((1 - half) * 512, 512), 512)] = far[...]
 
@@ -295,12 +281,12 @@
     return jax.ShapeDtypeStruct(dims, dtype)
 
 
-def call(kernel, outs, ins, scratch=(), flops=0, moved=0, limit=16):
+def call(kernel, outs, ins, scratch=(), flops=0, moved=0, limit=16, place=VMEM):
     return pl.pallas_call(
         kernel,
         out_shape=outs,
         in_specs=ins,
-        out_specs=jax.tree.map(lambda _: VMEM, outs),
+        out_specs=jax.tree.map(lambda _: place, outs),
         scratch_shapes=list(scratch),
         compiler_params=pltpu.CompilerParams(vmem_limit_bytes=limit * MIB),
         cost_estimate=pl.CostEstimate(flops=flops, bytes_accessed=moved, transcendentals=0),
@@ -313,8 +299,6 @@
     mine = lax.axis_index("ctx")
     dp = lax.axis_index("dp")
     x = dp // 8
-    where = jnp.stack([mine, dp % 2, dp // 2 % 4]).astype(jnp.int32)
-
     packed = call(
         pack_kernel,
         shape(BLOCKS, ROWS + TAIL, PACKED),
@@ -329,6 +313,7 @@
         ],
         limit=60,
     )(queries[0], key_states[0], value_states[0], output_grad[0], saved_output[0])
+    where = after(jnp.stack([mine, dp % 2, dp // 2 % 4]).astype(jnp.int32), packed)
     arrived = lax.all_to_all(packed, "ctx", 0, 0, tiled=True)
 
     inputs = layer_input[0]
@@ -336,38 +321,33 @@
     for k in range(4):
         piece = lax.dynamic_slice(inputs, (0, (x ^ k) * 1152), (ROWS, 1152))
         own.append(over_x(after(piece, packed), k))
-    near_low, near_high, far_rows = call(
+    near_rows, far_rows = call(
         turn_kernel,
-        [shape(288, 512)] * 2 + [shape(576, 512)],
-        [SMEM] + [ANY] * 4,
-        [
-            pltpu.VMEM((4, ROWS, 1152), BF),
-            pltpu.VMEM((1152, ROWS), BF),
-            pltpu.SemaphoreType.DMA((4,)),
-        ],
+        [shape(576, 512)] * 2,
+        [SMEM] + [VMEM] * 4,
+        [pltpu.VMEM((1152, ROWS), BF)],
     )(where, *own)
     far_rows = over_core(far_rows)
-    across_low = over_ctx(near_low, 4)
-
-    back, *values = call(
+    across_near = over_ctx(near_rows, 4)
+
+    results = call(
         attention_kernel,
-        [shape(BLOCKS, ROWS, BACK)] + [shape(2, ROWS, HEAD)] * 4,
-        [SMEM, SMEM, ANY],
+        [shape(2, ROWS, BACK)] * 4 + [shape(2, ROWS, HEAD)] * 4,
+        [SMEM, SMEM, VMEM],
         [
-            pltpu.VMEM((BLOCKS, ROWS + TAIL, PACKED), BF),
             pltpu.VMEM((BLOCKS, HEAD, ROWS), BF),
+            pltpu.VMEM((BLOCKS, ROWS, 256), BF),
             pltpu.VMEM((BLOCKS, ROWS, HEAD), F32),
             pltpu.VMEM((BLOCKS, ROWS, HEAD), F32),
-            pltpu.SemaphoreType.DMA,
         ],
         flops=4_000_000_000,
         moved=4_000_000,
     )(where, document_lengths, arrived)
-
-    values = [after(value, across_low) for value in values]
-    across_high = over_ctx(near_high, 4)
-    across_far = over_ctx(far_rows, 4)
-    pieces = [after(over_y(values[k], k), across_high) for k in range(4)]
+    backs, values = results[:4], results[4:]
+
+    across_far = over_ctx(after(far_rows, values[0]), 4)
+    early = over_y(backs[1], 1)
+    pieces = [after(over_y(values[k], k), across_near, early) for k in range(4)]
     joined, near, far = call(
         join_kernel,
         [shape(2, ROWS, 512), shape(ROWS, 512), shape(ROWS, 512)],
@@ -375,33 +355,33 @@
     )(where, *pieces)
     rights = [over_x(joined, k) for k in range(4)]
     rights = rights + [over_core(right) for right in rights]
-    returned = lax.all_to_all(after(back, joined), "ctx", 0, 0, tiled=True)
+    returned = [early if k == 1 else over_y(after(backs[k], joined), k) for k in range(4)]
 
     parts = call(
         weight_kernel,
         [shape(576, HEAD)] * 4,
-        [SMEM] + [ANY] * 14,
-        [
-            pltpu.VMEM((4, 576, 512), BF),
-            pltpu.VMEM((4, 512, 512), BF),
-            pltpu.VMEM((576, 512), BF),
-            pltpu.SemaphoreType.DMA((4, 6)),
-        ],
+        [SMEM] + [VMEM] * 12,
+        [pltpu.VMEM((576, 512), BF)],
         flops=1_300_000_000,
         moved=4_000_000,
-    )(where, near_low, near_high, far_rows, across_low, across_high, across_far, *rights)
+    )(where, after(near_rows, *returned), far_rows, across_near, across_far, *rights)
+    crossed = call(merge_kernel, shape(4, ROWS, BACK), [SMEM] + [VMEM] * 4)(
+        where, *[after(piece, parts[0]) for piece in returned]
+    )
+    crossed = over_ctx(crossed, 4)
     far = over_ctx(far, 4)
     reduced = [over_y(parts[k], k) for k in range(4)]
     blocks = call(
         sum_kernel, [shape(144, HEAD)] * 4, [SMEM] + [VMEM] * 4, [pltpu.VMEM((576, HEAD), BF)]
     )(where, *reduced)
     landed = [over_z(blocks[k], k) for k in range(4)]
-    weight_grad = call(last_kernel, shape(144, HEAD, dtype=F32), [VMEM] * 4)(*landed)
     query_grad, key_grad, value_grad = call(
         unpack_kernel,
         [shape(ROWS, 2048), shape(ROWS, 1024), shape(ROWS, 1024)],
-        [SMEM] + [VMEM] * 3,
-    )(where, returned, near, far)
+        [SMEM] + [VMEM] * 7,
+    )(where, *returned, crossed, near, far)
+    landed[1] = after(landed[1], query_grad)
+    weight_grad = call(last_kernel, shape(144, HEAD, dtype=F32), [VMEM] * 4)(*landed)
     return query_grad[None], key_grad[None], value_grad[None], weight_grad
 
 

time: 114 us -> 104 us (0.912)
  waiting for transfers between devices: 47.3 us -> 39.3 us
  Pallas kernels: 22.8 us -> 19 us
    ppermute x24 -> x27, waiting for transfers between devices: 47.3 us -> 39.3 us  [spread(): return lax.ppermute(block, ('ctx', 'dp'), route)]
    ppermute x24 -> x27, starting transfers between devices: 31.9 us -> 36.7 us  [spread(): return lax.ppermute(block, ('ctx', 'dp'), route)]
    all_to_all x1 -> x0, starting transfers between devices: 4.33 us -> none  [body(): returned = lax.all_to_all(after(back, joined), 'ctx', 0, 0, tiled=True)]
    pallas_call x3 -> x4, Pallas kernels: 16 us -> 12.2 us  [the longest x1 7.71 us: body(): call(attention_kernel, [shape(2, ROWS, BACK)] * 4 + [shape(2, ROWS, HEAD)...]
    dynamic_slice x1, local copies, waits for them, and re-layouts: 0.9 us -> 2.05 us  [body(): piece = lax.dynamic_slice(inputs, (0, (x ^ k) * 1152), (ROWS, 1152))]
  transfers between devices with their start and end apart: 26 -> 28, of which waited for: 12 -> 19; matrix products, arithmetic and copies ran while one was open for 1% -> 2% of each run, Pallas kernels for 16% -> 12%
where the time goes in v3:
time: 104 us
  starting transfers between devices  42.6 us (41%)
  waiting for transfers between devices  39.3 us (38%)
  Pallas kernels  19 us (18%)
  local copies, waits for them, and re-layouts  2.05 us (2%)
    ppermute x27, waiting for transfers between devices, spread(): return lax.ppermute(block, ('ctx', 'dp'), route)  39.3 us
    ppermute x27, starting transfers between devices, spread(): return lax.ppermute(block, ('ctx', 'dp'), route)  36.7 us
    pallas_call x1, Pallas kernels, body(): call(attention_kernel, [shape(2, ROWS, BACK)] * 4 + [shape(2, ROWS, HEAD)...  7.71 us
    all_to_all x1, starting transfers between devices, body(): arrived = lax.all_to_all(packed, 'ctx', 0, 0, tiled=True)  5.94 us
    pallas_call x1, Pallas kernels, body(): call(pack_kernel, shape(BLOCKS, ROWS + TAIL, PACKED), [ANY] * 5, [pltpu.V...  3.21 us
  transfers between devices with their start and end apart: 28, of which 19 were waited for; matrix products, arithmetic and copies ran while one was open for 2% of the time, Pallas kernels for 12%

profile of v3, /device:TPU:32, one launch (start us, length us, event | category | flops | bytes accessed | tf_op | source)
XLA Modules:
  0.0 103.7 jit_solution(12369222400846526187)
XLA Ops:
  0.6 3.2 %shard_map.102 = bf16[8,144,768]{2,1,0:T(8,128)(2,1)} custom-call(bf16[128,2048]{1,0:T(8,128)(2,1)} %bitcast.19, bf16[128,1024]{1,0:T(8,128)(2,1)} %bitcast.22, bf16[128,1024]{1,0:T(8,128)(2,1)} %bitcast.23, bf16[128,2048]{1,0:T(8,128)(2,1)} %bitcast.20, bf16[128,2048]{1,0:T(8,128)(2,1)} %bitcast.21), custom_call_target="tpu_custom_call" | custom-call | tf_op jit(solution)/shard_map/pallas_call | solution.py:302
  3.8 5.9 %all-to-all-start = ((bf16[8,144,768]{2,1,0:T(8,128)(2,1)}), bf16[8,144,768]{2,1,0:T(8,128)(2,1)S(1)}, u32[]{:S(2)}, u32[]{:S(2)}) async-start(bf16[8,144,768]{2,1,0:T(8,128)(2,1)} %shard_map.102), calls=%async_computation | async-start | bytes 3538944 | tf_op jit(solution)/shard_map/all_to_all | solution.py:317
  9.8 2.0 %dynamic-slice_bitcast_fusion = (bf16[128,1152]{1,0:T(8,128)(2,1)S(1)}, bf16[128,1152]{1,0:T(8,128)(2,1)}, bf16[128,1152]{1,0:T(8,128)(2,1)S(1)}, bf16[128,1152]{1,0:T(8,128)(2,1)S(1)}) fusion(bf16[1,128,4608]{2,1,0:T(8,128)(2,1)} %param.12, s32[]{:T(128)S(6)} %select_n.37, s32[]{:T(128)S(6)} %select_n.35, s32[]{:T(128)S(6)} %select_n.34, s32[]{:T(128)S(6)} %select_n.36), kind=kLoop, calls=%fused_computation | loop fusion | bytes 2359312 | tf_op jit(solution)/shard_map/dynamic_slice | solution.py:322
  11.8 1.5 %collective-permute-start = (bf16[128,1152]{1,0:T(8,128)(2,1)}, bf16[128,1152]{1,0:T(8,128)(2,1)S(1)}, u32[]{:S(2)}, u32[]{:S(2)}) collective-permute-start(bf16[128,1152]{1,0:T(8,128)(2,1)} %get-tuple-element.51), channel_id=1, source_target_pairs={{0,8},{1,9},{2,10},{3,11},{4,12},{5,13},{6,14},{7,15},{8,0},{9,1},... | collective-permute-start | bytes 884744 | tf_op jit(solution)/shard_map/ppermute | solution.py:31
  13.3 2.7 %collective-permute-start.1 = (bf16[128,1152]{1,0:T(8,128)(2,1)S(1)}, bf16[128,1152]{1,0:T(8,128)(2,1)S(1)}, u32[]{:S(2)}, u32[]{:S(2)}) collective-permute-start(bf16[128,1152]{1,0:T(8,128)(2,1)S(1)} %get-tuple-element.52), channel_id=1, source_target_pairs={{0,16},{1,17},{2,18},{3,19},{4,20},{5,21},{6,22},{7,23},{8,24},{9,... | collective-permute-start | bytes 884744 | tf_op jit(solution)/shard_map/ppermute | solution.py:31
  16.1 0.5 collective-permute-start.2
  16.6 5.4 %collective-permute-done.refs_1_ = bf16[128,1152]{1,0:T(8,128)(2,1)S(1)} collective-permute-done((bf16[128,1152]{1,0:T(8,128)(2,1)}, bf16[128,1152]{1,0:T(8,128)(2,1)S(1)}, u32[]{:S(2)}, u32[]{:S(2)}) %collective-permute-start) | collective-permute-done | bytes 294944 | tf_op jit(solution)/shard_map/ppermute | solution.py:31
  22.0 6.9 %collective-permute-done.1.refs_2_ = bf16[128,1152]{1,0:T(8,128)(2,1)S(1)} collective-permute-done((bf16[128,1152]{1,0:T(8,128)(2,1)S(1)}, bf16[128,1152]{1,0:T(8,128)(2,1)S(1)}, u32[]{:S(2)}, u32[]{:S(2)}) %collective-permute-start.1) | collective-permute-done | bytes 294944 | tf_op jit(solution)/shard_map/ppermute | solution.py:31
  28.9 2.4 %collective-permute-done.2.refs_3_ = bf16[128,1152]{1,0:T(8,128)(2,1)S(1)} collective-permute-done((bf16[128,1152]{1,0:T(8,128)(2,1)S(1)}, bf16[128,1152]{1,0:T(8,128)(2,1)S(1)}, u32[]{:S(2)}, u32[]{:S(2)}) %collective-permute-start.2) | collective-permute-done | bytes 294944 | tf_op jit(solution)/shard_map/ppermute | solution.py:31
  31.2 1.9 %shard_map.104 = (bf16[576,512]{1,0:T(8,128)(2,1)S(1)}, bf16[576,512]{1,0:T(8,128)(2,1)}) custom-call(s32[3]{0:T(128)S(1)} %pad_add_fusion.where, bf16[128,1152]{1,0:T(8,128)(2,1)S(1)} %get-tuple-element.50.refs_0_, bf16[128,1152]{1,0:T(8,128)(2,1)S(1)} %collective-permute-done.refs_1_, bf16[128,1152]{1,0:T(8,128)(2,1)S(1)} %collective-permute-done.1.refs_2_, ...), custom_call_target="tpu_custom_call" | custom-call | tf_op jit(solution)/shard_map/pallas_call | solution.py:324
  33.4 7.7 %shard_map.103 = (bf16[2,128,384]{2,1,0:T(8,128)(2,1)S(1)}, bf16[2,128,384]{2,1,0:T(8,128)(2,1)S(1)}, bf16[2,128,384]{2,1,0:T(8,128)(2,1)S(1)}, bf16[2,128,384]{...) custom-call(s32[3]{0:T(128)S(1)} %pad_add_fusion.where, ...), custom_call_target="tpu_custom_call" | custom-call | flops 4000000000 | bytes 4000000 | tf_op jit(solution)/shard_map/pallas_call | solution.py:333
  41.1 1.8 %collective-permute-start.4 = (bf16[2,128,384]{2,1,0:T(8,128)(2,1)S(1)}, bf16[2,128,384]{2,1,0:T(8,128)(2,1)S(1)}, u32[]{:S(2)}, u32[]{:S(2)}) collective-permute-start(bf16[2,128,384]{2,1,0:T(8,128)(2,1)S(1)} %get-tuple-element.55), channel_id=1, source_target_pairs={{0,32},{1,33},{2,34},{3,35},{4,36},{5,37},{6,38},{7,39},{8,40},{9,... | collective-permute-start | bytes 589832 | tf_op jit(solution)/shard_map/ppermute | solution.py:31
  42.9 2.1 %collective-permute-start.7 = (bf16[2,128,128]{2,1,0:T(8,128)(2,1)S(1)}, bf16[2,128,128]{2,1,0:T(8,128)(2,1)S(1)}, u32[]{:S(2)}, u32[]{:S(2)}) collective-permute-start(bf16[2,128,128]{2,1,0:T(8,128)(2,1)S(1)} %get-tuple-element.61), channel_id=1, source_target_pairs={{0,96},{1,97},{2,98},{3,99},{4,100},{5,101},{6,102},{7,103},{8,104... | collective-permute-start | bytes 196616 | tf_op jit(solution)/shard_map/ppermute | solution.py:31
  45.0 0.6 collective-permute-start.6
  45.6 0.6 collective-permute-done.3.refs_2_
  46.2 1.5 %collective-permute-start.5 = (bf16[2,128,128]{2,1,0:T(8,128)(2,1)S(1)}, bf16[2,128,128]{2,1,0:T(8,128)(2,1)S(1)}, u32[]{:S(2)}, u32[]{:S(2)}) collective-permute-start(bf16[2,128,128]{2,1,0:T(8,128)(2,1)S(1)} %get-tuple-element.57), channel_id=1, source_target_pairs={{0,32},{1,33},{2,34},{3,35},{4,36},{5,37},{6,38},{7,39},{8,40},{9,... | collective-permute-start | bytes 196616 | tf_op jit(solution)/shard_map/ppermute | solution.py:31
  47.7 0.7 collective-permute-done.7.refs_3_
  48.7 3.6 %collective-permute-done.6.refs_2_ = bf16[2,128,128]{2,1,0:T(8,128)(2,1)S(1)} collective-permute-done((bf16[2,128,128]{2,1,0:T(8,128)(2,1)S(1)}, bf16[2,128,128]{2,1,0:T(8,128)(2,1)S(1)}, u32[]{:S(2)}, u32[]{:S(2)}) %collective-permute-start.6) | collective-permute-done | bytes 65568 | tf_op jit(solution)/shard_map/ppermute | solution.py:31
  52.4 0.6 shard_map.105
  53.0 1.6 %collective-permute-start.8 = (bf16[2,128,384]{2,1,0:T(8,128)(2,1)S(1)}, bf16[2,128,384]{2,1,0:T(8,128)(2,1)S(1)}, u32[]{:S(2)}, u32[]{:S(2)}) collective-permute-start(bf16[2,128,384]{2,1,0:T(8,128)(2,1)S(1)} %get-tuple-element.66), channel_id=1, source_target_pairs={{0,64},{1,65},{2,66},{3,67},{4,68},{5,69},{6,70},{7,71},{8,72},{9,... | collective-permute-start | bytes 589832 | tf_op jit(solution)/shard_map/ppermute | solution.py:31
  54.6 1.5 %collective-permute-start.11 = (bf16[576,512]{1,0:T(8,128)(2,1)S(1)}, bf16[576,512]{1,0:T(8,128)(2,1)S(1)}, u32[]{:S(2)}, u32[]{:S(2)}) collective-permute-start(bf16[576,512]{1,0:T(8,128)(2,1)S(1)} %collective-permute-done.10.refs_1_), channel_id=1, source_target_pairs={{0,128},{1,129},{2,130},{3,131},{4,132},{5,133},{6,134},{7,135},{8... | collective-permute-start | bytes 1769480 | tf_op jit(solution)/shard_map/ppermute | solution.py:31
  56.1 0.8 collective-permute-start.14
  56.8 0.6 collective-permute-start.13
  57.4 2.8 %collective-permute-start.12 = (bf16[2,128,512]{2,1,0:T(8,128)(2,1)S(1)}, bf16[2,128,512]{2,1,0:T(8,128)(2,1)S(1)}, u32[]{:S(2)}, u32[]{:S(2)}) collective-permute-start(bf16[2,128,512]{2,1,0:T(8,128)(2,1)S(1)} %get-tuple-element.63.refs_4_), channel_id=1, source_target_pairs={{0,8},{1,9},{2,10},{3,11},{4,12},{5,13},{6,14},{7,15},{8,0},{9,1},... | collective-permute-start | bytes 786440 | tf_op jit(solution)/shard_map/ppermute | solution.py:31
  60.2 1.4 %collective-permute-start.9 = (bf16[2,128,384]{2,1,0:T(8,128)(2,1)S(1)}, bf16[2,128,384]{2,1,0:T(8,128)(2,1)S(1)}, u32[]{:S(2)}, u32[]{:S(2)}) collective-permute-start(bf16[2,128,384]{2,1,0:T(8,128)(2,1)S(1)} %get-tuple-element.68), channel_id=1, source_target_pairs={{0,96},{1,97},{2,98},{3,99},{4,100},{5,101},{6,102},{7,103},{8,104... | collective-permute-start | bytes 589832 | tf_op jit(solution)/shard_map/ppermute | solution.py:31
  61.6 5.5 %collective-permute-done.9.refs_3_ = bf16[2,128,384]{2,1,0:T(8,128)(2,1)S(1)} collective-permute-done((bf16[2,128,384]{2,1,0:T(8,128)(2,1)S(1)}, bf16[2,128,384]{2,1,0:T(8,128)(2,1)S(1)}, u32[]{:S(2)}, u32[]{:S(2)}) %collective-permute-start.9) | collective-permute-done | bytes 196640 | tf_op jit(solution)/shard_map/ppermute | solution.py:31
  67.1 2.4 %collective-permute-done.14.refs_7_ = bf16[2,128,512]{2,1,0:T(8,128)(2,1)S(1)} collective-permute-done((bf16[2,128,512]{2,1,0:T(8,128)(2,1)S(1)}, bf16[2,128,512]{2,1,0:T(8,128)(2,1)S(1)}, u32[]{:S(2)}, u32[]{:S(2)}) %collective-permute-start.14) | collective-permute-done | bytes 262176 | tf_op jit(solution)/shard_map/ppermute | solution.py:31
  69.5 0.5 collective-permute-start.17
  70.2 0.9 collective-permute-done.18.refs_11_
  71.1 0.4 collective-permute-done.17.refs_10_
  71.4 0.4 collective-permute-done.16.refs_9_
  71.8 2.0 %shard_map.106 = (bf16[576,128]{1,0:T(8,128)(2,1)S(1)}, bf16[576,128]{1,0:T(8,128)(2,1)S(1)}, bf16[576,128]{1,0:T(8,128)(2,1)S(1)}, bf16[576,128]{1,0:T(8,128)(2,1)S(1)}) custom-call(s32[3]{0:T(128)S(1)} %pad_add_fusion.where, bf16[576,512]{1,0:T(8,128)(2,1)S(1)} %get-tuple-element.69.refs_0_, bf16[576,512]{1,0:T(8,128)(2,1)S(1)} %collective-permute-done.10.refs_1_, ...), custom_call_target="tpu_custom_call" | custom-call | flops 1300000000 | bytes 4000000 | tf_op jit(solution)/shard_map/pallas_call | solution.py:360
  73.9 0.6 shard_map.107
  74.5 0.6 collective-permute-start.19
  75.1 0.6 collective-permute-start.21
  75.7 1.8 %collective-permute-start.22 = (bf16[576,128]{1,0:T(8,128)(2,1)S(1)}, bf16[576,128]{1,0:T(8,128)(2,1)S(1)}, u32[]{:S(2)}, u32[]{:S(2)}) collective-permute-start(bf16[576,128]{1,0:T(8,128)(2,1)S(1)} %get-tuple-element.83), channel_id=1, source_target_pairs={{0,64},{1,65},{2,66},{3,67},{4,68},{5,69},{6,70},{7,71},{8,72},{9,... | collective-permute-start | bytes 442376 | tf_op jit(solution)/shard_map/ppermute | solution.py:31
  77.4 2.4 %collective-permute-start.23 = (bf16[576,128]{1,0:T(8,128)(2,1)S(1)}, bf16[576,128]{1,0:T(8,128)(2,1)S(1)}, u32[]{:S(2)}, u32[]{:S(2)}) collective-permute-start(bf16[576,128]{1,0:T(8,128)(2,1)S(1)} %get-tuple-element.84), channel_id=1, source_target_pairs={{0,96},{1,97},{2,98},{3,99},{4,100},{5,101},{6,102},{7,103},{8,104... | collective-permute-start | bytes 442376 | tf_op jit(solution)/shard_map/ppermute | solution.py:31
  79.8 1.5 %collective-permute-start.20 = (bf16[128,512]{1,0:T(8,128)(2,1)S(1)}, bf16[128,512]{1,0:T(8,128)(2,1)S(1)}, u32[]{:S(2)}, u32[]{:S(2)}) collective-permute-start(bf16[128,512]{1,0:T(8,128)(2,1)S(1)} %get-tuple-element.78), channel_id=1, source_target_pairs={{0,128},{1,129},{2,130},{3,131},{4,132},{5,133},{6,134},{7,135},{8... | collective-permute-start | bytes 393224 | tf_op jit(solution)/shard_map/ppermute | solution.py:31
  81.3 0.6 collective-permute-done.21.refs_1_
  81.8 2.5 %collective-permute-done.22.refs_2_ = bf16[576,128]{1,0:T(8,128)(2,1)S(1)} collective-permute-done((bf16[576,128]{1,0:T(8,128)(2,1)S(1)}, bf16[576,128]{1,0:T(8,128)(2,1)S(1)}, u32[]{:S(2)}, u32[]{:S(2)}) %collective-permute-start.22) | collective-permute-done | bytes 147488 | tf_op jit(solution)/shard_map/ppermute | solution.py:31
  84.3 2.3 %collective-permute-done.23.refs_3_ = bf16[576,128]{1,0:T(8,128)(2,1)S(1)} collective-permute-done((bf16[576,128]{1,0:T(8,128)(2,1)S(1)}, bf16[576,128]{1,0:T(8,128)(2,1)S(1)}, u32[]{:S(2)}, u32[]{:S(2)}) %collective-permute-start.23) | collective-permute-done | bytes 147488 | tf_op jit(solution)/shard_map/ppermute | solution.py:31
  86.5 0.7 shard_map.109
  87.2 5.0 %collective-permute-start.24 = (bf16[144,128]{1,0:T(8,128)(2,1)S(1)}, bf16[144,128]{1,0:T(8,128)(2,1)S(1)}, u32[]{:S(2)}, u32[]{:S(2)}) collective-permute-start(bf16[144,128]{1,0:T(8,128)(2,1)S(1)} %get-tuple-element.86), channel_id=1, source_target_pairs={{0,2},{1,3},{2,0},{3,1},{4,6},{5,7},{6,4},{7,5},{8,10},{9,11},{10,... | collective-permute-start | bytes 110600 | tf_op jit(solution)/shard_map/ppermute | solution.py:31
  92.2 4.8 %collective-permute-start.25 = (bf16[144,128]{1,0:T(8,128)(2,1)S(1)}, bf16[144,128]{1,0:T(8,128)(2,1)S(1)}, u32[]{:S(2)}, u32[]{:S(2)}) collective-permute-start(bf16[144,128]{1,0:T(8,128)(2,1)S(1)} %get-tuple-element.88), channel_id=1, source_target_pairs={{0,4},{1,5},{2,6},{3,7},{4,0},{5,1},{6,2},{7,3},{8,12},{9,13},{10,... | collective-permute-start | bytes 110600 | tf_op jit(solution)/shard_map/ppermute | solution.py:31
  97.0 1.7 %shard_map.108 = (bf16[128,2048]{1,0:T(8,128)(2,1)}, bf16[128,1024]{1,0:T(8,128)(2,1)}, bf16[128,1024]{1,0:T(8,128)(2,1)}) custom-call(s32[3]{0:T(128)S(1)} %pad_add_fusion.where, bf16[2,128,384]{2,1,0:T(8,128)(2,1)S(1)} %get-tuple-element.73.refs_0_, bf16[2,128,384]{2,1,0:T(8,128)(2,1)S(1)} %collective-permute-done.4.refs_1_, ...), custom_call_target="tpu_custom_call" | custom-call | tf_op jit(solution)/shard_map/pallas_call | solution.py:378
  98.7 1.4 %collective-permute-done.25.refs_2_ = bf16[144,128]{1,0:T(8,128)(2,1)S(1)} collective-permute-done((bf16[144,128]{1,0:T(8,128)(2,1)S(1)}, bf16[144,128]{1,0:T(8,128)(2,1)S(1)}, u32[]{:S(2)}, u32[]{:S(2)}) %collective-permute-start.25) | collective-permute-done | bytes 36896 | tf_op jit(solution)/shard_map/ppermute | solution.py:31
  100.1 3.0 %collective-permute-done.26.refs_3_ = bf16[144,128]{1,0:T(8,128)(2,1)S(1)} collective-permute-done((bf16[144,128]{1,0:T(8,128)(2,1)S(1)}, bf16[144,128]{1,0:T(8,128)(2,1)S(1)}, u32[]{:S(2)}, u32[]{:S(2)}) %collective-permute-start.26) | collective-permute-done | bytes 36896 | tf_op jit(solution)/shard_map/ppermute | solution.py:31
  103.1 0.7 shard_map.110
  (21 shorter events, 0.9 us)
Async XLA Ops:
  3.8 29.6 %all-to-all-start = ((bf16[8,144,768]{2,1,0:T(8,128)(2,1)}), bf16[8,144,768]{2,1,0:T(8,128)(2,1)S(1)}, u32[]{:S(2)}, u32[]{:S(2)}) async-start(bf16[8,144,768]{2,1,0:T(8,128)(2,1)} %shard_map.102), calls=%async_computation | async-start | bytes 3538944 | tf_op jit(solution)/shard_map/all_to_all | solution.py:317
  9.8 23.6 %copy-start = (s32[1,8]{1,0:T(1,128)S(1)}, s32[1,8]{1,0:T(1,128)}, u32[]{:S(2)}) copy-start(s32[1,8]{1,0:T(1,128)} %lengths.1) | copy-start | bytes 100
  11.8 10.2 %collective-permute-start = (bf16[128,1152]{1,0:T(8,128)(2,1)}, bf16[128,1152]{1,0:T(8,128)(2,1)S(1)}, u32[]{:S(2)}, u32[]{:S(2)}) collective-permute-start(bf16[128,1152]{1,0:T(8,128)(2,1)} %get-tuple-element.51), channel_id=1, source_target_pairs={{0,8},{1,9},{2,10},{3,11},{4,12},{5,13},{6,14},{7,15},{8,0},{9,1},... | collective-permute-start | bytes 884744 | tf_op jit(solution)/shard_map/ppermute | solution.py:31
  13.3 15.5 %collective-permute-start.1 = (bf16[128,1152]{1,0:T(8,128)(2,1)S(1)}, bf16[128,1152]{1,0:T(8,128)(2,1)S(1)}, u32[]{:S(2)}, u32[]{:S(2)}) collective-permute-start(bf16[128,1152]{1,0:T(8,128)(2,1)S(1)} %get-tuple-element.52), channel_id=1, source_target_pairs={{0,16},{1,17},{2,18},{3,19},{4,20},{5,21},{6,22},{7,23},{8,24},{9,... | collective-permute-start | bytes 884744 | tf_op jit(solution)/shard_map/ppermute | solution.py:31
  16.1 15.2 %collective-permute-start.2 = (bf16[128,1152]{1,0:T(8,128)(2,1)S(1)}, bf16[128,1152]{1,0:T(8,128)(2,1)S(1)}, u32[]{:S(2)}, u32[]{:S(2)}) collective-permute-start(bf16[128,1152]{1,0:T(8,128)(2,1)S(1)} %get-tuple-element.53), channel_id=1, source_target_pairs={{0,24},{1,25},{2,26},{3,27},{4,28},{5,29},{6,30},{7,31},{8,16},{9,... | collective-permute-start | bytes 884744 | tf_op jit(solution)/shard_map/ppermute | solution.py:31
  33.1 13.1 %collective-permute-start.3 = (bf16[576,512]{1,0:T(8,128)(2,1)S(1)}, bf16[576,512]{1,0:T(8,128)(2,1)S(1)}, u32[]{:S(2)}, u32[]{:S(2)}) collective-permute-start(bf16[576,512]{1,0:T(8,128)(2,1)S(1)} %get-tuple-element.69.refs_0_), channel_id=1, source_target_pairs={{0,128},{1,129},{2,130},{3,131},{4,132},{5,133},{6,134},{7,135},{8... | collective-permute-start | bytes 1769480 | tf_op jit(solution)/shard_map/ppermute | solution.py:31
  33.4 21.2 %collective-permute-start.10 = (bf16[576,512]{1,0:T(8,128)(2,1)}, bf16[576,512]{1,0:T(8,128)(2,1)S(1)}, u32[]{:S(2)}, u32[]{:S(2)}) collective-permute-start(bf16[576,512]{1,0:T(8,128)(2,1)} %get-tuple-element.70), channel_id=1, source_target_pairs={{0,1},{1,0},{2,3},{3,2},{4,5},{5,4},{6,7},{7,6},{8,9},{9,8},{10,11... | collective-permute-start | bytes 1769480 | tf_op jit(solution)/shard_map/ppermute | solution.py:31
  41.1 7.6 %collective-permute-start.4 = (bf16[2,128,384]{2,1,0:T(8,128)(2,1)S(1)}, bf16[2,128,384]{2,1,0:T(8,128)(2,1)S(1)}, u32[]{:S(2)}, u32[]{:S(2)}) collective-permute-start(bf16[2,128,384]{2,1,0:T(8,128)(2,1)S(1)} %get-tuple-element.55), channel_id=1, source_target_pairs={{0,32},{1,33},{2,34},{3,35},{4,36},{5,37},{6,38},{7,39},{8,40},{9,... | collective-permute-start | bytes 589832 | tf_op jit(solution)/shard_map/ppermute | solution.py:31
  42.9 5.5 %collective-permute-start.7 = (bf16[2,128,128]{2,1,0:T(8,128)(2,1)S(1)}, bf16[2,128,128]{2,1,0:T(8,128)(2,1)S(1)}, u32[]{:S(2)}, u32[]{:S(2)}) collective-permute-start(bf16[2,128,128]{2,1,0:T(8,128)(2,1)S(1)} %get-tuple-element.61), channel_id=1, source_target_pairs={{0,96},{1,97},{2,98},{3,99},{4,100},{5,101},{6,102},{7,103},{8,104... | collective-permute-start | bytes 196616 | tf_op jit(solution)/shard_map/ppermute | solution.py:31
  45.0 7.3 %collective-permute-start.6 = (bf16[2,128,128]{2,1,0:T(8,128)(2,1)S(1)}, bf16[2,128,128]{2,1,0:T(8,128)(2,1)S(1)}, u32[]{:S(2)}, u32[]{:S(2)}) collective-permute-start(bf16[2,128,128]{2,1,0:T(8,128)(2,1)S(1)} %get-tuple-element.59), channel_id=1, source_target_pairs={{0,64},{1,65},{2,66},{3,67},{4,68},{5,69},{6,70},{7,71},{8,72},{9,... | collective-permute-start | bytes 196616 | tf_op jit(solution)/shard_map/ppermute | solution.py:31
  46.2 6.1 %collective-permute-start.5 = (bf16[2,128,128]{2,1,0:T(8,128)(2,1)S(1)}, bf16[2,128,128]{2,1,0:T(8,128)(2,1)S(1)}, u32[]{:S(2)}, u32[]{:S(2)}) collective-permute-start(bf16[2,128,128]{2,1,0:T(8,128)(2,1)S(1)} %get-tuple-element.57), channel_id=1, source_target_pairs={{0,32},{1,33},{2,34},{3,35},{4,36},{5,37},{6,38},{7,39},{8,40},{9,... | collective-permute-start | bytes 196616 | tf_op jit(solution)/shard_map/ppermute | solution.py:31
  53.0 7.3 %collective-permute-start.8 = (bf16[2,128,384]{2,1,0:T(8,128)(2,1)S(1)}, bf16[2,128,384]{2,1,0:T(8,128)(2,1)S(1)}, u32[]{:S(2)}, u32[]{:S(2)}) collective-permute-start(bf16[2,128,384]{2,1,0:T(8,128)(2,1)S(1)} %get-tuple-element.66), channel_id=1, source_target_pairs={{0,64},{1,65},{2,66},{3,67},{4,68},{5,69},{6,70},{7,71},{8,72},{9,... | collective-permute-start | bytes 589832 | tf_op jit(solution)/shard_map/ppermute | solution.py:31
  54.6 15.6 %collective-permute-start.11 = (bf16[576,512]{1,0:T(8,128)(2,1)S(1)}, bf16[576,512]{1,0:T(8,128)(2,1)S(1)}, u32[]{:S(2)}, u32[]{:S(2)}) collective-permute-start(bf16[576,512]{1,0:T(8,128)(2,1)S(1)} %collective-permute-done.10.refs_1_), channel_id=1, source_target_pairs={{0,128},{1,129},{2,130},{3,131},{4,132},{5,133},{6,134},{7,135},{8... | collective-permute-start | bytes 1769480 | tf_op jit(solution)/shard_map/ppermute | solution.py:31
  56.1 13.5 %collective-permute-start.14 = (bf16[2,128,512]{2,1,0:T(8,128)(2,1)S(1)}, bf16[2,128,512]{2,1,0:T(8,128)(2,1)S(1)}, u32[]{:S(2)}, u32[]{:S(2)}) collective-permute-start(bf16[2,128,512]{2,1,0:T(8,128)(2,1)S(1)} %get-tuple-element.63.refs_4_), channel_id=1, source_target_pairs={{0,24},{1,25},{2,26},{3,27},{4,28},{5,29},{6,30},{7,31},{8,16},{9,... | collective-permute-start | bytes 786440 | tf_op jit(solution)/shard_map/ppermute | solution.py:31
  56.8 12.7 %collective-permute-start.13 = (bf16[2,128,512]{2,1,0:T(8,128)(2,1)S(1)}, bf16[2,128,512]{2,1,0:T(8,128)(2,1)S(1)}, u32[]{:S(2)}, u32[]{:S(2)}) collective-permute-start(bf16[2,128,512]{2,1,0:T(8,128)(2,1)S(1)} %get-tuple-element.63.refs_4_), channel_id=1, source_target_pairs={{0,16},{1,17},{2,18},{3,19},{4,20},{5,21},{6,22},{7,23},{8,24},{9,... | collective-permute-start | bytes 786440 | tf_op jit(solution)/shard_map/ppermute | solution.py:31
  57.4 12.7 %collective-permute-start.12 = (bf16[2,128,512]{2,1,0:T(8,128)(2,1)S(1)}, bf16[2,128,512]{2,1,0:T(8,128)(2,1)S(1)}, u32[]{:S(2)}, u32[]{:S(2)}) collective-permute-start(bf16[2,128,512]{2,1,0:T(8,128)(2,1)S(1)} %get-tuple-element.63.refs_4_), channel_id=1, source_target_pairs={{0,8},{1,9},{2,10},{3,11},{4,12},{5,13},{6,14},{7,15},{8,0},{9,1},... | collective-permute-start | bytes 786440 | tf_op jit(solution)/shard_map/ppermute | solution.py:31
  60.2 6.9 %collective-permute-start.9 = (bf16[2,128,384]{2,1,0:T(8,128)(2,1)S(1)}, bf16[2,128,384]{2,1,0:T(8,128)(2,1)S(1)}, u32[]{:S(2)}, u32[]{:S(2)}) collective-permute-start(bf16[2,128,384]{2,1,0:T(8,128)(2,1)S(1)} %get-tuple-element.68), channel_id=1, source_target_pairs={{0,96},{1,97},{2,98},{3,99},{4,100},{5,101},{6,102},{7,103},{8,104... | collective-permute-start | bytes 589832 | tf_op jit(solution)/shard_map/ppermute | solution.py:31
  67.1 3.1 %collective-permute-start.15 = (bf16[2,128,512]{2,1,0:T(8,128)(2,1)S(1)}, bf16[2,128,512]{2,1,0:T(8,128)(2,1)S(1)}, u32[]{:S(2)}, u32[]{:S(2)}) collective-permute-start(bf16[2,128,512]{2,1,0:T(8,128)(2,1)S(1)} %get-tuple-element.63.refs_4_), channel_id=1, source_target_pairs={{0,1},{1,0},{2,3},{3,2},{4,5},{5,4},{6,7},{7,6},{8,9},{9,8},{10,11... | collective-permute-start | bytes 786440 | tf_op jit(solution)/shard_map/ppermute | solution.py:31
  69.5 1.5 %collective-permute-start.18 = (bf16[2,128,512]{2,1,0:T(8,128)(2,1)S(1)}, bf16[2,128,512]{2,1,0:T(8,128)(2,1)S(1)}, u32[]{:S(2)}, u32[]{:S(2)}) collective-permute-start(bf16[2,128,512]{2,1,0:T(8,128)(2,1)S(1)} %collective-permute-done.14.refs_7_), channel_id=1, source_target_pairs={{0,1},{1,0},{2,3},{3,2},{4,5},{5,4},{6,7},{7,6},{8,9},{9,8},{10,11... | collective-permute-start | bytes 786440 | tf_op jit(solution)/shard_map/ppermute | solution.py:31
  69.5 1.9 %collective-permute-start.17 = (bf16[2,128,512]{2,1,0:T(8,128)(2,1)S(1)}, bf16[2,128,512]{2,1,0:T(8,128)(2,1)S(1)}, u32[]{:S(2)}, u32[]{:S(2)}) collective-permute-start(bf16[2,128,512]{2,1,0:T(8,128)(2,1)S(1)} %collective-permute-done.13.refs_6_), channel_id=1, source_target_pairs={{0,1},{1,0},{2,3},{3,2},{4,5},{5,4},{6,7},{7,6},{8,9},{9,8},{10,11... | collective-permute-start | bytes 786440 | tf_op jit(solution)/shard_map/ppermute | solution.py:31
  70.2 1.7 %collective-permute-start.16 = (bf16[2,128,512]{2,1,0:T(8,128)(2,1)S(1)}, bf16[2,128,512]{2,1,0:T(8,128)(2,1)S(1)}, u32[]{:S(2)}, u32[]{:S(2)}) collective-permute-start(bf16[2,128,512]{2,1,0:T(8,128)(2,1)S(1)} %collective-permute-done.12.refs_5_), channel_id=1, source_target_pairs={{0,1},{1,0},{2,3},{3,2},{4,5},{5,4},{6,7},{7,6},{8,9},{9,8},{10,11... | collective-permute-start | bytes 786440 | tf_op jit(solution)/shard_map/ppermute | solution.py:31
  74.5 22.6 %collective-permute-start.19 = (bf16[4,128,384]{2,1,0:T(8,128)(2,1)S(1)}, bf16[4,128,384]{2,1,0:T(8,128)(2,1)S(1)}, u32[]{:S(2)}, u32[]{:S(2)}) collective-permute-start(bf16[4,128,384]{2,1,0:T(8,128)(2,1)S(1)} %shard_map.107), channel_id=1, source_target_pairs={{0,128},{1,129},{2,130},{3,131},{4,132},{5,133},{6,134},{7,135},{8... | collective-permute-start | bytes 1179656 | tf_op jit(solution)/shard_map/ppermute | solution.py:31
  75.1 6.7 %collective-permute-start.21 = (bf16[576,128]{1,0:T(8,128)(2,1)S(1)}, bf16[576,128]{1,0:T(8,128)(2,1)S(1)}, u32[]{:S(2)}, u32[]{:S(2)}) collective-permute-start(bf16[576,128]{1,0:T(8,128)(2,1)S(1)} %get-tuple-element.82), channel_id=1, source_target_pairs={{0,32},{1,33},{2,34},{3,35},{4,36},{5,37},{6,38},{7,39},{8,40},{9,... | collective-permute-start | bytes 442376 | tf_op jit(solution)/shard_map/ppermute | solution.py:31
  75.7 8.6 %collective-permute-start.22 = (bf16[576,128]{1,0:T(8,128)(2,1)S(1)}, bf16[576,128]{1,0:T(8,128)(2,1)S(1)}, u32[]{:S(2)}, u32[]{:S(2)}) collective-permute-start(bf16[576,128]{1,0:T(8,128)(2,1)S(1)} %get-tuple-element.83), channel_id=1, source_target_pairs={{0,64},{1,65},{2,66},{3,67},{4,68},{5,69},{6,70},{7,71},{8,72},{9,... | collective-permute-start | bytes 442376 | tf_op jit(solution)/shard_map/ppermute | solution.py:31
  77.4 9.1 %collective-permute-start.23 = (bf16[576,128]{1,0:T(8,128)(2,1)S(1)}, bf16[576,128]{1,0:T(8,128)(2,1)S(1)}, u32[]{:S(2)}, u32[]{:S(2)}) collective-permute-start(bf16[576,128]{1,0:T(8,128)(2,1)S(1)} %get-tuple-element.84), channel_id=1, source_target_pairs={{0,96},{1,97},{2,98},{3,99},{4,100},{5,101},{6,102},{7,103},{8,104... | collective-permute-start | bytes 442376 | tf_op jit(solution)/shard_map/ppermute | solution.py:31
  79.8 17.2 %collective-permute-start.20 = (bf16[128,512]{1,0:T(8,128)(2,1)S(1)}, bf16[128,512]{1,0:T(8,128)(2,1)S(1)}, u32[]{:S(2)}, u32[]{:S(2)}) collective-permute-start(bf16[128,512]{1,0:T(8,128)(2,1)S(1)} %get-tuple-element.78), channel_id=1, source_target_pairs={{0,128},{1,129},{2,130},{3,131},{4,132},{5,133},{6,134},{7,135},{8... | collective-permute-start | bytes 393224 | tf_op jit(solution)/shard_map/ppermute | solution.py:31
  87.2 11.5 %collective-permute-start.24 = (bf16[144,128]{1,0:T(8,128)(2,1)S(1)}, bf16[144,128]{1,0:T(8,128)(2,1)S(1)}, u32[]{:S(2)}, u32[]{:S(2)}) collective-permute-start(bf16[144,128]{1,0:T(8,128)(2,1)S(1)} %get-tuple-element.86), channel_id=1, source_target_pairs={{0,2},{1,3},{2,0},{3,1},{4,6},{5,7},{6,4},{7,5},{8,10},{9,11},{10,... | collective-permute-start | bytes 110600 | tf_op jit(solution)/shard_map/ppermute | solution.py:31
  92.2 7.9 %collective-permute-start.25 = (bf16[144,128]{1,0:T(8,128)(2,1)S(1)}, bf16[144,128]{1,0:T(8,128)(2,1)S(1)}, u32[]{:S(2)}, u32[]{:S(2)}) collective-permute-start(bf16[144,128]{1,0:T(8,128)(2,1)S(1)} %get-tuple-element.88), channel_id=1, source_target_pairs={{0,4},{1,5},{2,6},{3,7},{4,0},{5,1},{6,2},{7,3},{8,12},{9,13},{10,... | collective-permute-start | bytes 110600 | tf_op jit(solution)/shard_map/ppermute | solution.py:31
  97.0 6.1 %collective-permute-start.26 = (bf16[144,128]{1,0:T(8,128)(2,1)S(1)}, bf16[144,128]{1,0:T(8,128)(2,1)S(1)}, u32[]{:S(2)}, u32[]{:S(2)}) collective-permute-start(bf16[144,128]{1,0:T(8,128)(2,1)S(1)} %get-tuple-element.89), channel_id=1, source_target_pairs={{0,6},{1,7},{2,4},{3,5},{4,2},{5,3},{6,0},{7,1},{8,14},{9,15},{10,... | collective-permute-start | bytes 110600 | tf_op jit(solution)/shard_map/ppermute | solution.py:31

commit v4 on v3

--- a/solution.py
+++ b/solution.py
@@ -11,6 +11,7 @@
 HEAD = 128
 BLOCKS = 8
 TAIL = 16
+PAIR = 256
 PACKED = 768
 BACK = 384
 CAP = 50.0
@@ -104,8 +105,8 @@
 def attention_kernel(where, lengths, *refs):
     held = refs[0]
     backs = refs[1:5]
-    values = refs[5:9]
-    key_turned, dq, dk, dv = refs[9:]
+    values = refs[5:7]
+    key_turned, dq, dk, dv = refs[7:]
     mine = where[0]
     dk[...] = jnp.zeros_like(dk)
     dv[...] = jnp.zeros_like(dv)
@@ -118,48 +119,61 @@
         key_turned[n] = held[n, 0:ROWS, 512:640].T
 
     def block(b, carry):
-        base = b * ROWS
+        base = b * PAIR
         first = 0
         for end in ends:
             first = jnp.where(base >= end, end, first)
         kb0 = first // ROWS
-        count = b - kb0 + 1
-        lane = lax.broadcasted_iota(jnp.int32, (1, 256), 1)
-        query = base + lane % ROWS
-        begin = jnp.zeros((1, 256), jnp.int32)
+        count = 2 * b + 2 - kb0
+        lane = lax.broadcasted_iota(jnp.int32, (1, 2 * PAIR), 1)
+        query = base + lane % PAIR
+        begin = jnp.zeros((1, 2 * PAIR), jnp.int32)
         for end in ends:
             begin = jnp.where(query >= end, end, begin)
-        tail = held[b, ROWS:, 0:384].astype(F32)
-        tail = tail[:, 0:128] + tail[:, 128:256] + tail[:, 256:384]
-        head = lax.broadcasted_iota(jnp.int32, (TAIL, 128), 0)
+        head = lax.broadcasted_iota(jnp.int32, (TAIL, ROWS), 0)
+        tails = []
+        for n in range(2):
+            tail = held[2 * b + n, ROWS:, 0:384].astype(F32)
+            tails.append(tail[:, 0:128] + tail[:, 128:256] + tail[:, 256:384])
         delta = jnp.concatenate(
             [
                 jnp.sum(jnp.where(head == 2 * mine + s, tail, 0.0), axis=0, keepdims=True)
                 for s in range(2)
+                for tail in tails
             ],
             axis=1,
         )
-        queries = jnp.concatenate([held[b, 0:ROWS, 0:128], held[b, 0:ROWS, 128:256]], axis=0)
-        grads = jnp.concatenate([held[b, 0:ROWS, 256:384], held[b, 0:ROWS, 384:512]], axis=0)
-        sub = lax.broadcasted_iota(jnp.int32, (ROWS, 256), 0)
+
+        def stacked(at):
+            return jnp.concatenate(
+                [
+                    held[2 * b + n, 0:ROWS, at + s * 128 : at + s * 128 + 128]
+                    for s in range(2)
+                    for n in range(2)
+                ],
+                axis=0,
+            )
+
+        queries, grads = stacked(0), stacked(256)
+        sub = lax.broadcasted_iota(jnp.int32, (ROWS, 2 * PAIR), 0)
 
         def window(number):
             powers, tanhs = [], []
-            sums = jnp.zeros((1, 256), F32)
+            sums = jnp.zeros((1, 2 * PAIR), F32)
             for n in range(number):
                 kb = kb0 + n
                 raw = nt(held[kb, 0:ROWS, 512:640], queries)
                 tanh = jnp.tanh(raw * (SCALE / CAP))
                 key = sub + kb * ROWS
                 live = key >= begin
-                if n == number - 1:
+                if n >= number - 2:
                     live = live & (key <= query)
                 power = jnp.where(live, jnp.exp(CAP * tanh), 0.0)
                 sums = sums + jnp.sum(power, axis=0, keepdims=True)
                 powers.append(power)
                 tanhs.append(tanh)
             inverse = 1.0 / sums
-            turned = jnp.zeros((HEAD, 256), F32)
+            turned = jnp.zeros((HEAD, 2 * PAIR), F32)
             for n in range(number):
                 kb = kb0 + n
                 prob = powers[n] * inverse
@@ -169,11 +183,13 @@
                 dv[kb] += nn(prob.astype(BF), grads)
                 dk[kb] += nn(dscore, queries)
                 turned = turned + nn(key_turned[kb], dscore)
-            straight = turned.T
-            dq[b, :, 0:128] = straight[0:ROWS].astype(BF)
-            dq[b, :, 128:256] = straight[ROWS:].astype(BF)
-
-        for number in range(1, 6):
+            straight = turned.T.astype(BF)
+            for s in range(2):
+                for n in range(2):
+                    at = (s * 2 + n) * ROWS
+                    dq[2 * b + n, :, s * 128 : s * 128 + 128] = straight[at : at + ROWS]
+
+        for number in range(2, 7):
 
             @pl.when(count == number)
             def _():
@@ -181,13 +197,15 @@
 
         return carry
 
-    lax.fori_loop(0, BLOCKS, block, 0)
+    lax.fori_loop(0, BLOCKS // 2, block, 0)
     for k in range(4):
         for half in range(2):
             block = half * 4 + (mine % 4 ^ k)
-            backs[k][half, :, 0:256] = dq[block]
-            backs[k][half, :, 256:384] = dk[block].astype(BF)
-            values[k][half] = dv[block].astype(BF)
+            at = k % 2 * HEAD
+            backs[k][half, :, at : at + 256] = dq[block]
+            backs[k][half, :, at + 256 : at + 384] = dk[block].astype(BF)
+            value = backs[k] if k % 2 else values[k // 2]
+            value[half, :, 0:HEAD] = dv[block].astype(BF)
 
 
 def turn_kernel(where, *refs):
@@ -208,8 +226,8 @@
     half = mine // 4
     for k, piece in enumerate(pieces):
         columns = pl.ds(pl.multiple_of((mine % 4 ^ k) * HEAD, HEAD), HEAD)
-        joined[0, :, columns] = piece[0]
-        joined[1, :, columns] = piece[1]
+        joined[0, :, columns] = piece[0, :, 0:HEAD]
+        joined[1, :, columns] = piece[1, :, 0:HEAD]
     near[...] = joined[half]
     far[...] = joined[1 - half]
 
@@ -231,25 +249,29 @@
 def merge_kernel(where, *refs):
     mine = where[0]
     for k, piece in enumerate(refs[:4]):
-        refs[4][mine % 4 ^ k] = piece[1 - mine // 4]
+        at = k % 2 * HEAD
+        refs[4][mine % 4 ^ k] = piece[1 - mine // 4, :, at : at + BACK]
 
 
 def sum_kernel(where, *refs):
-    total = refs[8]
+    keep, send, total = refs[4:7]
     z_hi = where[2]
     value = refs[0][...].astype(F32)
     for ref in refs[1:4]:
         value = value + ref[...].astype(F32)
     total[...] = value.astype(BF)
-    for k, out in enumerate(refs[4:8]):
-        out[...] = total[pl.ds(pl.multiple_of((z_hi ^ k) * 144, 16), 144)]
-
-
-def last_kernel(*refs):
-    total = refs[0][...].astype(F32)
-    for ref in refs[1:4]:
-        total = total + ref[...].astype(F32)
-    refs[4][...] = total
+    for out, order in ((keep, (0, 3)), (send, (1, 2))):
+        for n, k in enumerate(order):
+            out[n] = total[pl.ds(pl.multiple_of((z_hi ^ k) * 144, 16), 144)]
+
+
+def fold_kernel(keep, landed, own, other):
+    own[...] = keep[0].astype(F32) + landed[0].astype(F32)
+    other[...] = (keep[1].astype(F32) + landed[1].astype(F32)).astype(BF)
+
+
+def last_kernel(own, landed, out):
+    out[...] = own[...] + landed[...].astype(F32)
 
 
 def unpack_kernel(where, *refs):
@@ -261,8 +283,9 @@
         head = mine ^ k
         wide = pl.ds(pl.multiple_of(head * 256, 256), 256)
         thin = pl.ds(pl.multiple_of(head * 128, 128), 128)
-        query_grad[:, wide] = piece[half, :, 0:256]
-        key_grad[:, thin] = piece[half, :, 256:384]
+        at = k % 2 * HEAD
+        query_grad[:, wide] = piece[half, :, at : at + 256]
+        key_grad[:, thin] = piece[half, :, at + 256 : at + 384]
         head = (1 - half) * 4 + k
         wide = pl.ds(pl.multiple_of(head * 256, 256), 256)
         thin = pl.ds(pl.multiple_of(head * 128, 128), 128)
@@ -332,7 +355,7 @@
 
     results = call(
         attention_kernel,
-        [shape(2, ROWS, BACK)] * 4 + [shape(2, ROWS, HEAD)] * 4,
+        [shape(2, ROWS, BACK), shape(2, ROWS, 512)] * 2 + [shape(2, ROWS, HEAD)] * 2,
         [SMEM, SMEM, VMEM],
         [
             pltpu.VMEM((BLOCKS, HEAD, ROWS), BF),
@@ -346,8 +369,8 @@
     backs, values = results[:4], results[4:]
 
     across_far = over_ctx(after(far_rows, values[0]), 4)
-    early = over_y(backs[1], 1)
-    pieces = [after(over_y(values[k], k), across_near, early) for k in range(4)]
+    first, third = over_y(backs[1], 1), over_y(backs[3], 3)
+    pieces = [values[0], first, over_y(values[1], 2), third]
     joined, near, far = call(
         join_kernel,
         [shape(2, ROWS, 512), shape(ROWS, 512), shape(ROWS, 512)],
@@ -355,7 +378,8 @@
     )(where, *pieces)
     rights = [over_x(joined, k) for k in range(4)]
     rights = rights + [over_core(right) for right in rights]
-    returned = [early if k == 1 else over_y(after(backs[k], joined), k) for k in range(4)]
+    second = over_y(after(backs[2], joined), 2)
+    returned = [backs[0], first, second, third]
 
     parts = call(
         weight_kernel,
@@ -364,24 +388,27 @@
         [pltpu.VMEM((576, 512), BF)],
         flops=1_300_000_000,
         moved=4_000_000,
-    )(where, after(near_rows, *returned), far_rows, across_near, across_far, *rights)
+    )(where, after(near_rows, second), far_rows, across_near, across_far, *rights)
     crossed = call(merge_kernel, shape(4, ROWS, BACK), [SMEM] + [VMEM] * 4)(
         where, *[after(piece, parts[0]) for piece in returned]
     )
     crossed = over_ctx(crossed, 4)
     far = over_ctx(far, 4)
     reduced = [over_y(parts[k], k) for k in range(4)]
-    blocks = call(
-        sum_kernel, [shape(144, HEAD)] * 4, [SMEM] + [VMEM] * 4, [pltpu.VMEM((576, HEAD), BF)]
+    keep, send = call(
+        sum_kernel, [shape(2, 144, HEAD)] * 2, [SMEM] + [VMEM] * 4, [pltpu.VMEM((576, HEAD), BF)]
     )(where, *reduced)
-    landed = [over_z(blocks[k], k) for k in range(4)]
+    own, other = call(
+        fold_kernel, [shape(144, HEAD, dtype=F32), shape(144, HEAD)], [VMEM] * 2
+    )(keep, over_z(send, 1))
+    landed = over_z(other, 3)
     query_grad, key_grad, value_grad = call(
         unpack_kernel,
         [shape(ROWS, 2048), shape(ROWS, 1024), shape(ROWS, 1024)],
         [SMEM] + [VMEM] * 7,
     )(where, *returned, crossed, near, far)
-    landed[1] = after(landed[1], query_grad)
-    weight_grad = call(last_kernel, shape(144, HEAD, dtype=F32), [VMEM] * 4)(*landed)
+    own = after(own, query_grad)
+    weight_grad = call(last_kernel, shape(144, HEAD, dtype=F32), [VMEM] * 2)(own, landed)
     return query_grad[None], key_grad[None], value_grad[None], weight_grad
 
 

time: 104 us -> 101 us (0.971); the launches traced: 104 us -> 102 us
  local copies, waits for them, and re-layouts: 2.05 us -> 0.94 us
    dynamic_slice x1, local copies, waits for them, and re-layouts: 2.05 us -> 0.93 us  [body(): piece = lax.dynamic_slice(inputs, (0, (x ^ k) * 1152), (ROWS, 1152))]
    pallas_call x3 -> x4, Pallas kernels: 9.03 us -> 8.6 us  [the longest x1 7.28 us: body(): call(attention_kernel, [shape(2, ROWS, BACK), shape(2, ROWS, 512)] * 2 +...]
    ppermute x27 -> x24, waiting for transfers between devices: 39.3 us -> 39 us  [spread(): return lax.ppermute(block, ('ctx', 'dp'), route)]
    ppermute x27 -> x24, starting transfers between devices: 36.7 us -> 36.6 us  [spread(): return lax.ppermute(block, ('ctx', 'dp'), route)]
  transfers between devices with their start and end apart: 28 -> 25, of which waited for: 19 -> 16; matrix products, arithmetic and copies ran while one was open for 2% -> 1% of each run, Pallas kernels for 12% -> 12%
where the time goes in v4:
time: 101 us; the launch traced here: 102 us
  starting transfers between devices  42.6 us (42%)
  waiting for transfers between devices  39.1 us (39%)
  Pallas kernels  18.6 us (18%)
    ppermute x24, waiting for transfers between devices, spread(): return lax.ppermute(block, ('ctx', 'dp'), route)  39 us
    ppermute x24, starting transfers between devices, spread(): return lax.ppermute(block, ('ctx', 'dp'), route)  36.6 us
    pallas_call x1, Pallas kernels, body(): call(attention_kernel, [shape(2, ROWS, BACK), shape(2, ROWS, 512)] * 2 +...  7.28 us
    all_to_all x1, starting transfers between devices, body(): arrived = lax.all_to_all(packed, 'ctx', 0, 0, tiled=True)  6.07 us
    pallas_call x1, Pallas kernels, body(): call(pack_kernel, shape(BLOCKS, ROWS + TAIL, PACKED), [ANY] * 5, [pltpu.V...  3.21 us
    pallas_call x1, Pallas kernels, body(): call(weight_kernel, [shape(576, HEAD)] * 4, [SMEM] + [VMEM] * 12, [pltpu....  2.03 us
  transfers between devices with their start and end apart: 25, of which 16 were waited for; matrix products, arithmetic and copies ran while one was open for 1% of the time, Pallas kernels for 12%

profile of v4, /device:TPU:32, one launch (start us, length us, event | category | flops | bytes accessed | tf_op | source)
XLA Modules:
  0.0 102.0 jit_solution(8125978888547545120)
XLA Ops:
  0.6 3.2 %shard_map.102 = bf16[8,144,768]{2,1,0:T(8,128)(2,1)} custom-call(bf16[128,2048]{1,0:T(8,128)(2,1)} %bitcast.19, bf16[128,1024]{1,0:T(8,128)(2,1)} %bitcast.22, bf16[128,1024]{1,0:T(8,128)(2,1)} %bitcast.23, bf16[128,2048]{1,0:T(8,128)(2,1)} %bitcast.20, bf16[128,2048]{1,0:T(8,128)(2,1)} %bitcast.21), custom_call_target="tpu_custom_call" | custom-call | tf_op jit(solution)/shard_map/pallas_call | solution.py:325
  3.9 6.1 %all-to-all-start = ((bf16[8,144,768]{2,1,0:T(8,128)(2,1)}), bf16[8,144,768]{2,1,0:T(8,128)(2,1)S(1)}, u32[]{:S(2)}, u32[]{:S(2)}) async-start(bf16[8,144,768]{2,1,0:T(8,128)(2,1)} %shard_map.102), calls=%async_computation | async-start | bytes 3538944 | tf_op jit(solution)/shard_map/all_to_all | solution.py:340
  9.9 0.9 dynamic-slice_bitcast_fusion
  10.9 1.5 %collective-permute-start.4 = (bf16[128,1152]{1,0:T(8,128)(2,1)}, bf16[128,1152]{1,0:T(8,128)(2,1)S(1)}, u32[]{:S(2)}, u32[]{:S(2)}) collective-permute-start(bf16[128,1152]{1,0:T(8,128)(2,1)} %get-tuple-element.49), channel_id=1, source_target_pairs={{0,8},{1,9},{2,10},{3,11},{4,12},{5,13},{6,14},{7,15},{8,0},{9,1},... | collective-permute-start | bytes 884744 | tf_op jit(solution)/shard_map/ppermute | solution.py:32
  12.4 2.7 %collective-permute-start.5 = (bf16[128,1152]{1,0:T(8,128)(2,1)}, bf16[128,1152]{1,0:T(8,128)(2,1)S(1)}, u32[]{:S(2)}, u32[]{:S(2)}) collective-permute-start(bf16[128,1152]{1,0:T(8,128)(2,1)} %get-tuple-element.50), channel_id=1, source_target_pairs={{0,16},{1,17},{2,18},{3,19},{4,20},{5,21},{6,22},{7,23},{8,24},{9,... | collective-permute-start | bytes 884744 | tf_op jit(solution)/shard_map/ppermute | solution.py:32
  15.1 0.5 collective-permute-start.6
  15.6 0.1 pad_add_fusion.where
  15.7 5.4 %collective-permute-done.4.refs_1_ = bf16[128,1152]{1,0:T(8,128)(2,1)S(1)} collective-permute-done((bf16[128,1152]{1,0:T(8,128)(2,1)}, bf16[128,1152]{1,0:T(8,128)(2,1)S(1)}, u32[]{:S(2)}, u32[]{:S(2)}) %collective-permute-start.4) | collective-permute-done | bytes 294944 | tf_op jit(solution)/shard_map/ppermute | solution.py:32
  21.0 6.9 %collective-permute-done.5.refs_2_ = bf16[128,1152]{1,0:T(8,128)(2,1)S(1)} collective-permute-done((bf16[128,1152]{1,0:T(8,128)(2,1)}, bf16[128,1152]{1,0:T(8,128)(2,1)S(1)}, u32[]{:S(2)}, u32[]{:S(2)}) %collective-permute-start.5) | collective-permute-done | bytes 294944 | tf_op jit(solution)/shard_map/ppermute | solution.py:32
  27.9 2.6 %collective-permute-done.6.refs_3_ = bf16[128,1152]{1,0:T(8,128)(2,1)S(1)} collective-permute-done((bf16[128,1152]{1,0:T(8,128)(2,1)}, bf16[128,1152]{1,0:T(8,128)(2,1)S(1)}, u32[]{:S(2)}, u32[]{:S(2)}) %collective-permute-start.6) | collective-permute-done | bytes 294944 | tf_op jit(solution)/shard_map/ppermute | solution.py:32
  30.5 1.9 %shard_map.105 = (bf16[576,512]{1,0:T(8,128)(2,1)S(1)}, bf16[576,512]{1,0:T(8,128)(2,1)}) custom-call(s32[3]{0:T(128)S(1)} %pad_add_fusion.where, bf16[128,1152]{1,0:T(8,128)(2,1)S(1)} %get-tuple-element.48.refs_0_, bf16[128,1152]{1,0:T(8,128)(2,1)S(1)} %collective-permute-done.4.refs_1_, bf16[128,1152]{1,0:T(8,128)(2,1)S(1)} %collective-permute-done.5.refs_2_, ...), custom_call_target="tpu_custom_call" | custom-call | tf_op jit(solution)/shard_map/pallas_call | solution.py:347
  32.4 0.3 collective-permute-start.8
  32.7 7.3 %shard_map.103 = (bf16[2,128,384]{2,1,0:T(8,128)(2,1)S(1)}, bf16[2,128,512]{2,1,0:T(8,128)(2,1)S(1)}, bf16[2,128,384]{2,1,0:T(8,128)(2,1)S(1)}, bf16[2,128,512]{...) custom-call(s32[3]{0:T(128)S(1)} %pad_add_fusion.where, s32[1,8]{1,0:T(1,128)S(1)} %copy-done, ...), custom_call_target="tpu_custom_call" | custom-call | flops 4000000000 | bytes 4000000 | tf_op jit(solution)/shard_map/pallas_call | solution.py:356
  40.0 1.8 %collective-permute-start = (bf16[2,128,512]{2,1,0:T(8,128)(2,1)S(1)}, bf16[2,128,512]{2,1,0:T(8,128)(2,1)S(1)}, u32[]{:S(2)}, u32[]{:S(2)}) collective-permute-start(bf16[2,128,512]{2,1,0:T(8,128)(2,1)S(1)} %get-tuple-element.41), channel_id=1, source_target_pairs={{0,32},{1,33},{2,34},{3,35},{4,36},{5,37},{6,38},{7,39},{8,40},{9,... | collective-permute-start | bytes 786440 | tf_op jit(solution)/shard_map/ppermute | solution.py:32
  41.8 2.1 %collective-permute-start.2 = (bf16[2,128,512]{2,1,0:T(8,128)(2,1)S(1)}, bf16[2,128,512]{2,1,0:T(8,128)(2,1)S(1)}, u32[]{:S(2)}, u32[]{:S(2)}) collective-permute-start(bf16[2,128,512]{2,1,0:T(8,128)(2,1)S(1)} %get-tuple-element.45), channel_id=1, source_target_pairs={{0,96},{1,97},{2,98},{3,99},{4,100},{5,101},{6,102},{7,103},{8,104... | collective-permute-start | bytes 786440 | tf_op jit(solution)/shard_map/ppermute | solution.py:32
  43.9 0.6 collective-permute-start.1
  44.4 1.5 %collective-permute-start.9 = (bf16[576,512]{1,0:T(8,128)(2,1)S(1)}, bf16[576,512]{1,0:T(8,128)(2,1)S(1)}, u32[]{:S(2)}, u32[]{:S(2)}) collective-permute-start(bf16[576,512]{1,0:T(8,128)(2,1)S(1)} %collective-permute-done.7.refs_1_), channel_id=1, source_target_pairs={{0,128},{1,129},{2,130},{3,131},{4,132},{5,133},{6,134},{7,135},{8... | collective-permute-start | bytes 1769480 | tf_op jit(solution)/shard_map/ppermute | solution.py:32
  45.9 5.2 %collective-permute-done.1.refs_2_ = bf16[2,128,128]{2,1,0:T(8,128)(2,1)S(1)} collective-permute-done((bf16[2,128,128]{2,1,0:T(8,128)(2,1)S(1)}, bf16[2,128,128]{2,1,0:T(8,128)(2,1)S(1)}, u32[]{:S(2)}, u32[]{:S(2)}) %collective-permute-start.1) | collective-permute-done | bytes 65568 | tf_op jit(solution)/shard_map/ppermute | solution.py:32
  51.1 0.2 collective-permute-done.2.refs_3_
  51.3 0.6 shard_map.104
  51.9 1.3 %collective-permute-start.12 = (bf16[2,128,512]{2,1,0:T(8,128)(2,1)S(1)}, bf16[2,128,512]{2,1,0:T(8,128)(2,1)S(1)}, u32[]{:S(2)}, u32[]{:S(2)}) collective-permute-start(bf16[2,128,512]{2,1,0:T(8,128)(2,1)S(1)} %get-tuple-element.46.refs_4_), channel_id=1, source_target_pairs={{0,24},{1,25},{2,26},{3,27},{4,28},{5,29},{6,30},{7,31},{8,16},{9,... | collective-permute-start | bytes 786440 | tf_op jit(solution)/shard_map/ppermute | solution.py:32
  53.2 1.0 collective-permute-start.11
  54.2 1.9 %collective-permute-start.10 = (bf16[2,128,512]{2,1,0:T(8,128)(2,1)S(1)}, bf16[2,128,512]{2,1,0:T(8,128)(2,1)S(1)}, u32[]{:S(2)}, u32[]{:S(2)}) collective-permute-start(bf16[2,128,512]{2,1,0:T(8,128)(2,1)S(1)} %get-tuple-element.46.refs_4_), channel_id=1, source_target_pairs={{0,8},{1,9},{2,10},{3,11},{4,12},{5,13},{6,14},{7,15},{8,0},{9,1},... | collective-permute-start | bytes 786440 | tf_op jit(solution)/shard_map/ppermute | solution.py:32
  56.1 1.5 %collective-permute-start.3 = (bf16[2,128,384]{2,1,0:T(8,128)(2,1)S(1)}, bf16[2,128,384]{2,1,0:T(8,128)(2,1)S(1)}, u32[]{:S(2)}, u32[]{:S(2)}) collective-permute-start(bf16[2,128,384]{2,1,0:T(8,128)(2,1)S(1)} %get-tuple-element.47), channel_id=1, source_target_pairs={{0,64},{1,65},{2,66},{3,67},{4,68},{5,69},{6,70},{7,71},{8,72},{9,... | collective-permute-start | bytes 589832 | tf_op jit(solution)/shard_map/ppermute | solution.py:32
  57.6 5.7 %collective-permute-done.3.refs_2_ = bf16[2,128,384]{2,1,0:T(8,128)(2,1)S(1)} collective-permute-done((bf16[2,128,384]{2,1,0:T(8,128)(2,1)S(1)}, bf16[2,128,384]{2,1,0:T(8,128)(2,1)S(1)}, u32[]{:S(2)}, u32[]{:S(2)}) %collective-permute-start.3) | collective-permute-done | bytes 196640 | tf_op jit(solution)/shard_map/ppermute | solution.py:32
  63.3 1.3 %collective-permute-done.12.refs_7_ = bf16[2,128,512]{2,1,0:T(8,128)(2,1)S(1)} collective-permute-done((bf16[2,128,512]{2,1,0:T(8,128)(2,1)S(1)}, bf16[2,128,512]{2,1,0:T(8,128)(2,1)S(1)}, u32[]{:S(2)}, u32[]{:S(2)}) %collective-permute-start.12) | collective-permute-done | bytes 262176 | tf_op jit(solution)/shard_map/ppermute | solution.py:32
  64.6 0.5 collective-permute-start.15
  65.1 0.1 collective-permute-done.10.refs_5_
  65.2 0.9 collective-permute-done.16.refs_11_
  66.1 0.4 collective-permute-done.15.refs_10_
  66.5 0.4 collective-permute-done.14.refs_9_
  66.8 2.0 %shard_map.106 = (bf16[576,128]{1,0:T(8,128)(2,1)S(1)}, bf16[576,128]{1,0:T(8,128)(2,1)S(1)}, bf16[576,128]{1,0:T(8,128)(2,1)S(1)}, bf16[576,128]{1,0:T(8,128)(2,1)S(1)}) custom-call(s32[3]{0:T(128)S(1)} %pad_add_fusion.where, bf16[576,512]{1,0:T(8,128)(2,1)S(1)} %get-tuple-element.53.refs_0_, bf16[576,512]{1,0:T(8,128)(2,1)S(1)} %collective-permute-done.7.refs_1_, ...), custom_call_target="tpu_custom_call" | custom-call | flops 1300000000 | bytes 4000000 | tf_op jit(solution)/shard_map/pallas_call | solution.py:384
  68.9 0.6 shard_map.107
  69.5 1.5 %collective-permute-start.17 = (bf16[4,128,384]{2,1,0:T(8,128)(2,1)S(1)}, bf16[4,128,384]{2,1,0:T(8,128)(2,1)S(1)}, u32[]{:S(2)}, u32[]{:S(2)}) collective-permute-start(bf16[4,128,384]{2,1,0:T(8,128)(2,1)S(1)} %shard_map.107), channel_id=1, source_target_pairs={{0,128},{1,129},{2,130},{3,131},{4,132},{5,133},{6,134},{7,135},{8... | collective-permute-start | bytes 1179656 | tf_op jit(solution)/shard_map/ppermute | solution.py:32
  71.0 0.3 collective-permute-start.19
  71.2 3.1 %collective-permute-start.20 = (bf16[576,128]{1,0:T(8,128)(2,1)S(1)}, bf16[576,128]{1,0:T(8,128)(2,1)S(1)}, u32[]{:S(2)}, u32[]{:S(2)}) collective-permute-start(bf16[576,128]{1,0:T(8,128)(2,1)S(1)} %get-tuple-element.67), channel_id=1, source_target_pairs={{0,64},{1,65},{2,66},{3,67},{4,68},{5,69},{6,70},{7,71},{8,72},{9,... | collective-permute-start | bytes 442376 | tf_op jit(solution)/shard_map/ppermute | solution.py:32
  74.4 1.3 %collective-permute-start.21 = (bf16[576,128]{1,0:T(8,128)(2,1)S(1)}, bf16[576,128]{1,0:T(8,128)(2,1)S(1)}, u32[]{:S(2)}, u32[]{:S(2)}) collective-permute-start(bf16[576,128]{1,0:T(8,128)(2,1)S(1)} %get-tuple-element.68), channel_id=1, source_target_pairs={{0,96},{1,97},{2,98},{3,99},{4,100},{5,101},{6,102},{7,103},{8,104... | collective-permute-start | bytes 442376 | tf_op jit(solution)/shard_map/ppermute | solution.py:32
  75.7 0.6 collective-permute-start.18
  76.3 1.4 %collective-permute-done.19.refs_1_ = bf16[576,128]{1,0:T(8,128)(2,1)S(1)} collective-permute-done((bf16[576,128]{1,0:T(8,128)(2,1)S(1)}, bf16[576,128]{1,0:T(8,128)(2,1)S(1)}, u32[]{:S(2)}, u32[]{:S(2)}) %collective-permute-start.19) | collective-permute-done | bytes 147488 | tf_op jit(solution)/shard_map/ppermute | solution.py:32
  77.7 3.5 %collective-permute-done.20.refs_2_ = bf16[576,128]{1,0:T(8,128)(2,1)S(1)} collective-permute-done((bf16[576,128]{1,0:T(8,128)(2,1)S(1)}, bf16[576,128]{1,0:T(8,128)(2,1)S(1)}, u32[]{:S(2)}, u32[]{:S(2)}) %collective-permute-start.20) | collective-permute-done | bytes 147488 | tf_op jit(solution)/shard_map/ppermute | solution.py:32
  81.2 2.3 %collective-permute-done.21.refs_3_ = bf16[576,128]{1,0:T(8,128)(2,1)S(1)} collective-permute-done((bf16[576,128]{1,0:T(8,128)(2,1)S(1)}, bf16[576,128]{1,0:T(8,128)(2,1)S(1)}, u32[]{:S(2)}, u32[]{:S(2)}) %collective-permute-start.21) | collective-permute-done | bytes 147488 | tf_op jit(solution)/shard_map/ppermute | solution.py:32
  83.5 0.7 shard_map.109
  84.1 6.0 %collective-permute-start.22 = (bf16[2,144,128]{2,1,0:T(8,128)(2,1)S(1)}, bf16[2,144,128]{2,1,0:T(8,128)(2,1)S(1)}, u32[]{:S(2)}, u32[]{:S(2)}) collective-permute-start(bf16[2,144,128]{2,1,0:T(8,128)(2,1)S(1)} %get-tuple-element.70), channel_id=1, source_target_pairs={{0,2},{1,3},{2,0},{3,1},{4,6},{5,7},{6,4},{7,5},{8,10},{9,11},{10,... | collective-permute-start | bytes 221192 | tf_op jit(solution)/shard_map/ppermute | solution.py:32
  90.2 2.7 %collective-permute-done.22.landed = bf16[2,144,128]{2,1,0:T(8,128)(2,1)S(1)} collective-permute-done((bf16[2,144,128]{2,1,0:T(8,128)(2,1)S(1)}, bf16[2,144,128]{2,1,0:T(8,128)(2,1)S(1)}, u32[]{:S(2)}, u32[]{:S(2)}) %collective-permute-start.22) | collective-permute-done | bytes 73760 | tf_op jit(solution)/shard_map/ppermute | solution.py:32
  92.8 6.6 %collective-permute-start.23 = (bf16[144,128]{1,0:T(8,128)(2,1)S(1)}, bf16[144,128]{1,0:T(8,128)(2,1)S(1)}, u32[]{:S(2)}, u32[]{:S(2)}) collective-permute-start(bf16[144,128]{1,0:T(8,128)(2,1)S(1)} %get-tuple-element.73), channel_id=1, source_target_pairs={{0,6},{1,7},{2,4},{3,5},{4,2},{5,3},{6,0},{7,1},{8,14},{9,15},{10,... | collective-permute-start | bytes 110600 | tf_op jit(solution)/shard_map/ppermute | solution.py:32
  99.4 1.7 %shard_map.108 = (bf16[128,2048]{1,0:T(8,128)(2,1)}, bf16[128,1024]{1,0:T(8,128)(2,1)}, bf16[128,1024]{1,0:T(8,128)(2,1)}) custom-call(s32[3]{0:T(128)S(1)} %pad_add_fusion.where, bf16[2,128,384]{2,1,0:T(8,128)(2,1)S(1)} %get-tuple-element.57.refs_0_, bf16[2,128,512]{2,1,0:T(8,128)(2,1)S(1)} %collective-permute-done.refs_1_, ...), custom_call_target="tpu_custom_call" | custom-call | tf_op jit(solution)/shard_map/pallas_call | solution.py:405
  101.1 0.3 collective-permute-done.23.landed
  101.4 0.6 shard_map.111
  (18 shorter events, 0.1 us)
Async XLA Ops:
  3.9 6.1 %copy-start.1 = (bf16[1,128,4608]{2,1,0:T(8,128)(2,1)S(1)}, bf16[1,128,4608]{2,1,0:T(8,128)(2,1)}, u32[]{:S(2)}) copy-start(bf16[1,128,4608]{2,1,0:T(8,128)(2,1)} %param.12) | copy-start | bytes 3538948
  3.9 28.8 %all-to-all-start = ((bf16[8,144,768]{2,1,0:T(8,128)(2,1)}), bf16[8,144,768]{2,1,0:T(8,128)(2,1)S(1)}, u32[]{:S(2)}, u32[]{:S(2)}) async-start(bf16[8,144,768]{2,1,0:T(8,128)(2,1)} %shard_map.102), calls=%async_computation | async-start | bytes 3538944 | tf_op jit(solution)/shard_map/all_to_all | solution.py:340
  9.9 22.7 %copy-start = (s32[1,8]{1,0:T(1,128)S(1)}, s32[1,8]{1,0:T(1,128)}, u32[]{:S(2)}) copy-start(s32[1,8]{1,0:T(1,128)} %lengths.1) | copy-start | bytes 100
  10.9 10.2 %collective-permute-start.4 = (bf16[128,1152]{1,0:T(8,128)(2,1)}, bf16[128,1152]{1,0:T(8,128)(2,1)S(1)}, u32[]{:S(2)}, u32[]{:S(2)}) collective-permute-start(bf16[128,1152]{1,0:T(8,128)(2,1)} %get-tuple-element.49), channel_id=1, source_target_pairs={{0,8},{1,9},{2,10},{3,11},{4,12},{5,13},{6,14},{7,15},{8,0},{9,1},... | collective-permute-start | bytes 884744 | tf_op jit(solution)/shard_map/ppermute | solution.py:32
  12.4 15.5 %collective-permute-start.5 = (bf16[128,1152]{1,0:T(8,128)(2,1)}, bf16[128,1152]{1,0:T(8,128)(2,1)S(1)}, u32[]{:S(2)}, u32[]{:S(2)}) collective-permute-start(bf16[128,1152]{1,0:T(8,128)(2,1)} %get-tuple-element.50), channel_id=1, source_target_pairs={{0,16},{1,17},{2,18},{3,19},{4,20},{5,21},{6,22},{7,23},{8,24},{9,... | collective-permute-start | bytes 884744 | tf_op jit(solution)/shard_map/ppermute | solution.py:32
  15.1 15.4 %collective-permute-start.6 = (bf16[128,1152]{1,0:T(8,128)(2,1)}, bf16[128,1152]{1,0:T(8,128)(2,1)S(1)}, u32[]{:S(2)}, u32[]{:S(2)}) collective-permute-start(bf16[128,1152]{1,0:T(8,128)(2,1)} %get-tuple-element.51), channel_id=1, source_target_pairs={{0,24},{1,25},{2,26},{3,27},{4,28},{5,29},{6,30},{7,31},{8,16},{9,... | collective-permute-start | bytes 884744 | tf_op jit(solution)/shard_map/ppermute | solution.py:32
  32.4 12.1 %collective-permute-start.7 = (bf16[576,512]{1,0:T(8,128)(2,1)}, bf16[576,512]{1,0:T(8,128)(2,1)S(1)}, u32[]{:S(2)}, u32[]{:S(2)}) collective-permute-start(bf16[576,512]{1,0:T(8,128)(2,1)} %get-tuple-element.54), channel_id=1, source_target_pairs={{0,1},{1,0},{2,3},{3,2},{4,5},{5,4},{6,7},{7,6},{8,9},{9,8},{10,11... | collective-permute-start | bytes 1769480 | tf_op jit(solution)/shard_map/ppermute | solution.py:32
  32.4 23.7 %collective-permute-start.8 = (bf16[576,512]{1,0:T(8,128)(2,1)S(1)}, bf16[576,512]{1,0:T(8,128)(2,1)S(1)}, u32[]{:S(2)}, u32[]{:S(2)}) collective-permute-start(bf16[576,512]{1,0:T(8,128)(2,1)S(1)} %get-tuple-element.53.refs_0_), channel_id=1, source_target_pairs={{0,128},{1,129},{2,130},{3,131},{4,132},{5,133},{6,134},{7,135},{8... | collective-permute-start | bytes 1769480 | tf_op jit(solution)/shard_map/ppermute | solution.py:32
  40.0 11.2 %collective-permute-start = (bf16[2,128,512]{2,1,0:T(8,128)(2,1)S(1)}, bf16[2,128,512]{2,1,0:T(8,128)(2,1)S(1)}, u32[]{:S(2)}, u32[]{:S(2)}) collective-permute-start(bf16[2,128,512]{2,1,0:T(8,128)(2,1)S(1)} %get-tuple-element.41), channel_id=1, source_target_pairs={{0,32},{1,33},{2,34},{3,35},{4,36},{5,37},{6,38},{7,39},{8,40},{9,... | collective-permute-start | bytes 786440 | tf_op jit(solution)/shard_map/ppermute | solution.py:32
  41.8 9.5 %collective-permute-start.2 = (bf16[2,128,512]{2,1,0:T(8,128)(2,1)S(1)}, bf16[2,128,512]{2,1,0:T(8,128)(2,1)S(1)}, u32[]{:S(2)}, u32[]{:S(2)}) collective-permute-start(bf16[2,128,512]{2,1,0:T(8,128)(2,1)S(1)} %get-tuple-element.45), channel_id=1, source_target_pairs={{0,96},{1,97},{2,98},{3,99},{4,100},{5,101},{6,102},{7,103},{8,104... | collective-permute-start | bytes 786440 | tf_op jit(solution)/shard_map/ppermute | solution.py:32
  43.9 7.3 %collective-permute-start.1 = (bf16[2,128,128]{2,1,0:T(8,128)(2,1)S(1)}, bf16[2,128,128]{2,1,0:T(8,128)(2,1)S(1)}, u32[]{:S(2)}, u32[]{:S(2)}) collective-permute-start(bf16[2,128,128]{2,1,0:T(8,128)(2,1)S(1)} %get-tuple-element.44), channel_id=1, source_target_pairs={{0,64},{1,65},{2,66},{3,67},{4,68},{5,69},{6,70},{7,71},{8,72},{9,... | collective-permute-start | bytes 196616 | tf_op jit(solution)/shard_map/ppermute | solution.py:32
  44.4 20.7 %collective-permute-start.9 = (bf16[576,512]{1,0:T(8,128)(2,1)S(1)}, bf16[576,512]{1,0:T(8,128)(2,1)S(1)}, u32[]{:S(2)}, u32[]{:S(2)}) collective-permute-start(bf16[576,512]{1,0:T(8,128)(2,1)S(1)} %collective-permute-done.7.refs_1_), channel_id=1, source_target_pairs={{0,128},{1,129},{2,130},{3,131},{4,132},{5,133},{6,134},{7,135},{8... | collective-permute-start | bytes 1769480 | tf_op jit(solution)/shard_map/ppermute | solution.py:32
  51.9 12.6 %collective-permute-start.12 = (bf16[2,128,512]{2,1,0:T(8,128)(2,1)S(1)}, bf16[2,128,512]{2,1,0:T(8,128)(2,1)S(1)}, u32[]{:S(2)}, u32[]{:S(2)}) collective-permute-start(bf16[2,128,512]{2,1,0:T(8,128)(2,1)S(1)} %get-tuple-element.46.refs_4_), channel_id=1, source_target_pairs={{0,24},{1,25},{2,26},{3,27},{4,28},{5,29},{6,30},{7,31},{8,16},{9,... | collective-permute-start | bytes 786440 | tf_op jit(solution)/shard_map/ppermute | solution.py:32
  53.2 11.3 %collective-permute-start.11 = (bf16[2,128,512]{2,1,0:T(8,128)(2,1)S(1)}, bf16[2,128,512]{2,1,0:T(8,128)(2,1)S(1)}, u32[]{:S(2)}, u32[]{:S(2)}) collective-permute-start(bf16[2,128,512]{2,1,0:T(8,128)(2,1)S(1)} %get-tuple-element.46.refs_4_), channel_id=1, source_target_pairs={{0,16},{1,17},{2,18},{3,19},{4,20},{5,21},{6,22},{7,23},{8,24},{9,... | collective-permute-start | bytes 786440 | tf_op jit(solution)/shard_map/ppermute | solution.py:32
  54.2 11.0 %collective-permute-start.10 = (bf16[2,128,512]{2,1,0:T(8,128)(2,1)S(1)}, bf16[2,128,512]{2,1,0:T(8,128)(2,1)S(1)}, u32[]{:S(2)}, u32[]{:S(2)}) collective-permute-start(bf16[2,128,512]{2,1,0:T(8,128)(2,1)S(1)} %get-tuple-element.46.refs_4_), channel_id=1, source_target_pairs={{0,8},{1,9},{2,10},{3,11},{4,12},{5,13},{6,14},{7,15},{8,0},{9,1},... | collective-permute-start | bytes 786440 | tf_op jit(solution)/shard_map/ppermute | solution.py:32
  56.1 7.2 %collective-permute-start.3 = (bf16[2,128,384]{2,1,0:T(8,128)(2,1)S(1)}, bf16[2,128,384]{2,1,0:T(8,128)(2,1)S(1)}, u32[]{:S(2)}, u32[]{:S(2)}) collective-permute-start(bf16[2,128,384]{2,1,0:T(8,128)(2,1)S(1)} %get-tuple-element.47), channel_id=1, source_target_pairs={{0,64},{1,65},{2,66},{3,67},{4,68},{5,69},{6,70},{7,71},{8,72},{9,... | collective-permute-start | bytes 589832 | tf_op jit(solution)/shard_map/ppermute | solution.py:32
  63.3 1.9 %collective-permute-start.13 = (bf16[2,128,512]{2,1,0:T(8,128)(2,1)S(1)}, bf16[2,128,512]{2,1,0:T(8,128)(2,1)S(1)}, u32[]{:S(2)}, u32[]{:S(2)}) collective-permute-start(bf16[2,128,512]{2,1,0:T(8,128)(2,1)S(1)} %get-tuple-element.46.refs_4_), channel_id=1, source_target_pairs={{0,1},{1,0},{2,3},{3,2},{4,5},{5,4},{6,7},{7,6},{8,9},{9,8},{10,11... | collective-permute-start | bytes 786440 | tf_op jit(solution)/shard_map/ppermute | solution.py:32
  64.6 1.5 %collective-permute-start.16 = (bf16[2,128,512]{2,1,0:T(8,128)(2,1)S(1)}, bf16[2,128,512]{2,1,0:T(8,128)(2,1)S(1)}, u32[]{:S(2)}, u32[]{:S(2)}) collective-permute-start(bf16[2,128,512]{2,1,0:T(8,128)(2,1)S(1)} %collective-permute-done.12.refs_7_), channel_id=1, source_target_pairs={{0,1},{1,0},{2,3},{3,2},{4,5},{5,4},{6,7},{7,6},{8,9},{9,8},{10,11... | collective-permute-start | bytes 786440 | tf_op jit(solution)/shard_map/ppermute | solution.py:32
  64.6 1.9 %collective-permute-start.15 = (bf16[2,128,512]{2,1,0:T(8,128)(2,1)S(1)}, bf16[2,128,512]{2,1,0:T(8,128)(2,1)S(1)}, u32[]{:S(2)}, u32[]{:S(2)}) collective-permute-start(bf16[2,128,512]{2,1,0:T(8,128)(2,1)S(1)} %collective-permute-done.11.refs_6_), channel_id=1, source_target_pairs={{0,1},{1,0},{2,3},{3,2},{4,5},{5,4},{6,7},{7,6},{8,9},{9,8},{10,11... | collective-permute-start | bytes 786440 | tf_op jit(solution)/shard_map/ppermute | solution.py:32
  65.2 1.7 %collective-permute-start.14 = (bf16[2,128,512]{2,1,0:T(8,128)(2,1)S(1)}, bf16[2,128,512]{2,1,0:T(8,128)(2,1)S(1)}, u32[]{:S(2)}, u32[]{:S(2)}) collective-permute-start(bf16[2,128,512]{2,1,0:T(8,128)(2,1)S(1)} %collective-permute-done.10.refs_5_), channel_id=1, source_target_pairs={{0,1},{1,0},{2,3},{3,2},{4,5},{5,4},{6,7},{7,6},{8,9},{9,8},{10,11... | collective-permute-start | bytes 786440 | tf_op jit(solution)/shard_map/ppermute | solution.py:32
  69.5 29.9 %collective-permute-start.17 = (bf16[4,128,384]{2,1,0:T(8,128)(2,1)S(1)}, bf16[4,128,384]{2,1,0:T(8,128)(2,1)S(1)}, u32[]{:S(2)}, u32[]{:S(2)}) collective-permute-start(bf16[4,128,384]{2,1,0:T(8,128)(2,1)S(1)} %shard_map.107), channel_id=1, source_target_pairs={{0,128},{1,129},{2,130},{3,131},{4,132},{5,133},{6,134},{7,135},{8... | collective-permute-start | bytes 1179656 | tf_op jit(solution)/shard_map/ppermute | solution.py:32
  71.0 6.7 %collective-permute-start.19 = (bf16[576,128]{1,0:T(8,128)(2,1)S(1)}, bf16[576,128]{1,0:T(8,128)(2,1)S(1)}, u32[]{:S(2)}, u32[]{:S(2)}) collective-permute-start(bf16[576,128]{1,0:T(8,128)(2,1)S(1)} %get-tuple-element.66), channel_id=1, source_target_pairs={{0,32},{1,33},{2,34},{3,35},{4,36},{5,37},{6,38},{7,39},{8,40},{9,... | collective-permute-start | bytes 442376 | tf_op jit(solution)/shard_map/ppermute | solution.py:32
  71.2 10.0 %collective-permute-start.20 = (bf16[576,128]{1,0:T(8,128)(2,1)S(1)}, bf16[576,128]{1,0:T(8,128)(2,1)S(1)}, u32[]{:S(2)}, u32[]{:S(2)}) collective-permute-start(bf16[576,128]{1,0:T(8,128)(2,1)S(1)} %get-tuple-element.67), channel_id=1, source_target_pairs={{0,64},{1,65},{2,66},{3,67},{4,68},{5,69},{6,70},{7,71},{8,72},{9,... | collective-permute-start | bytes 442376 | tf_op jit(solution)/shard_map/ppermute | solution.py:32
  74.4 9.1 %collective-permute-start.21 = (bf16[576,128]{1,0:T(8,128)(2,1)S(1)}, bf16[576,128]{1,0:T(8,128)(2,1)S(1)}, u32[]{:S(2)}, u32[]{:S(2)}) collective-permute-start(bf16[576,128]{1,0:T(8,128)(2,1)S(1)} %get-tuple-element.68), channel_id=1, source_target_pairs={{0,96},{1,97},{2,98},{3,99},{4,100},{5,101},{6,102},{7,103},{8,104... | collective-permute-start | bytes 442376 | tf_op jit(solution)/shard_map/ppermute | solution.py:32
  75.7 23.8 %collective-permute-start.18 = (bf16[128,512]{1,0:T(8,128)(2,1)S(1)}, bf16[128,512]{1,0:T(8,128)(2,1)S(1)}, u32[]{:S(2)}, u32[]{:S(2)}) collective-permute-start(bf16[128,512]{1,0:T(8,128)(2,1)S(1)} %get-tuple-element.62), channel_id=1, source_target_pairs={{0,128},{1,129},{2,130},{3,131},{4,132},{5,133},{6,134},{7,135},{8... | collective-permute-start | bytes 393224 | tf_op jit(solution)/shard_map/ppermute | solution.py:32
  84.1 8.7 %collective-permute-start.22 = (bf16[2,144,128]{2,1,0:T(8,128)(2,1)S(1)}, bf16[2,144,128]{2,1,0:T(8,128)(2,1)S(1)}, u32[]{:S(2)}, u32[]{:S(2)}) collective-permute-start(bf16[2,144,128]{2,1,0:T(8,128)(2,1)S(1)} %get-tuple-element.70), channel_id=1, source_target_pairs={{0,2},{1,3},{2,0},{3,1},{4,6},{5,7},{6,4},{7,5},{8,10},{9,11},{10,... | collective-permute-start | bytes 221192 | tf_op jit(solution)/shard_map/ppermute | solution.py:32
  92.8 8.5 %collective-permute-start.23 = (bf16[144,128]{1,0:T(8,128)(2,1)S(1)}, bf16[144,128]{1,0:T(8,128)(2,1)S(1)}, u32[]{:S(2)}, u32[]{:S(2)}) collective-permute-start(bf16[144,128]{1,0:T(8,128)(2,1)S(1)} %get-tuple-element.73), channel_id=1, source_target_pairs={{0,6},{1,7},{2,4},{3,5},{4,2},{5,3},{6,0},{7,1},{8,14},{9,15},{10,... | collective-permute-start | bytes 110600 | tf_op jit(solution)/shard_map/ppermute | solution.py:32

commit v5 on v4

--- a/solution.py
+++ b/solution.py
@@ -350,7 +350,6 @@
         [SMEM] + [VMEM] * 4,
         [pltpu.VMEM((1152, ROWS), BF)],
     )(where, *own)
-    far_rows = over_core(far_rows)
     across_near = over_ctx(near_rows, 4)
 
     results = call(
@@ -368,7 +367,8 @@
     )(where, document_lengths, arrived)
     backs, values = results[:4], results[4:]
 
-    across_far = over_ctx(after(far_rows, values[0]), 4)
+    far_rows = over_core(after(far_rows, values[0]))
+    across_far = over_ctx(far_rows, 4)
     first, third = over_y(backs[1], 1), over_y(backs[3], 3)
     pieces = [values[0], first, over_y(values[1], 2), third]
     joined, near, far = call(

time: 101 us -> 101 us (level); the launches traced: 102 us -> 100 us
  starting transfers between devices: 42.6 us -> 40.1 us
  Pallas kernels: 18.6 us -> 16.2 us
  waiting for transfers between devices: 39.1 us -> 41.5 us
    ppermute x24, starting transfers between devices: 36.6 us -> 34 us  [spread(): return lax.ppermute(block, ('ctx', 'dp'), route)]
    ppermute x24, waiting for transfers between devices: 39 us -> 41.5 us  [spread(): return lax.ppermute(block, ('ctx', 'dp'), route)]
    pallas_call x1, Pallas kernels: 7.28 us -> 5.72 us  [body(): call(attention_kernel, [shape(2, ROWS, BACK), shape(2, ROWS, 512)] * 2 +...]
  transfers between devices with their start and end apart: 25 -> 25, of which waited for: 16 -> 16; matrix products, arithmetic and copies ran while one was open for 1% -> 1% of each run, Pallas kernels for 12% -> 4%
where the time goes in v5:
time: 101 us; the launch traced here: 100 us
  waiting for transfers between devices  41.5 us (41%)
  starting transfers between devices  40.1 us (40%)
  Pallas kernels  16.2 us (16%)
  local copies, waits for them, and re-layouts  1.76 us (2%)
    ppermute x24, waiting for transfers between devices, spread(): return lax.ppermute(block, ('ctx', 'dp'), route)  41.5 us
    ppermute x24, starting transfers between devices, spread(): return lax.ppermute(block, ('ctx', 'dp'), route)  34 us
    all_to_all x1, starting transfers between devices, body(): arrived = lax.all_to_all(packed, 'ctx', 0, 0, tiled=True)  6.07 us
    pallas_call x1, Pallas kernels, body(): call(attention_kernel, [shape(2, ROWS, BACK), shape(2, ROWS, 512)] * 2 +...  5.72 us
    pallas_call x1, Pallas kernels, body(): call(pack_kernel, shape(BLOCKS, ROWS + TAIL, PACKED), [ANY] * 5, [pltpu.V...  3.22 us
    pallas_call x1, Pallas kernels, body(): call(weight_kernel, [shape(576, HEAD)] * 4, [SMEM] + [VMEM] * 12, [pltpu....  2.03 us
  transfers between devices with their start and end apart: 25, of which 16 were waited for; matrix products, arithmetic and copies ran while one was open for 1% of the time, Pallas kernels for 4%

profile of v5, /device:TPU:32, one launch (start us, length us, event | category | flops | bytes accessed | tf_op | source)
XLA Modules:
  0.0 100.4 jit_solution(6278398141562771029)
XLA Ops:
  0.6 3.2 %shard_map.102 = bf16[8,144,768]{2,1,0:T(8,128)(2,1)} custom-call(bf16[128,2048]{1,0:T(8,128)(2,1)} %bitcast.19, bf16[128,1024]{1,0:T(8,128)(2,1)} %bitcast.22, bf16[128,1024]{1,0:T(8,128)(2,1)} %bitcast.23, bf16[128,2048]{1,0:T(8,128)(2,1)} %bitcast.20, bf16[128,2048]{1,0:T(8,128)(2,1)} %bitcast.21), custom_call_target="tpu_custom_call" | custom-call | tf_op jit(solution)/shard_map/pallas_call | solution.py:325
  3.9 6.1 %all-to-all-start = ((bf16[8,144,768]{2,1,0:T(8,128)(2,1)}), bf16[8,144,768]{2,1,0:T(8,128)(2,1)S(1)}, u32[]{:S(2)}, u32[]{:S(2)}) async-start(bf16[8,144,768]{2,1,0:T(8,128)(2,1)} %shard_map.102), calls=%async_computation | async-start | bytes 3538944 | tf_op jit(solution)/shard_map/all_to_all | solution.py:340
  10.0 0.9 dynamic-slice_bitcast_fusion
  10.9 1.5 %collective-permute-start.4 = (bf16[128,1152]{1,0:T(8,128)(2,1)}, bf16[128,1152]{1,0:T(8,128)(2,1)S(1)}, u32[]{:S(2)}, u32[]{:S(2)}) collective-permute-start(bf16[128,1152]{1,0:T(8,128)(2,1)} %get-tuple-element.49), channel_id=1, source_target_pairs={{0,8},{1,9},{2,10},{3,11},{4,12},{5,13},{6,14},{7,15},{8,0},{9,1},... | collective-permute-start | bytes 884744 | tf_op jit(solution)/shard_map/ppermute | solution.py:32
  12.4 2.7 %collective-permute-start.5 = (bf16[128,1152]{1,0:T(8,128)(2,1)}, bf16[128,1152]{1,0:T(8,128)(2,1)S(1)}, u32[]{:S(2)}, u32[]{:S(2)}) collective-permute-start(bf16[128,1152]{1,0:T(8,128)(2,1)} %get-tuple-element.50), channel_id=1, source_target_pairs={{0,16},{1,17},{2,18},{3,19},{4,20},{5,21},{6,22},{7,23},{8,24},{9,... | collective-permute-start | bytes 884744 | tf_op jit(solution)/shard_map/ppermute | solution.py:32
  15.1 0.5 collective-permute-start.6
  15.7 5.4 %collective-permute-done.4.refs_1_ = bf16[128,1152]{1,0:T(8,128)(2,1)S(1)} collective-permute-done((bf16[128,1152]{1,0:T(8,128)(2,1)}, bf16[128,1152]{1,0:T(8,128)(2,1)S(1)}, u32[]{:S(2)}, u32[]{:S(2)}) %collective-permute-start.4) | collective-permute-done | bytes 294944 | tf_op jit(solution)/shard_map/ppermute | solution.py:32
  21.1 6.9 %collective-permute-done.5.refs_2_ = bf16[128,1152]{1,0:T(8,128)(2,1)S(1)} collective-permute-done((bf16[128,1152]{1,0:T(8,128)(2,1)}, bf16[128,1152]{1,0:T(8,128)(2,1)S(1)}, u32[]{:S(2)}, u32[]{:S(2)}) %collective-permute-start.5) | collective-permute-done | bytes 294944 | tf_op jit(solution)/shard_map/ppermute | solution.py:32
  27.9 2.6 %collective-permute-done.6.refs_3_ = bf16[128,1152]{1,0:T(8,128)(2,1)S(1)} collective-permute-done((bf16[128,1152]{1,0:T(8,128)(2,1)}, bf16[128,1152]{1,0:T(8,128)(2,1)S(1)}, u32[]{:S(2)}, u32[]{:S(2)}) %collective-permute-start.6) | collective-permute-done | bytes 294944 | tf_op jit(solution)/shard_map/ppermute | solution.py:32
  30.5 1.1 %shard_map.105 = (bf16[576,512]{1,0:T(8,128)(2,1)S(1)}, bf16[576,512]{1,0:T(8,128)(2,1)S(1)}) custom-call(s32[3]{0:T(128)S(1)} %pad_add_fusion.where, bf16[128,1152]{1,0:T(8,128)(2,1)S(1)} %get-tuple-element.48.refs_0_, bf16[128,1152]{1,0:T(8,128)(2,1)S(1)} %collective-permute-done.4.refs_1_, bf16[128,1152]{1,0:T(8,128)(2,1)S(1)} %collective-permute-done.5.refs_2_, ...), custom_call_target="tpu_custom_call" | custom-call | tf_op jit(solution)/shard_map/pallas_call | solution.py:347
  31.6 0.8 copy-done
  32.4 5.7 %shard_map.103 = (bf16[2,128,384]{2,1,0:T(8,128)(2,1)S(1)}, bf16[2,128,512]{2,1,0:T(8,128)(2,1)S(1)}, bf16[2,128,384]{2,1,0:T(8,128)(2,1)S(1)}, bf16[2,128,512]{...) custom-call(s32[3]{0:T(128)S(1)} %pad_add_fusion.where, ...), custom_call_target="tpu_custom_call" | custom-call | flops 4000000000 | bytes 4000000 | tf_op jit(solution)/shard_map/pallas_call | solution.py:355
  38.1 0.5 collective-permute-start.7
  38.7 0.6 collective-permute-start.8
  39.2 1.1 %collective-permute-start = (bf16[2,128,512]{2,1,0:T(8,128)(2,1)S(1)}, bf16[2,128,512]{2,1,0:T(8,128)(2,1)S(1)}, u32[]{:S(2)}, u32[]{:S(2)}) collective-permute-start(bf16[2,128,512]{2,1,0:T(8,128)(2,1)S(1)} %get-tuple-element.41), channel_id=1, source_target_pairs={{0,32},{1,33},{2,34},{3,35},{4,36},{5,37},{6,38},{7,39},{8,40},{9,... | collective-permute-start | bytes 786440 | tf_op jit(solution)/shard_map/ppermute | solution.py:32
  40.3 2.1 %collective-permute-start.2 = (bf16[2,128,512]{2,1,0:T(8,128)(2,1)S(1)}, bf16[2,128,512]{2,1,0:T(8,128)(2,1)S(1)}, u32[]{:S(2)}, u32[]{:S(2)}) collective-permute-start(bf16[2,128,512]{2,1,0:T(8,128)(2,1)S(1)} %get-tuple-element.45), channel_id=1, source_target_pairs={{0,96},{1,97},{2,98},{3,99},{4,100},{5,101},{6,102},{7,103},{8,104... | collective-permute-start | bytes 786440 | tf_op jit(solution)/shard_map/ppermute | solution.py:32
  42.4 0.9 collective-permute-start.1
  43.3 1.5 %collective-permute-start.9 = (bf16[576,512]{1,0:T(8,128)(2,1)S(1)}, bf16[576,512]{1,0:T(8,128)(2,1)S(1)}, u32[]{:S(2)}, u32[]{:S(2)}) collective-permute-start(bf16[576,512]{1,0:T(8,128)(2,1)S(1)} %collective-permute-done.7.refs_1_), channel_id=1, source_target_pairs={{0,128},{1,129},{2,130},{3,131},{4,132},{5,133},{6,134},{7,135},{8... | collective-permute-start | bytes 1769480 | tf_op jit(solution)/shard_map/ppermute | solution.py:32
  44.8 6.1 %collective-permute-done.1.refs_2_ = bf16[2,128,128]{2,1,0:T(8,128)(2,1)S(1)} collective-permute-done((bf16[2,128,128]{2,1,0:T(8,128)(2,1)S(1)}, bf16[2,128,128]{2,1,0:T(8,128)(2,1)S(1)}, u32[]{:S(2)}, u32[]{:S(2)}) %collective-permute-start.1) | collective-permute-done | bytes 65568 | tf_op jit(solution)/shard_map/ppermute | solution.py:32
  50.9 0.2 collective-permute-done.2.refs_3_
  51.0 0.6 shard_map.104
  51.6 1.8 %collective-permute-start.12 = (bf16[2,128,512]{2,1,0:T(8,128)(2,1)S(1)}, bf16[2,128,512]{2,1,0:T(8,128)(2,1)S(1)}, u32[]{:S(2)}, u32[]{:S(2)}) collective-permute-start(bf16[2,128,512]{2,1,0:T(8,128)(2,1)S(1)} %get-tuple-element.46.refs_4_), channel_id=1, source_target_pairs={{0,24},{1,25},{2,26},{3,27},{4,28},{5,29},{6,30},{7,31},{8,16},{9,... | collective-permute-start | bytes 786440 | tf_op jit(solution)/shard_map/ppermute | solution.py:32
  53.4 1.4 %collective-permute-start.11 = (bf16[2,128,512]{2,1,0:T(8,128)(2,1)S(1)}, bf16[2,128,512]{2,1,0:T(8,128)(2,1)S(1)}, u32[]{:S(2)}, u32[]{:S(2)}) collective-permute-start(bf16[2,128,512]{2,1,0:T(8,128)(2,1)S(1)} %get-tuple-element.46.refs_4_), channel_id=1, source_target_pairs={{0,16},{1,17},{2,18},{3,19},{4,20},{5,21},{6,22},{7,23},{8,24},{9,... | collective-permute-start | bytes 786440 | tf_op jit(solution)/shard_map/ppermute | solution.py:32
  54.8 1.0 collective-permute-start.10
  55.8 1.6 %collective-permute-start.3 = (bf16[2,128,384]{2,1,0:T(8,128)(2,1)S(1)}, bf16[2,128,384]{2,1,0:T(8,128)(2,1)S(1)}, u32[]{:S(2)}, u32[]{:S(2)}) collective-permute-start(bf16[2,128,384]{2,1,0:T(8,128)(2,1)S(1)} %get-tuple-element.47), channel_id=1, source_target_pairs={{0,64},{1,65},{2,66},{3,67},{4,68},{5,69},{6,70},{7,71},{8,72},{9,... | collective-permute-start | bytes 589832 | tf_op jit(solution)/shard_map/ppermute | solution.py:32
  57.4 5.6 %collective-permute-done.3.refs_2_ = bf16[2,128,384]{2,1,0:T(8,128)(2,1)S(1)} collective-permute-done((bf16[2,128,384]{2,1,0:T(8,128)(2,1)S(1)}, bf16[2,128,384]{2,1,0:T(8,128)(2,1)S(1)}, u32[]{:S(2)}, u32[]{:S(2)}) %collective-permute-start.3) | collective-permute-done | bytes 196640 | tf_op jit(solution)/shard_map/ppermute | solution.py:32
  63.0 2.5 %collective-permute-done.12.refs_7_ = bf16[2,128,512]{2,1,0:T(8,128)(2,1)S(1)} collective-permute-done((bf16[2,128,512]{2,1,0:T(8,128)(2,1)S(1)}, bf16[2,128,512]{2,1,0:T(8,128)(2,1)S(1)}, u32[]{:S(2)}, u32[]{:S(2)}) %collective-permute-start.12) | collective-permute-done | bytes 262176 | tf_op jit(solution)/shard_map/ppermute | solution.py:32
  65.5 0.5 collective-permute-start.15
  66.1 0.9 collective-permute-done.16.refs_11_
  67.1 0.4 collective-permute-done.15.refs_10_
  67.4 0.4 collective-permute-done.14.refs_9_
  67.8 2.0 %shard_map.106 = (bf16[576,128]{1,0:T(8,128)(2,1)S(1)}, bf16[576,128]{1,0:T(8,128)(2,1)S(1)}, bf16[576,128]{1,0:T(8,128)(2,1)S(1)}, bf16[576,128]{1,0:T(8,128)(2,1)S(1)}) custom-call(s32[3]{0:T(128)S(1)} %pad_add_fusion.where, bf16[576,512]{1,0:T(8,128)(2,1)S(1)} %get-tuple-element.53.refs_0_, bf16[576,512]{1,0:T(8,128)(2,1)S(1)} %collective-permute-done.7.refs_1_, ...), custom_call_target="tpu_custom_call" | custom-call | flops 1300000000 | bytes 4000000 | tf_op jit(solution)/shard_map/pallas_call | solution.py:384
  69.9 0.6 shard_map.107
  70.4 1.5 %collective-permute-start.17 = (bf16[4,128,384]{2,1,0:T(8,128)(2,1)S(1)}, bf16[4,128,384]{2,1,0:T(8,128)(2,1)S(1)}, u32[]{:S(2)}, u32[]{:S(2)}) collective-permute-start(bf16[4,128,384]{2,1,0:T(8,128)(2,1)S(1)} %shard_map.107), channel_id=1, source_target_pairs={{0,128},{1,129},{2,130},{3,131},{4,132},{5,133},{6,134},{7,135},{8... | collective-permute-start | bytes 1179656 | tf_op jit(solution)/shard_map/ppermute | solution.py:32
  72.0 0.3 collective-permute-start.19
  72.2 3.5 %collective-permute-start.20 = (bf16[576,128]{1,0:T(8,128)(2,1)S(1)}, bf16[576,128]{1,0:T(8,128)(2,1)S(1)}, u32[]{:S(2)}, u32[]{:S(2)}) collective-permute-start(bf16[576,128]{1,0:T(8,128)(2,1)S(1)} %get-tuple-element.67), channel_id=1, source_target_pairs={{0,64},{1,65},{2,66},{3,67},{4,68},{5,69},{6,70},{7,71},{8,72},{9,... | collective-permute-start | bytes 442376 | tf_op jit(solution)/shard_map/ppermute | solution.py:32
  75.8 0.9 collective-permute-start.21
  76.7 0.6 collective-permute-start.18
  77.3 1.5 %collective-permute-done.19.refs_1_ = bf16[576,128]{1,0:T(8,128)(2,1)S(1)} collective-permute-done((bf16[576,128]{1,0:T(8,128)(2,1)S(1)}, bf16[576,128]{1,0:T(8,128)(2,1)S(1)}, u32[]{:S(2)}, u32[]{:S(2)}) %collective-permute-start.19) | collective-permute-done | bytes 147488 | tf_op jit(solution)/shard_map/ppermute | solution.py:32
  78.7 3.9 %collective-permute-done.20.refs_2_ = bf16[576,128]{1,0:T(8,128)(2,1)S(1)} collective-permute-done((bf16[576,128]{1,0:T(8,128)(2,1)S(1)}, bf16[576,128]{1,0:T(8,128)(2,1)S(1)}, u32[]{:S(2)}, u32[]{:S(2)}) %collective-permute-start.20) | collective-permute-done | bytes 147488 | tf_op jit(solution)/shard_map/ppermute | solution.py:32
  82.6 2.3 %collective-permute-done.21.refs_3_ = bf16[576,128]{1,0:T(8,128)(2,1)S(1)} collective-permute-done((bf16[576,128]{1,0:T(8,128)(2,1)S(1)}, bf16[576,128]{1,0:T(8,128)(2,1)S(1)}, u32[]{:S(2)}, u32[]{:S(2)}) %collective-permute-start.21) | collective-permute-done | bytes 147488 | tf_op jit(solution)/shard_map/ppermute | solution.py:32
  84.9 0.7 shard_map.109
  85.5 4.6 %collective-permute-start.22 = (bf16[2,144,128]{2,1,0:T(8,128)(2,1)S(1)}, bf16[2,144,128]{2,1,0:T(8,128)(2,1)S(1)}, u32[]{:S(2)}, u32[]{:S(2)}) collective-permute-start(bf16[2,144,128]{2,1,0:T(8,128)(2,1)S(1)} %get-tuple-element.70), channel_id=1, source_target_pairs={{0,2},{1,3},{2,0},{3,1},{4,6},{5,7},{6,4},{7,5},{8,10},{9,11},{10,... | collective-permute-start | bytes 221192 | tf_op jit(solution)/shard_map/ppermute | solution.py:32
  90.2 2.7 %collective-permute-done.22.landed = bf16[2,144,128]{2,1,0:T(8,128)(2,1)S(1)} collective-permute-done((bf16[2,144,128]{2,1,0:T(8,128)(2,1)S(1)}, bf16[2,144,128]{2,1,0:T(8,128)(2,1)S(1)}, u32[]{:S(2)}, u32[]{:S(2)}) %collective-permute-start.22) | collective-permute-done | bytes 73760 | tf_op jit(solution)/shard_map/ppermute | solution.py:32
  92.8 5.0 %collective-permute-start.23 = (bf16[144,128]{1,0:T(8,128)(2,1)S(1)}, bf16[144,128]{1,0:T(8,128)(2,1)S(1)}, u32[]{:S(2)}, u32[]{:S(2)}) collective-permute-start(bf16[144,128]{1,0:T(8,128)(2,1)S(1)} %get-tuple-element.73), channel_id=1, source_target_pairs={{0,6},{1,7},{2,4},{3,5},{4,2},{5,3},{6,0},{7,1},{8,14},{9,15},{10,... | collective-permute-start | bytes 110600 | tf_op jit(solution)/shard_map/ppermute | solution.py:32
  97.8 1.7 %shard_map.108 = (bf16[128,2048]{1,0:T(8,128)(2,1)}, bf16[128,1024]{1,0:T(8,128)(2,1)}, bf16[128,1024]{1,0:T(8,128)(2,1)}) custom-call(s32[3]{0:T(128)S(1)} %pad_add_fusion.where, bf16[2,128,384]{2,1,0:T(8,128)(2,1)S(1)} %get-tuple-element.57.refs_0_, bf16[2,128,512]{2,1,0:T(8,128)(2,1)S(1)} %collective-permute-done.refs_1_, ...), custom_call_target="tpu_custom_call" | custom-call | tf_op jit(solution)/shard_map/pallas_call | solution.py:405
  99.5 0.3 collective-permute-done.23.landed
  99.8 0.6 shard_map.111
  (22 shorter events, 0.2 us)
Async XLA Ops:
  3.9 6.1 %copy-start.3 = (bf16[1,128,4608]{2,1,0:T(8,128)(2,1)S(1)}, bf16[1,128,4608]{2,1,0:T(8,128)(2,1)}, u32[]{:S(2)}) copy-start(bf16[1,128,4608]{2,1,0:T(8,128)(2,1)} %param.12) | copy-start | bytes 3538948
  3.9 28.5 %all-to-all-start = ((bf16[8,144,768]{2,1,0:T(8,128)(2,1)}), bf16[8,144,768]{2,1,0:T(8,128)(2,1)S(1)}, u32[]{:S(2)}, u32[]{:S(2)}) async-start(bf16[8,144,768]{2,1,0:T(8,128)(2,1)} %shard_map.102), calls=%async_computation | async-start | bytes 3538944 | tf_op jit(solution)/shard_map/all_to_all | solution.py:340
  10.0 22.4 %copy-start.2 = (s32[1,8]{1,0:T(1,128)S(1)}, s32[1,8]{1,0:T(1,128)}, u32[]{:S(2)}) copy-start(s32[1,8]{1,0:T(1,128)} %lengths.1) | copy-start | bytes 100
  10.9 10.2 %collective-permute-start.4 = (bf16[128,1152]{1,0:T(8,128)(2,1)}, bf16[128,1152]{1,0:T(8,128)(2,1)S(1)}, u32[]{:S(2)}, u32[]{:S(2)}) collective-permute-start(bf16[128,1152]{1,0:T(8,128)(2,1)} %get-tuple-element.49), channel_id=1, source_target_pairs={{0,8},{1,9},{2,10},{3,11},{4,12},{5,13},{6,14},{7,15},{8,0},{9,1},... | collective-permute-start | bytes 884744 | tf_op jit(solution)/shard_map/ppermute | solution.py:32
  12.4 15.5 %collective-permute-start.5 = (bf16[128,1152]{1,0:T(8,128)(2,1)}, bf16[128,1152]{1,0:T(8,128)(2,1)S(1)}, u32[]{:S(2)}, u32[]{:S(2)}) collective-permute-start(bf16[128,1152]{1,0:T(8,128)(2,1)} %get-tuple-element.50), channel_id=1, source_target_pairs={{0,16},{1,17},{2,18},{3,19},{4,20},{5,21},{6,22},{7,23},{8,24},{9,... | collective-permute-start | bytes 884744 | tf_op jit(solution)/shard_map/ppermute | solution.py:32
  15.1 15.4 %collective-permute-start.6 = (bf16[128,1152]{1,0:T(8,128)(2,1)}, bf16[128,1152]{1,0:T(8,128)(2,1)S(1)}, u32[]{:S(2)}, u32[]{:S(2)}) collective-permute-start(bf16[128,1152]{1,0:T(8,128)(2,1)} %get-tuple-element.51), channel_id=1, source_target_pairs={{0,24},{1,25},{2,26},{3,27},{4,28},{5,29},{6,30},{7,31},{8,16},{9,... | collective-permute-start | bytes 884744 | tf_op jit(solution)/shard_map/ppermute | solution.py:32
  31.6 0.8 copy-start
  32.4 5.7 %copy-start.1 = (bf16[576,512]{1,0:T(8,128)(2,1)S(1)}, bf16[576,512]{1,0:T(8,128)(2,1)}, u32[]{:S(2)}) copy-start(bf16[576,512]{1,0:T(8,128)(2,1)} %copy-done) | copy-start | bytes 1769476
  38.1 5.2 %collective-permute-start.7 = (bf16[576,512]{1,0:T(8,128)(2,1)S(1)}, bf16[576,512]{1,0:T(8,128)(2,1)S(1)}, u32[]{:S(2)}, u32[]{:S(2)}) collective-permute-start(bf16[576,512]{1,0:T(8,128)(2,1)S(1)} %copy-done.1), channel_id=1, source_target_pairs={{0,1},{1,0},{2,3},{3,2},{4,5},{5,4},{6,7},{7,6},{8,9},{9,8},{10,11... | collective-permute-start | bytes 1769480 | tf_op jit(solution)/shard_map/ppermute | solution.py:32
  38.7 17.2 %collective-permute-start.8 = (bf16[576,512]{1,0:T(8,128)(2,1)S(1)}, bf16[576,512]{1,0:T(8,128)(2,1)S(1)}, u32[]{:S(2)}, u32[]{:S(2)}) collective-permute-start(bf16[576,512]{1,0:T(8,128)(2,1)S(1)} %get-tuple-element.53.refs_0_), channel_id=1, source_target_pairs={{0,128},{1,129},{2,130},{3,131},{4,132},{5,133},{6,134},{7,135},{8... | collective-permute-start | bytes 1769480 | tf_op jit(solution)/shard_map/ppermute | solution.py:32
  39.2 11.6 %collective-permute-start = (bf16[2,128,512]{2,1,0:T(8,128)(2,1)S(1)}, bf16[2,128,512]{2,1,0:T(8,128)(2,1)S(1)}, u32[]{:S(2)}, u32[]{:S(2)}) collective-permute-start(bf16[2,128,512]{2,1,0:T(8,128)(2,1)S(1)} %get-tuple-element.41), channel_id=1, source_target_pairs={{0,32},{1,33},{2,34},{3,35},{4,36},{5,37},{6,38},{7,39},{8,40},{9,... | collective-permute-start | bytes 786440 | tf_op jit(solution)/shard_map/ppermute | solution.py:32
  40.3 10.7 %collective-permute-start.2 = (bf16[2,128,512]{2,1,0:T(8,128)(2,1)S(1)}, bf16[2,128,512]{2,1,0:T(8,128)(2,1)S(1)}, u32[]{:S(2)}, u32[]{:S(2)}) collective-permute-start(bf16[2,128,512]{2,1,0:T(8,128)(2,1)S(1)} %get-tuple-element.45), channel_id=1, source_target_pairs={{0,96},{1,97},{2,98},{3,99},{4,100},{5,101},{6,102},{7,103},{8,104... | collective-permute-start | bytes 786440 | tf_op jit(solution)/shard_map/ppermute | solution.py:32
  42.4 8.5 %collective-permute-start.1 = (bf16[2,128,128]{2,1,0:T(8,128)(2,1)S(1)}, bf16[2,128,128]{2,1,0:T(8,128)(2,1)S(1)}, u32[]{:S(2)}, u32[]{:S(2)}) collective-permute-start(bf16[2,128,128]{2,1,0:T(8,128)(2,1)S(1)} %get-tuple-element.44), channel_id=1, source_target_pairs={{0,64},{1,65},{2,66},{3,67},{4,68},{5,69},{6,70},{7,71},{8,72},{9,... | collective-permute-start | bytes 196616 | tf_op jit(solution)/shard_map/ppermute | solution.py:32
  43.3 24.5 %collective-permute-start.9 = (bf16[576,512]{1,0:T(8,128)(2,1)S(1)}, bf16[576,512]{1,0:T(8,128)(2,1)S(1)}, u32[]{:S(2)}, u32[]{:S(2)}) collective-permute-start(bf16[576,512]{1,0:T(8,128)(2,1)S(1)} %collective-permute-done.7.refs_1_), channel_id=1, source_target_pairs={{0,128},{1,129},{2,130},{3,131},{4,132},{5,133},{6,134},{7,135},{8... | collective-permute-start | bytes 1769480 | tf_op jit(solution)/shard_map/ppermute | solution.py:32
  51.6 13.9 %collective-permute-start.12 = (bf16[2,128,512]{2,1,0:T(8,128)(2,1)S(1)}, bf16[2,128,512]{2,1,0:T(8,128)(2,1)S(1)}, u32[]{:S(2)}, u32[]{:S(2)}) collective-permute-start(bf16[2,128,512]{2,1,0:T(8,128)(2,1)S(1)} %get-tuple-element.46.refs_4_), channel_id=1, source_target_pairs={{0,24},{1,25},{2,26},{3,27},{4,28},{5,29},{6,30},{7,31},{8,16},{9,... | collective-permute-start | bytes 786440 | tf_op jit(solution)/shard_map/ppermute | solution.py:32
  53.4 12.1 %collective-permute-start.11 = (bf16[2,128,512]{2,1,0:T(8,128)(2,1)S(1)}, bf16[2,128,512]{2,1,0:T(8,128)(2,1)S(1)}, u32[]{:S(2)}, u32[]{:S(2)}) collective-permute-start(bf16[2,128,512]{2,1,0:T(8,128)(2,1)S(1)} %get-tuple-element.46.refs_4_), channel_id=1, source_target_pairs={{0,16},{1,17},{2,18},{3,19},{4,20},{5,21},{6,22},{7,23},{8,24},{9,... | collective-permute-start | bytes 786440 | tf_op jit(solution)/shard_map/ppermute | solution.py:32
  54.8 11.3 %collective-permute-start.10 = (bf16[2,128,512]{2,1,0:T(8,128)(2,1)S(1)}, bf16[2,128,512]{2,1,0:T(8,128)(2,1)S(1)}, u32[]{:S(2)}, u32[]{:S(2)}) collective-permute-start(bf16[2,128,512]{2,1,0:T(8,128)(2,1)S(1)} %get-tuple-element.46.refs_4_), channel_id=1, source_target_pairs={{0,8},{1,9},{2,10},{3,11},{4,12},{5,13},{6,14},{7,15},{8,0},{9,1},... | collective-permute-start | bytes 786440 | tf_op jit(solution)/shard_map/ppermute | solution.py:32
  55.8 7.2 %collective-permute-start.3 = (bf16[2,128,384]{2,1,0:T(8,128)(2,1)S(1)}, bf16[2,128,384]{2,1,0:T(8,128)(2,1)S(1)}, u32[]{:S(2)}, u32[]{:S(2)}) collective-permute-start(bf16[2,128,384]{2,1,0:T(8,128)(2,1)S(1)} %get-tuple-element.47), channel_id=1, source_target_pairs={{0,64},{1,65},{2,66},{3,67},{4,68},{5,69},{6,70},{7,71},{8,72},{9,... | collective-permute-start | bytes 589832 | tf_op jit(solution)/shard_map/ppermute | solution.py:32
  63.0 3.1 %collective-permute-start.13 = (bf16[2,128,512]{2,1,0:T(8,128)(2,1)S(1)}, bf16[2,128,512]{2,1,0:T(8,128)(2,1)S(1)}, u32[]{:S(2)}, u32[]{:S(2)}) collective-permute-start(bf16[2,128,512]{2,1,0:T(8,128)(2,1)S(1)} %get-tuple-element.46.refs_4_), channel_id=1, source_target_pairs={{0,1},{1,0},{2,3},{3,2},{4,5},{5,4},{6,7},{7,6},{8,9},{9,8},{10,11... | collective-permute-start | bytes 786440 | tf_op jit(solution)/shard_map/ppermute | solution.py:32
  65.5 1.5 %collective-permute-start.16 = (bf16[2,128,512]{2,1,0:T(8,128)(2,1)S(1)}, bf16[2,128,512]{2,1,0:T(8,128)(2,1)S(1)}, u32[]{:S(2)}, u32[]{:S(2)}) collective-permute-start(bf16[2,128,512]{2,1,0:T(8,128)(2,1)S(1)} %collective-permute-done.12.refs_7_), channel_id=1, source_target_pairs={{0,1},{1,0},{2,3},{3,2},{4,5},{5,4},{6,7},{7,6},{8,9},{9,8},{10,11... | collective-permute-start | bytes 786440 | tf_op jit(solution)/shard_map/ppermute | solution.py:32
  65.5 1.9 %collective-permute-start.15 = (bf16[2,128,512]{2,1,0:T(8,128)(2,1)S(1)}, bf16[2,128,512]{2,1,0:T(8,128)(2,1)S(1)}, u32[]{:S(2)}, u32[]{:S(2)}) collective-permute-start(bf16[2,128,512]{2,1,0:T(8,128)(2,1)S(1)} %collective-permute-done.11.refs_6_), channel_id=1, source_target_pairs={{0,1},{1,0},{2,3},{3,2},{4,5},{5,4},{6,7},{7,6},{8,9},{9,8},{10,11... | collective-permute-start | bytes 786440 | tf_op jit(solution)/shard_map/ppermute | solution.py:32
  66.1 1.7 %collective-permute-start.14 = (bf16[2,128,512]{2,1,0:T(8,128)(2,1)S(1)}, bf16[2,128,512]{2,1,0:T(8,128)(2,1)S(1)}, u32[]{:S(2)}, u32[]{:S(2)}) collective-permute-start(bf16[2,128,512]{2,1,0:T(8,128)(2,1)S(1)} %collective-permute-done.10.refs_5_), channel_id=1, source_target_pairs={{0,1},{1,0},{2,3},{3,2},{4,5},{5,4},{6,7},{7,6},{8,9},{9,8},{10,11... | collective-permute-start | bytes 786440 | tf_op jit(solution)/shard_map/ppermute | solution.py:32
  70.4 27.4 %collective-permute-start.17 = (bf16[4,128,384]{2,1,0:T(8,128)(2,1)S(1)}, bf16[4,128,384]{2,1,0:T(8,128)(2,1)S(1)}, u32[]{:S(2)}, u32[]{:S(2)}) collective-permute-start(bf16[4,128,384]{2,1,0:T(8,128)(2,1)S(1)} %shard_map.107), channel_id=1, source_target_pairs={{0,128},{1,129},{2,130},{3,131},{4,132},{5,133},{6,134},{7,135},{8... | collective-permute-start | bytes 1179656 | tf_op jit(solution)/shard_map/ppermute | solution.py:32
  72.0 6.7 %collective-permute-start.19 = (bf16[576,128]{1,0:T(8,128)(2,1)S(1)}, bf16[576,128]{1,0:T(8,128)(2,1)S(1)}, u32[]{:S(2)}, u32[]{:S(2)}) collective-permute-start(bf16[576,128]{1,0:T(8,128)(2,1)S(1)} %get-tuple-element.66), channel_id=1, source_target_pairs={{0,32},{1,33},{2,34},{3,35},{4,36},{5,37},{6,38},{7,39},{8,40},{9,... | collective-permute-start | bytes 442376 | tf_op jit(solution)/shard_map/ppermute | solution.py:32
  72.2 10.4 %collective-permute-start.20 = (bf16[576,128]{1,0:T(8,128)(2,1)S(1)}, bf16[576,128]{1,0:T(8,128)(2,1)S(1)}, u32[]{:S(2)}, u32[]{:S(2)}) collective-permute-start(bf16[576,128]{1,0:T(8,128)(2,1)S(1)} %get-tuple-element.67), channel_id=1, source_target_pairs={{0,64},{1,65},{2,66},{3,67},{4,68},{5,69},{6,70},{7,71},{8,72},{9,... | collective-permute-start | bytes 442376 | tf_op jit(solution)/shard_map/ppermute | solution.py:32
  75.8 9.1 %collective-permute-start.21 = (bf16[576,128]{1,0:T(8,128)(2,1)S(1)}, bf16[576,128]{1,0:T(8,128)(2,1)S(1)}, u32[]{:S(2)}, u32[]{:S(2)}) collective-permute-start(bf16[576,128]{1,0:T(8,128)(2,1)S(1)} %get-tuple-element.68), channel_id=1, source_target_pairs={{0,96},{1,97},{2,98},{3,99},{4,100},{5,101},{6,102},{7,103},{8,104... | collective-permute-start | bytes 442376 | tf_op jit(solution)/shard_map/ppermute | solution.py:32
  76.7 21.1 %collective-permute-start.18 = (bf16[128,512]{1,0:T(8,128)(2,1)S(1)}, bf16[128,512]{1,0:T(8,128)(2,1)S(1)}, u32[]{:S(2)}, u32[]{:S(2)}) collective-permute-start(bf16[128,512]{1,0:T(8,128)(2,1)S(1)} %get-tuple-element.62), channel_id=1, source_target_pairs={{0,128},{1,129},{2,130},{3,131},{4,132},{5,133},{6,134},{7,135},{8... | collective-permute-start | bytes 393224 | tf_op jit(solution)/shard_map/ppermute | solution.py:32
  85.5 7.3 %collective-permute-start.22 = (bf16[2,144,128]{2,1,0:T(8,128)(2,1)S(1)}, bf16[2,144,128]{2,1,0:T(8,128)(2,1)S(1)}, u32[]{:S(2)}, u32[]{:S(2)}) collective-permute-start(bf16[2,144,128]{2,1,0:T(8,128)(2,1)S(1)} %get-tuple-element.70), channel_id=1, source_target_pairs={{0,2},{1,3},{2,0},{3,1},{4,6},{5,7},{6,4},{7,5},{8,10},{9,11},{10,... | collective-permute-start | bytes 221192 | tf_op jit(solution)/shard_map/ppermute | solution.py:32
  92.8 6.9 %collective-permute-start.23 = (bf16[144,128]{1,0:T(8,128)(2,1)S(1)}, bf16[144,128]{1,0:T(8,128)(2,1)S(1)}, u32[]{:S(2)}, u32[]{:S(2)}) collective-permute-start(bf16[144,128]{1,0:T(8,128)(2,1)S(1)} %get-tuple-element.73), channel_id=1, source_target_pairs={{0,6},{1,7},{2,4},{3,5},{4,2},{5,3},{6,0},{7,1},{8,14},{9,15},{10,... | collective-permute-start | bytes 110600 | tf_op jit(solution)/shard_map/ppermute | solution.py:32

commit v6 on v5

--- a/solution.py
+++ b/solution.py
@@ -381,6 +381,10 @@
     second = over_y(after(backs[2], joined), 2)
     returned = [backs[0], first, second, third]
 
+    crossed_blocks = call(merge_kernel, shape(4, ROWS, BACK), [SMEM] + [VMEM] * 4)(
+        where, *[after(piece, rights[1]) for piece in returned]
+    )
+    crossed = over_ctx(crossed_blocks, 4)
     parts = call(
         weight_kernel,
         [shape(576, HEAD)] * 4,
@@ -388,11 +392,7 @@
         [pltpu.VMEM((576, 512), BF)],
         flops=1_300_000_000,
         moved=4_000_000,
-    )(where, after(near_rows, second), far_rows, across_near, across_far, *rights)
-    crossed = call(merge_kernel, shape(4, ROWS, BACK), [SMEM] + [VMEM] * 4)(
-        where, *[after(piece, parts[0]) for piece in returned]
-    )
-    crossed = over_ctx(crossed, 4)
+    )(where, after(near_rows, crossed_blocks), far_rows, across_near, across_far, *rights)
     far = over_ctx(far, 4)
     reduced = [over_y(parts[k], k) for k in range(4)]
     keep, send = call(

time: 101 us -> 100 us (0.990)
  starting transfers between devices: 40.1 us -> 38.9 us
  local copies, waits for them, and re-layouts: 1.76 us -> 2.87 us
    dynamic_slice x1, local copies, waits for them, and re-layouts: 0.94 us -> 2.05 us  [body(): piece = lax.dynamic_slice(inputs, (0, (x ^ k) * 1152), (ROWS, 1152))]
    ppermute x24, starting transfers between devices: 34 us -> 32.9 us  [spread(): return lax.ppermute(block, ('ctx', 'dp'), route)]
  transfers between devices with their start and end apart: 25 -> 25, of which waited for: 16 -> 13; matrix products, arithmetic and copies ran while one was open for 1% -> 2% of each run, Pallas kernels for 4% -> 7%
where the time goes in v6:
time: 100 us
  waiting for transfers between devices  40.6 us (41%)
  starting transfers between devices  38.9 us (39%)
  Pallas kernels  16.8 us (17%)
  local copies, waits for them, and re-layouts  2.87 us (3%)
    ppermute x24, waiting for transfers between devices, spread(): return lax.ppermute(block, ('ctx', 'dp'), route)  40.6 us
    ppermute x24, starting transfers between devices, spread(): return lax.ppermute(block, ('ctx', 'dp'), route)  32.9 us
    pallas_call x1, Pallas kernels, body(): call(attention_kernel, [shape(2, ROWS, BACK), shape(2, ROWS, 512)] * 2 +...  6.35 us
    all_to_all x1, starting transfers between devices, body(): arrived = lax.all_to_all(packed, 'ctx', 0, 0, tiled=True)  5.94 us
    pallas_call x1, Pallas kernels, body(): call(pack_kernel, shape(BLOCKS, ROWS + TAIL, PACKED), [ANY] * 5, [pltpu.V...  3.21 us
    dynamic_slice x1, local copies, waits for them, and re-layouts, body(): piece = lax.dynamic_slice(inputs, (0, (x ^ k) * 1152), (ROWS, 1152))  2.05 us
    pallas_call x1, Pallas kernels, body(): call(weight_kernel, [shape(576, HEAD)] * 4, [SMEM] + [VMEM] * 12, [pltpu....  2.04 us
  transfers between devices with their start and end apart: 25, of which 13 were waited for; matrix products, arithmetic and copies ran while one was open for 2% of the time, Pallas kernels for 7%

profile of v6, /device:TPU:32, one launch (start us, length us, event | category | flops | bytes accessed | tf_op | source)
XLA Modules:
  0.0 100.0 jit_solution(13614907253685527348)
XLA Ops:
  0.6 3.2 %shard_map.102 = bf16[8,144,768]{2,1,0:T(8,128)(2,1)} custom-call(bf16[128,2048]{1,0:T(8,128)(2,1)} %bitcast.19, bf16[128,1024]{1,0:T(8,128)(2,1)} %bitcast.22, bf16[128,1024]{1,0:T(8,128)(2,1)} %bitcast.23, bf16[128,2048]{1,0:T(8,128)(2,1)} %bitcast.20, bf16[128,2048]{1,0:T(8,128)(2,1)} %bitcast.21), custom_call_target="tpu_custom_call" | custom-call | tf_op jit(solution)/shard_map/pallas_call | solution.py:325
  3.8 5.9 %all-to-all-start = ((bf16[8,144,768]{2,1,0:T(8,128)(2,1)}), bf16[8,144,768]{2,1,0:T(8,128)(2,1)S(1)}, u32[]{:S(2)}, u32[]{:S(2)}) async-start(bf16[8,144,768]{2,1,0:T(8,128)(2,1)} %shard_map.102), calls=%async_computation | async-start | bytes 3538944 | tf_op jit(solution)/shard_map/all_to_all | solution.py:340
  9.8 2.0 %dynamic-slice_bitcast_fusion = (bf16[128,1152]{1,0:T(8,128)(2,1)S(1)}, bf16[128,1152]{1,0:T(8,128)(2,1)}, bf16[128,1152]{1,0:T(8,128)(2,1)S(1)}, bf16[128,1152]{1,0:T(8,128)(2,1)S(1)}) fusion(bf16[1,128,4608]{2,1,0:T(8,128)(2,1)} %param.12, s32[]{:T(128)S(6)} %select_n.37, s32[]{:T(128)S(6)} %select_n.35, s32[]{:T(128)S(6)} %select_n.34, s32[]{:T(128)S(6)} %select_n.36), kind=kLoop, calls=%fused_computation | loop fusion | bytes 2359312 | tf_op jit(solution)/shard_map/dynamic_slice | solution.py:345
  11.8 1.5 %collective-permute-start.7 = (bf16[128,1152]{1,0:T(8,128)(2,1)}, bf16[128,1152]{1,0:T(8,128)(2,1)S(1)}, u32[]{:S(2)}, u32[]{:S(2)}) collective-permute-start(bf16[128,1152]{1,0:T(8,128)(2,1)} %get-tuple-element.58), channel_id=1, source_target_pairs={{0,8},{1,9},{2,10},{3,11},{4,12},{5,13},{6,14},{7,15},{8,0},{9,1},... | collective-permute-start | bytes 884744 | tf_op jit(solution)/shard_map/ppermute | solution.py:32
  13.3 2.7 %collective-permute-start.8 = (bf16[128,1152]{1,0:T(8,128)(2,1)S(1)}, bf16[128,1152]{1,0:T(8,128)(2,1)S(1)}, u32[]{:S(2)}, u32[]{:S(2)}) collective-permute-start(bf16[128,1152]{1,0:T(8,128)(2,1)S(1)} %get-tuple-element.59), channel_id=1, source_target_pairs={{0,16},{1,17},{2,18},{3,19},{4,20},{5,21},{6,22},{7,23},{8,24},{9,... | collective-permute-start | bytes 884744 | tf_op jit(solution)/shard_map/ppermute | solution.py:32
  16.1 0.5 collective-permute-start.9
  16.5 0.1 pad_add_fusion.where
  16.6 5.4 %collective-permute-done.7.refs_1_ = bf16[128,1152]{1,0:T(8,128)(2,1)S(1)} collective-permute-done((bf16[128,1152]{1,0:T(8,128)(2,1)}, bf16[128,1152]{1,0:T(8,128)(2,1)S(1)}, u32[]{:S(2)}, u32[]{:S(2)}) %collective-permute-start.7) | collective-permute-done | bytes 294944 | tf_op jit(solution)/shard_map/ppermute | solution.py:32
  22.0 6.9 %collective-permute-done.8.refs_2_ = bf16[128,1152]{1,0:T(8,128)(2,1)S(1)} collective-permute-done((bf16[128,1152]{1,0:T(8,128)(2,1)S(1)}, bf16[128,1152]{1,0:T(8,128)(2,1)S(1)}, u32[]{:S(2)}, u32[]{:S(2)}) %collective-permute-start.8) | collective-permute-done | bytes 294944 | tf_op jit(solution)/shard_map/ppermute | solution.py:32
  28.9 2.4 %collective-permute-done.9.refs_3_ = bf16[128,1152]{1,0:T(8,128)(2,1)S(1)} collective-permute-done((bf16[128,1152]{1,0:T(8,128)(2,1)S(1)}, bf16[128,1152]{1,0:T(8,128)(2,1)S(1)}, u32[]{:S(2)}, u32[]{:S(2)}) %collective-permute-start.9) | collective-permute-done | bytes 294944 | tf_op jit(solution)/shard_map/ppermute | solution.py:32
  31.2 1.1 %shard_map.107 = (bf16[576,512]{1,0:T(8,128)(2,1)S(1)}, bf16[576,512]{1,0:T(8,128)(2,1)S(1)}) custom-call(s32[3]{0:T(128)S(1)} %pad_add_fusion.where, bf16[128,1152]{1,0:T(8,128)(2,1)S(1)} %get-tuple-element.57.refs_0_, bf16[128,1152]{1,0:T(8,128)(2,1)S(1)} %collective-permute-done.7.refs_1_, bf16[128,1152]{1,0:T(8,128)(2,1)S(1)} %collective-permute-done.8.refs_2_, ...), custom_call_target="tpu_custom_call" | custom-call | tf_op jit(solution)/shard_map/pallas_call | solution.py:347
  32.3 0.8 copy-done
  33.1 6.4 %shard_map.103 = (bf16[2,128,384]{2,1,0:T(8,128)(2,1)S(1)}, bf16[2,128,512]{2,1,0:T(8,128)(2,1)S(1)}, bf16[2,128,384]{2,1,0:T(8,128)(2,1)S(1)}, bf16[2,128,512]{...) custom-call(s32[3]{0:T(128)S(1)} %pad_add_fusion.where, ...), custom_call_target="tpu_custom_call" | custom-call | flops 4000000000 | bytes 4000000 | tf_op jit(solution)/shard_map/pallas_call | solution.py:355
  39.5 0.1 collective-permute-start.10
  39.6 0.4 collective-permute-start.11
  39.9 1.8 %collective-permute-start = (bf16[2,128,512]{2,1,0:T(8,128)(2,1)S(1)}, bf16[2,128,512]{2,1,0:T(8,128)(2,1)S(1)}, u32[]{:S(2)}, u32[]{:S(2)}) collective-permute-start(bf16[2,128,512]{2,1,0:T(8,128)(2,1)S(1)} %get-tuple-element.41), channel_id=1, source_target_pairs={{0,32},{1,33},{2,34},{3,35},{4,36},{5,37},{6,38},{7,39},{8,40},{9,... | collective-permute-start | bytes 786440 | tf_op jit(solution)/shard_map/ppermute | solution.py:32
  41.7 2.1 %collective-permute-start.2 = (bf16[2,128,512]{2,1,0:T(8,128)(2,1)S(1)}, bf16[2,128,512]{2,1,0:T(8,128)(2,1)S(1)}, u32[]{:S(2)}, u32[]{:S(2)}) collective-permute-start(bf16[2,128,512]{2,1,0:T(8,128)(2,1)S(1)} %get-tuple-element.45), channel_id=1, source_target_pairs={{0,96},{1,97},{2,98},{3,99},{4,100},{5,101},{6,102},{7,103},{8,104... | collective-permute-start | bytes 786440 | tf_op jit(solution)/shard_map/ppermute | solution.py:32
  43.8 0.6 collective-permute-start.1
  44.4 1.5 %collective-permute-start.12 = (bf16[576,512]{1,0:T(8,128)(2,1)S(1)}, bf16[576,512]{1,0:T(8,128)(2,1)S(1)}, u32[]{:S(2)}, u32[]{:S(2)}) collective-permute-start(bf16[576,512]{1,0:T(8,128)(2,1)S(1)} %collective-permute-done.10.refs_1_), channel_id=1, source_target_pairs={{0,128},{1,129},{2,130},{3,131},{4,132},{5,133},{6,134},{7,135},{8... | collective-permute-start | bytes 1769480 | tf_op jit(solution)/shard_map/ppermute | solution.py:32
  45.8 6.4 %collective-permute-done.1.refs_2_ = bf16[2,128,128]{2,1,0:T(8,128)(2,1)S(1)} collective-permute-done((bf16[2,128,128]{2,1,0:T(8,128)(2,1)S(1)}, bf16[2,128,128]{2,1,0:T(8,128)(2,1)S(1)}, u32[]{:S(2)}, u32[]{:S(2)}) %collective-permute-start.1) | collective-permute-done | bytes 65568 | tf_op jit(solution)/shard_map/ppermute | solution.py:32
  52.2 0.0 collective-permute-done.refs_1_
  52.2 0.2 collective-permute-done.2.refs_3_
  52.4 0.6 shard_map.104
  53.0 0.9 collective-permute-start.14
  53.9 1.4 %collective-permute-start.13 = (bf16[2,128,512]{2,1,0:T(8,128)(2,1)S(1)}, bf16[2,128,512]{2,1,0:T(8,128)(2,1)S(1)}, u32[]{:S(2)}, u32[]{:S(2)}) collective-permute-start(bf16[2,128,512]{2,1,0:T(8,128)(2,1)S(1)} %get-tuple-element.46.refs_4_), channel_id=1, source_target_pairs={{0,16},{1,17},{2,18},{3,19},{4,20},{5,21},{6,22},{7,23},{8,24},{9,... | collective-permute-start | bytes 786440 | tf_op jit(solution)/shard_map/ppermute | solution.py:32
  55.3 1.9 %collective-permute-start.4 = (bf16[2,128,512]{2,1,0:T(8,128)(2,1)S(1)}, bf16[2,128,512]{2,1,0:T(8,128)(2,1)S(1)}, u32[]{:S(2)}, u32[]{:S(2)}) collective-permute-start(bf16[2,128,512]{2,1,0:T(8,128)(2,1)S(1)} %get-tuple-element.46.refs_4_), channel_id=1, source_target_pairs={{0,8},{1,9},{2,10},{3,11},{4,12},{5,13},{6,14},{7,15},{8,0},{9,1},... | collective-permute-start | bytes 786440 | tf_op jit(solution)/shard_map/ppermute | solution.py:32
  57.2 1.6 %collective-permute-start.3 = (bf16[2,128,384]{2,1,0:T(8,128)(2,1)S(1)}, bf16[2,128,384]{2,1,0:T(8,128)(2,1)S(1)}, u32[]{:S(2)}, u32[]{:S(2)}) collective-permute-start(bf16[2,128,384]{2,1,0:T(8,128)(2,1)S(1)} %get-tuple-element.47), channel_id=1, source_target_pairs={{0,64},{1,65},{2,66},{3,67},{4,68},{5,69},{6,70},{7,71},{8,72},{9,... | collective-permute-start | bytes 589832 | tf_op jit(solution)/shard_map/ppermute | solution.py:32
  58.8 5.6 %collective-permute-done.3.refs_2_ = bf16[2,128,384]{2,1,0:T(8,128)(2,1)S(1)} collective-permute-done((bf16[2,128,384]{2,1,0:T(8,128)(2,1)S(1)}, bf16[2,128,384]{2,1,0:T(8,128)(2,1)S(1)}, u32[]{:S(2)}, u32[]{:S(2)}) %collective-permute-start.3) | collective-permute-done | bytes 196640 | tf_op jit(solution)/shard_map/ppermute | solution.py:32
  64.4 2.5 %collective-permute-done.14.refs_7_ = bf16[2,128,512]{2,1,0:T(8,128)(2,1)S(1)} collective-permute-done((bf16[2,128,512]{2,1,0:T(8,128)(2,1)S(1)}, bf16[2,128,512]{2,1,0:T(8,128)(2,1)S(1)}, u32[]{:S(2)}, u32[]{:S(2)}) %collective-permute-start.14) | collective-permute-done | bytes 262176 | tf_op jit(solution)/shard_map/ppermute | solution.py:32
  66.9 0.5 collective-permute-start.17
  67.4 0.1 collective-permute-done.4.refs_5_
  67.5 0.6 shard_map.105
  68.1 1.5 %collective-permute-start.5 = (bf16[4,128,384]{2,1,0:T(8,128)(2,1)S(1)}, bf16[4,128,384]{2,1,0:T(8,128)(2,1)S(1)}, u32[]{:S(2)}, u32[]{:S(2)}) collective-permute-start(bf16[4,128,384]{2,1,0:T(8,128)(2,1)S(1)} %shard_map.105), channel_id=1, source_target_pairs={{0,128},{1,129},{2,130},{3,131},{4,132},{5,133},{6,134},{7,135},{8... | collective-permute-start | bytes 1179656 | tf_op jit(solution)/shard_map/ppermute | solution.py:32
  69.7 2.0 %shard_map.108 = (bf16[576,128]{1,0:T(8,128)(2,1)S(1)}, bf16[576,128]{1,0:T(8,128)(2,1)S(1)}, bf16[576,128]{1,0:T(8,128)(2,1)S(1)}, bf16[576,128]{1,0:T(8,128)(2,1)S(1)}) custom-call(s32[3]{0:T(128)S(1)} %pad_add_fusion.where, bf16[576,512]{1,0:T(8,128)(2,1)S(1)} %get-tuple-element.62.refs_0_, bf16[576,512]{1,0:T(8,128)(2,1)S(1)} %collective-permute-done.10.refs_1_, ...), custom_call_target="tpu_custom_call" | custom-call | flops 1300000000 | bytes 4000000 | tf_op jit(solution)/shard_map/pallas_call | solution.py:388
  71.7 0.3 collective-permute-start.19
  72.1 3.5 %collective-permute-start.20 = (bf16[576,128]{1,0:T(8,128)(2,1)S(1)}, bf16[576,128]{1,0:T(8,128)(2,1)S(1)}, u32[]{:S(2)}, u32[]{:S(2)}) collective-permute-start(bf16[576,128]{1,0:T(8,128)(2,1)S(1)} %get-tuple-element.67), channel_id=1, source_target_pairs={{0,64},{1,65},{2,66},{3,67},{4,68},{5,69},{6,70},{7,71},{8,72},{9,... | collective-permute-start | bytes 442376 | tf_op jit(solution)/shard_map/ppermute | solution.py:32
  75.6 0.9 collective-permute-start.21
  76.5 0.9 collective-permute-start.6
  77.5 1.0 %collective-permute-done.19.refs_1_ = bf16[576,128]{1,0:T(8,128)(2,1)S(1)} collective-permute-done((bf16[576,128]{1,0:T(8,128)(2,1)S(1)}, bf16[576,128]{1,0:T(8,128)(2,1)S(1)}, u32[]{:S(2)}, u32[]{:S(2)}) %collective-permute-start.19) | collective-permute-done | bytes 147488 | tf_op jit(solution)/shard_map/ppermute | solution.py:32
  78.5 4.3 %collective-permute-done.20.refs_2_ = bf16[576,128]{1,0:T(8,128)(2,1)S(1)} collective-permute-done((bf16[576,128]{1,0:T(8,128)(2,1)S(1)}, bf16[576,128]{1,0:T(8,128)(2,1)S(1)}, u32[]{:S(2)}, u32[]{:S(2)}) %collective-permute-start.20) | collective-permute-done | bytes 147488 | tf_op jit(solution)/shard_map/ppermute | solution.py:32
  82.8 2.5 %collective-permute-done.21.refs_3_ = bf16[576,128]{1,0:T(8,128)(2,1)S(1)} collective-permute-done((bf16[576,128]{1,0:T(8,128)(2,1)S(1)}, bf16[576,128]{1,0:T(8,128)(2,1)S(1)}, u32[]{:S(2)}, u32[]{:S(2)}) %collective-permute-start.21) | collective-permute-done | bytes 147488 | tf_op jit(solution)/shard_map/ppermute | solution.py:32
  85.3 0.7 shard_map.109
  86.0 3.3 %collective-permute-start.22 = (bf16[2,144,128]{2,1,0:T(8,128)(2,1)S(1)}, bf16[2,144,128]{2,1,0:T(8,128)(2,1)S(1)}, u32[]{:S(2)}, u32[]{:S(2)}) collective-permute-start(bf16[2,144,128]{2,1,0:T(8,128)(2,1)S(1)} %get-tuple-element.70), channel_id=1, source_target_pairs={{0,2},{1,3},{2,0},{3,1},{4,6},{5,7},{6,4},{7,5},{8,10},{9,11},{10,... | collective-permute-start | bytes 221192 | tf_op jit(solution)/shard_map/ppermute | solution.py:32
  89.3 2.7 %collective-permute-done.22.landed = bf16[2,144,128]{2,1,0:T(8,128)(2,1)S(1)} collective-permute-done((bf16[2,144,128]{2,1,0:T(8,128)(2,1)S(1)}, bf16[2,144,128]{2,1,0:T(8,128)(2,1)S(1)}, u32[]{:S(2)}, u32[]{:S(2)}) %collective-permute-start.22) | collective-permute-done | bytes 73760 | tf_op jit(solution)/shard_map/ppermute | solution.py:32
  92.0 5.0 %collective-permute-start.23 = (bf16[144,128]{1,0:T(8,128)(2,1)S(1)}, bf16[144,128]{1,0:T(8,128)(2,1)S(1)}, u32[]{:S(2)}, u32[]{:S(2)}) collective-permute-start(bf16[144,128]{1,0:T(8,128)(2,1)S(1)} %get-tuple-element.73), channel_id=1, source_target_pairs={{0,6},{1,7},{2,4},{3,5},{4,2},{5,3},{6,0},{7,1},{8,14},{9,15},{10,... | collective-permute-start | bytes 110600 | tf_op jit(solution)/shard_map/ppermute | solution.py:32
  97.0 1.7 %shard_map.106 = (bf16[128,2048]{1,0:T(8,128)(2,1)}, bf16[128,1024]{1,0:T(8,128)(2,1)}, bf16[128,1024]{1,0:T(8,128)(2,1)}) custom-call(s32[3]{0:T(128)S(1)} %pad_add_fusion.where, bf16[2,128,384]{2,1,0:T(8,128)(2,1)S(1)} %get-tuple-element.48.refs_0_, bf16[2,128,512]{2,1,0:T(8,128)(2,1)S(1)} %collective-permute-done.refs_1_, ...), custom_call_target="tpu_custom_call" | custom-call | tf_op jit(solution)/shard_map/pallas_call | solution.py:405
  98.7 0.7 collective-permute-done.23.landed
  99.4 0.6 shard_map.111
  (20 shorter events, 0.1 us)
Async XLA Ops:
  3.8 29.3 %all-to-all-start = ((bf16[8,144,768]{2,1,0:T(8,128)(2,1)}), bf16[8,144,768]{2,1,0:T(8,128)(2,1)S(1)}, u32[]{:S(2)}, u32[]{:S(2)}) async-start(bf16[8,144,768]{2,1,0:T(8,128)(2,1)} %shard_map.102), calls=%async_computation | async-start | bytes 3538944 | tf_op jit(solution)/shard_map/all_to_all | solution.py:340
  9.8 23.3 %copy-start.2 = (s32[1,8]{1,0:T(1,128)S(1)}, s32[1,8]{1,0:T(1,128)}, u32[]{:S(2)}) copy-start(s32[1,8]{1,0:T(1,128)} %lengths.1) | copy-start | bytes 100
  11.8 10.2 %collective-permute-start.7 = (bf16[128,1152]{1,0:T(8,128)(2,1)}, bf16[128,1152]{1,0:T(8,128)(2,1)S(1)}, u32[]{:S(2)}, u32[]{:S(2)}) collective-permute-start(bf16[128,1152]{1,0:T(8,128)(2,1)} %get-tuple-element.58), channel_id=1, source_target_pairs={{0,8},{1,9},{2,10},{3,11},{4,12},{5,13},{6,14},{7,15},{8,0},{9,1},... | collective-permute-start | bytes 884744 | tf_op jit(solution)/shard_map/ppermute | solution.py:32
  13.3 15.5 %collective-permute-start.8 = (bf16[128,1152]{1,0:T(8,128)(2,1)S(1)}, bf16[128,1152]{1,0:T(8,128)(2,1)S(1)}, u32[]{:S(2)}, u32[]{:S(2)}) collective-permute-start(bf16[128,1152]{1,0:T(8,128)(2,1)S(1)} %get-tuple-element.59), channel_id=1, source_target_pairs={{0,16},{1,17},{2,18},{3,19},{4,20},{5,21},{6,22},{7,23},{8,24},{9,... | collective-permute-start | bytes 884744 | tf_op jit(solution)/shard_map/ppermute | solution.py:32
  16.1 15.2 %collective-permute-start.9 = (bf16[128,1152]{1,0:T(8,128)(2,1)S(1)}, bf16[128,1152]{1,0:T(8,128)(2,1)S(1)}, u32[]{:S(2)}, u32[]{:S(2)}) collective-permute-start(bf16[128,1152]{1,0:T(8,128)(2,1)S(1)} %get-tuple-element.60), channel_id=1, source_target_pairs={{0,24},{1,25},{2,26},{3,27},{4,28},{5,29},{6,30},{7,31},{8,16},{9,... | collective-permute-start | bytes 884744 | tf_op jit(solution)/shard_map/ppermute | solution.py:32
  32.3 0.8 copy-start
  33.1 6.4 %copy-start.1 = (bf16[576,512]{1,0:T(8,128)(2,1)S(1)}, bf16[576,512]{1,0:T(8,128)(2,1)}, u32[]{:S(2)}) copy-start(bf16[576,512]{1,0:T(8,128)(2,1)} %copy-done) | copy-start | bytes 1769476
  39.5 4.9 %collective-permute-start.10 = (bf16[576,512]{1,0:T(8,128)(2,1)S(1)}, bf16[576,512]{1,0:T(8,128)(2,1)S(1)}, u32[]{:S(2)}, u32[]{:S(2)}) collective-permute-start(bf16[576,512]{1,0:T(8,128)(2,1)S(1)} %copy-done.1), channel_id=1, source_target_pairs={{0,1},{1,0},{2,3},{3,2},{4,5},{5,4},{6,7},{7,6},{8,9},{9,8},{10,11... | collective-permute-start | bytes 1769480 | tf_op jit(solution)/shard_map/ppermute | solution.py:32
  39.6 17.6 %collective-permute-start.11 = (bf16[576,512]{1,0:T(8,128)(2,1)S(1)}, bf16[576,512]{1,0:T(8,128)(2,1)S(1)}, u32[]{:S(2)}, u32[]{:S(2)}) collective-permute-start(bf16[576,512]{1,0:T(8,128)(2,1)S(1)} %get-tuple-element.62.refs_0_), channel_id=1, source_target_pairs={{0,128},{1,129},{2,130},{3,131},{4,132},{5,133},{6,134},{7,135},{8... | collective-permute-start | bytes 1769480 | tf_op jit(solution)/shard_map/ppermute | solution.py:32
  39.9 12.3 %collective-permute-start = (bf16[2,128,512]{2,1,0:T(8,128)(2,1)S(1)}, bf16[2,128,512]{2,1,0:T(8,128)(2,1)S(1)}, u32[]{:S(2)}, u32[]{:S(2)}) collective-permute-start(bf16[2,128,512]{2,1,0:T(8,128)(2,1)S(1)} %get-tuple-element.41), channel_id=1, source_target_pairs={{0,32},{1,33},{2,34},{3,35},{4,36},{5,37},{6,38},{7,39},{8,40},{9,... | collective-permute-start | bytes 786440 | tf_op jit(solution)/shard_map/ppermute | solution.py:32
  41.7 10.7 %collective-permute-start.2 = (bf16[2,128,512]{2,1,0:T(8,128)(2,1)S(1)}, bf16[2,128,512]{2,1,0:T(8,128)(2,1)S(1)}, u32[]{:S(2)}, u32[]{:S(2)}) collective-permute-start(bf16[2,128,512]{2,1,0:T(8,128)(2,1)S(1)} %get-tuple-element.45), channel_id=1, source_target_pairs={{0,96},{1,97},{2,98},{3,99},{4,100},{5,101},{6,102},{7,103},{8,104... | collective-permute-start | bytes 786440 | tf_op jit(solution)/shard_map/ppermute | solution.py:32
  43.8 8.5 %collective-permute-start.1 = (bf16[2,128,128]{2,1,0:T(8,128)(2,1)S(1)}, bf16[2,128,128]{2,1,0:T(8,128)(2,1)S(1)}, u32[]{:S(2)}, u32[]{:S(2)}) collective-permute-start(bf16[2,128,128]{2,1,0:T(8,128)(2,1)S(1)} %get-tuple-element.44), channel_id=1, source_target_pairs={{0,64},{1,65},{2,66},{3,67},{4,68},{5,69},{6,70},{7,71},{8,72},{9,... | collective-permute-start | bytes 196616 | tf_op jit(solution)/shard_map/ppermute | solution.py:32
  44.4 25.3 %collective-permute-start.12 = (bf16[576,512]{1,0:T(8,128)(2,1)S(1)}, bf16[576,512]{1,0:T(8,128)(2,1)S(1)}, u32[]{:S(2)}, u32[]{:S(2)}) collective-permute-start(bf16[576,512]{1,0:T(8,128)(2,1)S(1)} %collective-permute-done.10.refs_1_), channel_id=1, source_target_pairs={{0,128},{1,129},{2,130},{3,131},{4,132},{5,133},{6,134},{7,135},{8... | collective-permute-start | bytes 1769480 | tf_op jit(solution)/shard_map/ppermute | solution.py:32
  53.0 13.9 %collective-permute-start.14 = (bf16[2,128,512]{2,1,0:T(8,128)(2,1)S(1)}, bf16[2,128,512]{2,1,0:T(8,128)(2,1)S(1)}, u32[]{:S(2)}, u32[]{:S(2)}) collective-permute-start(bf16[2,128,512]{2,1,0:T(8,128)(2,1)S(1)} %get-tuple-element.46.refs_4_), channel_id=1, source_target_pairs={{0,24},{1,25},{2,26},{3,27},{4,28},{5,29},{6,30},{7,31},{8,16},{9,... | collective-permute-start | bytes 786440 | tf_op jit(solution)/shard_map/ppermute | solution.py:32
  53.9 13.0 %collective-permute-start.13 = (bf16[2,128,512]{2,1,0:T(8,128)(2,1)S(1)}, bf16[2,128,512]{2,1,0:T(8,128)(2,1)S(1)}, u32[]{:S(2)}, u32[]{:S(2)}) collective-permute-start(bf16[2,128,512]{2,1,0:T(8,128)(2,1)S(1)} %get-tuple-element.46.refs_4_), channel_id=1, source_target_pairs={{0,16},{1,17},{2,18},{3,19},{4,20},{5,21},{6,22},{7,23},{8,24},{9,... | collective-permute-start | bytes 786440 | tf_op jit(solution)/shard_map/ppermute | solution.py:32
  55.3 12.2 %collective-permute-start.4 = (bf16[2,128,512]{2,1,0:T(8,128)(2,1)S(1)}, bf16[2,128,512]{2,1,0:T(8,128)(2,1)S(1)}, u32[]{:S(2)}, u32[]{:S(2)}) collective-permute-start(bf16[2,128,512]{2,1,0:T(8,128)(2,1)S(1)} %get-tuple-element.46.refs_4_), channel_id=1, source_target_pairs={{0,8},{1,9},{2,10},{3,11},{4,12},{5,13},{6,14},{7,15},{8,0},{9,1},... | collective-permute-start | bytes 786440 | tf_op jit(solution)/shard_map/ppermute | solution.py:32
  57.2 7.2 %collective-permute-start.3 = (bf16[2,128,384]{2,1,0:T(8,128)(2,1)S(1)}, bf16[2,128,384]{2,1,0:T(8,128)(2,1)S(1)}, u32[]{:S(2)}, u32[]{:S(2)}) collective-permute-start(bf16[2,128,384]{2,1,0:T(8,128)(2,1)S(1)} %get-tuple-element.47), channel_id=1, source_target_pairs={{0,64},{1,65},{2,66},{3,67},{4,68},{5,69},{6,70},{7,71},{8,72},{9,... | collective-permute-start | bytes 589832 | tf_op jit(solution)/shard_map/ppermute | solution.py:32
  64.4 3.7 %collective-permute-start.15 = (bf16[2,128,512]{2,1,0:T(8,128)(2,1)S(1)}, bf16[2,128,512]{2,1,0:T(8,128)(2,1)S(1)}, u32[]{:S(2)}, u32[]{:S(2)}) collective-permute-start(bf16[2,128,512]{2,1,0:T(8,128)(2,1)S(1)} %get-tuple-element.46.refs_4_), channel_id=1, source_target_pairs={{0,1},{1,0},{2,3},{3,2},{4,5},{5,4},{6,7},{7,6},{8,9},{9,8},{10,11... | collective-permute-start | bytes 786440 | tf_op jit(solution)/shard_map/ppermute | solution.py:32
  66.9 2.8 %collective-permute-start.18 = (bf16[2,128,512]{2,1,0:T(8,128)(2,1)S(1)}, bf16[2,128,512]{2,1,0:T(8,128)(2,1)S(1)}, u32[]{:S(2)}, u32[]{:S(2)}) collective-permute-start(bf16[2,128,512]{2,1,0:T(8,128)(2,1)S(1)} %collective-permute-done.14.refs_7_), channel_id=1, source_target_pairs={{0,1},{1,0},{2,3},{3,2},{4,5},{5,4},{6,7},{7,6},{8,9},{9,8},{10,11... | collective-permute-start | bytes 786440 | tf_op jit(solution)/shard_map/ppermute | solution.py:32
  66.9 2.8 %collective-permute-start.17 = (bf16[2,128,512]{2,1,0:T(8,128)(2,1)S(1)}, bf16[2,128,512]{2,1,0:T(8,128)(2,1)S(1)}, u32[]{:S(2)}, u32[]{:S(2)}) collective-permute-start(bf16[2,128,512]{2,1,0:T(8,128)(2,1)S(1)} %collective-permute-done.13.refs_6_), channel_id=1, source_target_pairs={{0,1},{1,0},{2,3},{3,2},{4,5},{5,4},{6,7},{7,6},{8,9},{9,8},{10,11... | collective-permute-start | bytes 786440 | tf_op jit(solution)/shard_map/ppermute | solution.py:32
  67.5 2.2 %collective-permute-start.16 = (bf16[2,128,512]{2,1,0:T(8,128)(2,1)S(1)}, bf16[2,128,512]{2,1,0:T(8,128)(2,1)S(1)}, u32[]{:S(2)}, u32[]{:S(2)}) collective-permute-start(bf16[2,128,512]{2,1,0:T(8,128)(2,1)S(1)} %collective-permute-done.4.refs_5_), channel_id=1, source_target_pairs={{0,1},{1,0},{2,3},{3,2},{4,5},{5,4},{6,7},{7,6},{8,9},{9,8},{10,11... | collective-permute-start | bytes 786440 | tf_op jit(solution)/shard_map/ppermute | solution.py:32
  68.1 28.9 %collective-permute-start.5 = (bf16[4,128,384]{2,1,0:T(8,128)(2,1)S(1)}, bf16[4,128,384]{2,1,0:T(8,128)(2,1)S(1)}, u32[]{:S(2)}, u32[]{:S(2)}) collective-permute-start(bf16[4,128,384]{2,1,0:T(8,128)(2,1)S(1)} %shard_map.105), channel_id=1, source_target_pairs={{0,128},{1,129},{2,130},{3,131},{4,132},{5,133},{6,134},{7,135},{8... | collective-permute-start | bytes 1179656 | tf_op jit(solution)/shard_map/ppermute | solution.py:32
  71.7 6.8 %collective-permute-start.19 = (bf16[576,128]{1,0:T(8,128)(2,1)S(1)}, bf16[576,128]{1,0:T(8,128)(2,1)S(1)}, u32[]{:S(2)}, u32[]{:S(2)}) collective-permute-start(bf16[576,128]{1,0:T(8,128)(2,1)S(1)} %get-tuple-element.66), channel_id=1, source_target_pairs={{0,32},{1,33},{2,34},{3,35},{4,36},{5,37},{6,38},{7,39},{8,40},{9,... | collective-permute-start | bytes 442376 | tf_op jit(solution)/shard_map/ppermute | solution.py:32
  72.1 10.7 %collective-permute-start.20 = (bf16[576,128]{1,0:T(8,128)(2,1)S(1)}, bf16[576,128]{1,0:T(8,128)(2,1)S(1)}, u32[]{:S(2)}, u32[]{:S(2)}) collective-permute-start(bf16[576,128]{1,0:T(8,128)(2,1)S(1)} %get-tuple-element.67), channel_id=1, source_target_pairs={{0,64},{1,65},{2,66},{3,67},{4,68},{5,69},{6,70},{7,71},{8,72},{9,... | collective-permute-start | bytes 442376 | tf_op jit(solution)/shard_map/ppermute | solution.py:32
  75.6 9.7 %collective-permute-start.21 = (bf16[576,128]{1,0:T(8,128)(2,1)S(1)}, bf16[576,128]{1,0:T(8,128)(2,1)S(1)}, u32[]{:S(2)}, u32[]{:S(2)}) collective-permute-start(bf16[576,128]{1,0:T(8,128)(2,1)S(1)} %get-tuple-element.68), channel_id=1, source_target_pairs={{0,96},{1,97},{2,98},{3,99},{4,100},{5,101},{6,102},{7,103},{8,104... | collective-permute-start | bytes 442376 | tf_op jit(solution)/shard_map/ppermute | solution.py:32
  76.5 20.5 %collective-permute-start.6 = (bf16[128,512]{1,0:T(8,128)(2,1)S(1)}, bf16[128,512]{1,0:T(8,128)(2,1)S(1)}, u32[]{:S(2)}, u32[]{:S(2)}) collective-permute-start(bf16[128,512]{1,0:T(8,128)(2,1)S(1)} %get-tuple-element.53), channel_id=1, source_target_pairs={{0,128},{1,129},{2,130},{3,131},{4,132},{5,133},{6,134},{7,135},{8... | collective-permute-start | bytes 393224 | tf_op jit(solution)/shard_map/ppermute | solution.py:32
  86.0 6.0 %collective-permute-start.22 = (bf16[2,144,128]{2,1,0:T(8,128)(2,1)S(1)}, bf16[2,144,128]{2,1,0:T(8,128)(2,1)S(1)}, u32[]{:S(2)}, u32[]{:S(2)}) collective-permute-start(bf16[2,144,128]{2,1,0:T(8,128)(2,1)S(1)} %get-tuple-element.70), channel_id=1, source_target_pairs={{0,2},{1,3},{2,0},{3,1},{4,6},{5,7},{6,4},{7,5},{8,10},{9,11},{10,... | collective-permute-start | bytes 221192 | tf_op jit(solution)/shard_map/ppermute | solution.py:32
  92.0 7.4 %collective-permute-start.23 = (bf16[144,128]{1,0:T(8,128)(2,1)S(1)}, bf16[144,128]{1,0:T(8,128)(2,1)S(1)}, u32[]{:S(2)}, u32[]{:S(2)}) collective-permute-start(bf16[144,128]{1,0:T(8,128)(2,1)S(1)} %get-tuple-element.73), channel_id=1, source_target_pairs={{0,6},{1,7},{2,4},{3,5},{4,2},{5,3},{6,0},{7,1},{8,14},{9,15},{10,... | collective-permute-start | bytes 110600 | tf_op jit(solution)/shard_map/ppermute | solution.py:32
